TPU v7x, 32 devices: a whole 2x2x4 slice. The times are simulated.
32 devices in a mesh: dp: 16 (over z, y, x), tensor: 2 (over core).
Axes of the slice: x: 2, y: 2, z: 4, core: 2. Of those that a mesh axis runs over, the one named last changes fastest.
Arguments:
- hidden_in: bfloat16 [8192, 1536], P(('dp', 'tensor')), may hold values from -6 to 6
- segment_ids: int32 [8192], P('dp'), may hold values from 0 to 31, as said below
- routes: int32 [8192, 4], P('dp'), may hold values from 0 to 7, all different within a row
- slot_order: int32 [16, 2048], P('dp'), may hold values from 0 to 2047, each once within a row
- gain_attn: bfloat16 [1536], P('dp'), may hold values from 0.099609375 to 1.8984375
- w_query: bfloat16 [1536, 1536], P('dp', 'tensor'), may hold values from -0.3125 to 0.3125
- w_key: bfloat16 [1536, 256], P('dp', 'tensor'), may hold values from -0.3125 to 0.3125
- w_value: bfloat16 [1536, 256], P('dp', 'tensor'), may hold values from -0.15625 to 0.15625
- w_out: bfloat16 [1536, 1536], P('tensor', 'dp'), may hold values from -0.625 to 0.625
- gain_ffn: bfloat16 [1536], P('dp'), may hold values from 0.099609375 to 1.8984375
- w_router: bfloat16 [1536, 8], P('dp'), may hold values from -0.078125 to 0.078125
- w_gate: bfloat16 [8, 1536, 768], P(None, 'dp', 'tensor'), may hold values from -0.15625 to 0.15625
- w_up: bfloat16 [8, 1536, 768], P(None, 'dp', 'tensor'), may hold values from -0.15625 to 0.15625
- w_down: bfloat16 [8, 768, 1536], P(None, 'tensor', 'dp'), may hold values from -0.4375 to 0.4375
- grad_out: bfloat16 [8192, 1536], P(('dp', 'tensor')), may hold values from -6 to 6
Outputs:
- layer_out: float32 [8192, 1536], P(('dp', 'tensor'))
- grad_in: float32 [8192, 1536], P(('dp', 'tensor'))
- grad_gain_attn: float32 [1536], P('dp')
- grad_w_query: float32 [1536, 1536], P('dp', 'tensor')
- grad_w_key: float32 [1536, 256], P('dp', 'tensor')
- grad_w_value: float32 [1536, 256], P('dp', 'tensor')
- grad_w_out: float32 [1536, 1536], P('tensor', 'dp')
- grad_gain_ffn: float32 [1536], P('dp')
- grad_w_router: float32 [1536, 8], P('dp')
- grad_w_gate: float32 [8, 1536, 768], P(None, 'dp', 'tensor')
- grad_w_up: float32 [8, 1536, 768], P(None, 'dp', 'tensor')
- grad_w_down: float32 [8, 768, 1536], P(None, 'tensor', 'dp')
Inputs may be any that keep to these rules, and one draw needn't show every extreme that they name: `segment_ids`: within each sequence of 512 tokens the ids start at 0, never fall and rise by at most one from token to token; documents never span two sequences.
All inputs are finite; a program needn't handle non-finite values.
Results may differ from a plain program's by a relative error of at most 0.023.
The roundings to bfloat16 on the way count: a program that leaves them out, or rounds other values in their place, can miss the bound.
Values may be sent and summed in bfloat16 or wider, within the bound.
No kernel may reach another device: no remote copies, remote signals or barrier semaphores. Data moves between devices by JAX's collectives and lax.ppermute only.
A program may use at most 256 MiB of HBM per device.

v0:
```python
import math

import jax
import jax.numpy as jnp
from jax import lax
from jax.sharding import PartitionSpec as P

HD = 128


epsilon = 1e-06
highest = lax.Precision.HIGHEST


def rms_parts(values):
    inverse_root = lax.rsqrt(jnp.mean(values * values, axis=-1, keepdims=True) + epsilon)
    return (values * inverse_root, inverse_root)


def norm_backward(grad_normed, scaled, inverse_root, gain):
    grad_scaled = grad_normed * gain
    inner = jnp.mean(grad_scaled * scaled, axis=-1, keepdims=True)
    return inverse_root * (grad_scaled - scaled * inner)


def rope_tables(length, size):
    inverse = 10000.0 ** (-jnp.arange(size // 2, dtype=jnp.float32) / (size // 2))
    angle = jnp.arange(length, dtype=jnp.float32)[:, None] * inverse[None, :]
    return (jnp.cos(angle), jnp.sin(angle))


def rotate(values, cosine, sine_table):
    half_size = values.shape[-1] // 2
    first_half = values[..., :half_size]
    second = values[..., half_size:]
    cos_wide = cosine[:, None, :]
    sin_wide = sine_table[:, None, :]
    return jnp.concatenate(
        [first_half * cos_wide - second * sin_wide, second * cos_wide + first_half * sin_wide],
        axis=-1,
    )


def unrotate(values, cosine, sine_table):
    half_size = values.shape[-1] // 2
    first_half = values[..., :half_size]
    second = values[..., half_size:]
    cos_wide = cosine[:, None, :]
    sin_wide = sine_table[:, None, :]
    return jnp.concatenate(
        [first_half * cos_wide + second * sin_wide, second * cos_wide - first_half * sin_wide],
        axis=-1,
    )


def queue_slots(route, order_row, experts, capacity):
    length, top_count = route.shape
    slot_count = length * top_count
    flat_routes = route.reshape(-1)
    inverse = (
        jnp.zeros((slot_count,), jnp.int32)
        .at[order_row]
        .set(jnp.arange(slot_count, dtype=jnp.int32))
    )
    ranked = flat_routes[inverse]
    onehot = (ranked[:, None] == jnp.arange(experts, dtype=jnp.int32)[None, :]).astype(jnp.int32)
    before = jnp.cumsum(onehot, axis=0) - onehot
    ranked_pos = jnp.sum(before * onehot, axis=1)
    position = ranked_pos[order_row]
    placing = jnp.where(position < capacity, flat_routes * capacity + position, experts * capacity)
    token_of = (
        jnp.full((experts * capacity + 1,), length, jnp.int32)
        .at[placing]
        .set(jnp.arange(slot_count, dtype=jnp.int32) // top_count)
    )
    return (placing, token_of[: experts * capacity])


def geglu(gate_pre, up_pre):
    return jax.nn.gelu(gate_pre) * up_pre


def per_device(
    hidden_in,
    segment_ids,
    routes,
    slot_order,
    gain_attn,
    w_query,
    w_key,
    w_value,
    w_out,
    gain_ffn,
    w_router,
    w_gate,
    w_up,
    w_down,
    grad_out,
):
    tok_rows, width = hidden_in.shape
    seq_len = segment_ids.shape[0]
    top_count = routes.shape[1]
    experts = w_gate.shape[0]
    capacity = 9 * seq_len * top_count // (8 * experts)
    tensor_rank = lax.axis_index("tensor")
    gain_a, query_w, key_w, value_w, out_w = (
        lax.all_gather(gain_attn, "dp", axis=0, tiled=True),
        lax.all_gather(w_query, "dp", axis=0, tiled=True),
        lax.all_gather(w_key, "dp", axis=0, tiled=True),
        lax.all_gather(w_value, "dp", axis=0, tiled=True),
        lax.all_gather(w_out, "dp", axis=1, tiled=True),
    )
    gain_af = gain_a.astype(jnp.float32)
    scaled_in, root_in = rms_parts(hidden_in.astype(jnp.float32))
    normed_local = (scaled_in * gain_af).astype(jnp.bfloat16)
    normed = lax.all_gather(normed_local, "tensor", axis=0, tiled=True)
    head_count = query_w.shape[1] // HD
    kv_local = key_w.shape[1] // HD
    per_group = head_count // kv_local
    cosine, sine_table = rope_tables(seq_len, HD)
    query_f = jnp.dot(normed, query_w, preferred_element_type=jnp.float32).reshape(
        seq_len, head_count, HD
    )
    key_f = jnp.dot(normed, key_w, preferred_element_type=jnp.float32).reshape(
        seq_len, kv_local, HD
    )
    value_r = (
        jnp.dot(normed, value_w, preferred_element_type=jnp.float32)
        .astype(jnp.bfloat16)
        .reshape(seq_len, kv_local, HD)
    )
    query_r = rotate(query_f, cosine, sine_table).astype(jnp.bfloat16)
    key_r = rotate(key_f, cosine, sine_table).astype(jnp.bfloat16)
    query_g = query_r.reshape(seq_len, kv_local, per_group, HD)
    scale = 1.0 / math.sqrt(HD)
    positions = jnp.arange(seq_len, dtype=jnp.int32)

    def block_scores():
        raw = (
            jnp.einsum("qgrd,kgd->grqk", query_g, key_r, preferred_element_type=jnp.float32) * scale
        )
        allowed = (segment_ids[:, None] == segment_ids[None, :]) & (
            positions[None, :] <= positions[:, None]
        )
        return (jnp.where(allowed[None, None], raw, -1e30), query_g)

    masked, rows_q = block_scores()
    peak = jnp.max(masked, axis=-1, keepdims=True)
    expo_vals = jnp.exp(masked - peak)
    total = jnp.sum(expo_vals, axis=-1, keepdims=True)
    probabilities = (expo_vals / total).astype(jnp.bfloat16)
    mixed_block = jnp.einsum(
        "grqk,kgd->qgrd", probabilities, value_r, preferred_element_type=jnp.float32
    )
    mixed_parts = mixed_block.reshape(seq_len, head_count * HD).astype(jnp.bfloat16)
    lse_parts = peak + jnp.log(total)
    attn_local = lax.psum_scatter(
        jnp.dot(mixed_parts, out_w, preferred_element_type=jnp.float32).astype(jnp.bfloat16),
        "tensor",
        scatter_dimension=0,
        tiled=True,
    ).astype(jnp.float32)
    middle = hidden_in.astype(jnp.float32) + attn_local
    gain_f, router_w, gate_w, upper_w, down_w = (
        lax.all_gather(gain_ffn, "dp", axis=0, tiled=True),
        lax.all_gather(w_router, "dp", axis=0, tiled=True),
        lax.all_gather(w_gate, "dp", axis=1, tiled=True),
        lax.all_gather(w_up, "dp", axis=1, tiled=True),
        lax.all_gather(w_down, "dp", axis=2, tiled=True),
    )
    scaled_mid, root_mid = rms_parts(middle)
    normed2_local = (scaled_mid * gain_f.astype(jnp.float32)).astype(jnp.bfloat16)
    normed2 = lax.all_gather(normed2_local, "tensor", axis=0, tiled=True)
    logits = jnp.dot(normed2, router_w, preferred_element_type=jnp.float32)
    chosen = jnp.take_along_axis(logits, routes, axis=1)
    gate_weights = jax.nn.softmax(chosen, axis=-1)
    placing, token_of = queue_slots(routes, slot_order[0], experts, capacity)
    padded = jnp.concatenate([normed2, jnp.zeros((1, width), jnp.bfloat16)], axis=0)
    expert_in = padded[token_of].reshape(experts, capacity, width)
    gate_pre = jnp.einsum("ecd,edh->ech", expert_in, gate_w, preferred_element_type=jnp.float32)
    up_pre = jnp.einsum("ecd,edh->ech", expert_in, upper_w, preferred_element_type=jnp.float32)
    activated = geglu(gate_pre, up_pre).astype(jnp.bfloat16)
    expert_out = jnp.einsum("ech,ehd->ecd", activated, down_w, preferred_element_type=jnp.float32)
    out_padded = jnp.concatenate(
        [expert_out.reshape(experts * capacity, width), jnp.zeros((1, width), jnp.float32)], axis=0
    )
    picked = out_padded[placing].reshape(seq_len, top_count, width)
    branch = jnp.sum(gate_weights[:, :, None] * picked, axis=1)
    branch_local = lax.psum_scatter(
        branch.astype(jnp.bfloat16), "tensor", scatter_dimension=0, tiled=True
    ).astype(jnp.float32)
    layer_out = middle + branch_local
    grad_full = lax.all_gather(grad_out, "tensor", axis=0, tiled=True)
    grad_gates_part = jnp.sum(picked * grad_full[:, None, :].astype(jnp.float32), axis=-1)
    gate_of = (
        jnp.zeros((experts * capacity + 1,), jnp.float32)
        .at[placing]
        .set(gate_weights.reshape(-1))[: experts * capacity]
    )
    grad_padded = jnp.concatenate([grad_full, jnp.zeros((1, width), jnp.bfloat16)], axis=0)
    grad_expert_out = (
        (gate_of[:, None] * grad_padded[token_of])
        .astype(jnp.bfloat16)
        .reshape(experts, capacity, width)
    )
    grad_act = jnp.einsum(
        "ecd,ehd->ech", grad_expert_out, down_w, preferred_element_type=jnp.float32
    )
    geglu_value, act_pull = jax.vjp(geglu, gate_pre, up_pre)
    grad_gate_pre, grad_up_pre = act_pull(grad_act)
    grad_gate_r = grad_gate_pre.astype(jnp.bfloat16)
    grad_up_r = grad_up_pre.astype(jnp.bfloat16)
    grad_expert_in = jnp.einsum(
        "ech,edh->ecd", grad_gate_r, gate_w, preferred_element_type=jnp.float32
    ) + jnp.einsum("ech,edh->ecd", grad_up_r, upper_w, preferred_element_type=jnp.float32)
    in_padded = jnp.concatenate(
        [grad_expert_in.reshape(experts * capacity, width), jnp.zeros((1, width), jnp.float32)],
        axis=0,
    )
    grad_normed2_part = jnp.sum(in_padded[placing].reshape(seq_len, top_count, width), axis=1)
    grad_normed2, grad_gates = (
        lax.psum_scatter(
            grad_normed2_part.astype(jnp.bfloat16), "tensor", scatter_dimension=0, tiled=True
        ).astype(jnp.float32),
        lax.psum_scatter(
            grad_gates_part.astype(jnp.bfloat16), "tensor", scatter_dimension=0, tiled=True
        ).astype(jnp.float32),
    )
    row_begin = tensor_rank * tok_rows
    local_gates = lax.dynamic_slice_in_dim(gate_weights, row_begin, tok_rows, 0)
    local_routes = lax.dynamic_slice_in_dim(routes, row_begin, tok_rows, 0)
    grad_chosen = local_gates * (
        grad_gates - jnp.sum(local_gates * grad_gates, axis=-1, keepdims=True)
    )
    onehot_routes = (
        local_routes[:, :, None] == jnp.arange(experts, dtype=jnp.int32)[None, None, :]
    ).astype(jnp.float32)
    grad_logits = jnp.sum(grad_chosen[:, :, None] * onehot_routes, axis=1)
    grad_normed2 = grad_normed2 + jnp.einsum(
        "te,de->td", grad_logits, router_w.astype(jnp.float32), precision=highest
    )
    grad_router_part = jnp.einsum(
        "td,te->de", normed2_local.astype(jnp.float32), grad_logits, precision=highest
    )
    grad_gain_f_part = jnp.sum(grad_normed2 * scaled_mid, axis=0)
    grad_middle = grad_out.astype(jnp.float32) + norm_backward(
        grad_normed2, scaled_mid, root_mid, gain_f.astype(jnp.float32)
    )
    grad_gate_w = jnp.einsum(
        "ecd,ech->edh", expert_in, grad_gate_r, preferred_element_type=jnp.float32
    )
    grad_upper_w = jnp.einsum(
        "ecd,ech->edh", expert_in, grad_up_r, preferred_element_type=jnp.float32
    )
    grad_down_w = jnp.einsum(
        "ech,ecd->ehd", activated, grad_expert_out, preferred_element_type=jnp.float32
    )
    grad_mid_full = lax.all_gather(grad_middle.astype(jnp.bfloat16), "tensor", axis=0, tiled=True)
    grad_out_w = jnp.einsum(
        "qc,qd->cd", mixed_parts, grad_mid_full, preferred_element_type=jnp.float32
    )
    grad_mixed = jnp.einsum("qd,cd->qc", grad_mid_full, out_w, preferred_element_type=jnp.float32)
    grad_mixed = grad_mixed.astype(jnp.bfloat16).reshape(seq_len, kv_local, per_group, HD)
    masked, rows_q = block_scores()
    probs_float = jnp.exp(masked - lse_parts)
    probabilities = probs_float.astype(jnp.bfloat16)
    grad_probs = jnp.einsum(
        "qgrd,kgd->grqk", grad_mixed, value_r, preferred_element_type=jnp.float32
    )
    inner = jnp.sum(grad_probs * probs_float, axis=-1, keepdims=True)
    grad_scores = (probs_float * (grad_probs - inner)).astype(jnp.bfloat16)
    grad_query_parts = (
        jnp.einsum("grqk,kgd->qgrd", grad_scores, key_r, preferred_element_type=jnp.float32) * scale
    )
    grad_key = (
        jnp.einsum("grqk,qgrd->kgd", grad_scores, rows_q, preferred_element_type=jnp.float32)
        * scale
    )
    grad_value = jnp.einsum(
        "grqk,qgrd->kgd", probabilities, grad_mixed, preferred_element_type=jnp.float32
    )
    grad_query_rot = grad_query_parts.reshape(seq_len, head_count, HD)
    grad_query = (
        unrotate(grad_query_rot, cosine, sine_table)
        .astype(jnp.bfloat16)
        .reshape(seq_len, head_count * HD)
    )
    grad_key_r = (
        unrotate(grad_key, cosine, sine_table).astype(jnp.bfloat16).reshape(seq_len, kv_local * HD)
    )
    grad_value_r = grad_value.astype(jnp.bfloat16).reshape(seq_len, kv_local * HD)
    grad_query_w = jnp.einsum("qd,qc->dc", normed, grad_query, preferred_element_type=jnp.float32)
    grad_key_w = jnp.einsum("qd,qc->dc", normed, grad_key_r, preferred_element_type=jnp.float32)
    grad_value_w = jnp.einsum("qd,qc->dc", normed, grad_value_r, preferred_element_type=jnp.float32)
    grad_normed = lax.psum_scatter(
        (
            jnp.einsum("qc,dc->qd", grad_query, query_w, preferred_element_type=jnp.float32)
            + jnp.einsum("qc,dc->qd", grad_key_r, key_w, preferred_element_type=jnp.float32)
            + jnp.einsum("qc,dc->qd", grad_value_r, value_w, preferred_element_type=jnp.float32)
        ).astype(jnp.bfloat16),
        "tensor",
        scatter_dimension=0,
        tiled=True,
    ).astype(jnp.float32)
    grad_gain_a_part = jnp.sum(grad_normed * scaled_in, axis=0)
    grad_in = grad_middle + norm_backward(grad_normed, scaled_in, root_in, gain_af)
    summed_gain_a, summed_gain_f, summed_router = (
        lax.psum(grad_gain_a_part.astype(jnp.bfloat16), "tensor").astype(jnp.float32),
        lax.psum(grad_gain_f_part.astype(jnp.bfloat16), "tensor").astype(jnp.float32),
        lax.psum(grad_router_part.astype(jnp.bfloat16), "tensor").astype(jnp.float32),
    )
    results = (
        lax.psum_scatter(grad_query_w, "dp", scatter_dimension=0, tiled=True),
        lax.psum_scatter(grad_key_w, "dp", scatter_dimension=0, tiled=True),
        lax.psum_scatter(grad_value_w, "dp", scatter_dimension=0, tiled=True),
        lax.psum_scatter(grad_out_w, "dp", scatter_dimension=1, tiled=True),
        lax.psum_scatter(summed_gain_a, "dp", scatter_dimension=0, tiled=True),
        lax.psum_scatter(summed_gain_f, "dp", scatter_dimension=0, tiled=True),
        lax.psum_scatter(summed_router, "dp", scatter_dimension=0, tiled=True),
        lax.psum_scatter(grad_gate_w, "dp", scatter_dimension=1, tiled=True),
        lax.psum_scatter(grad_upper_w, "dp", scatter_dimension=1, tiled=True),
        lax.psum_scatter(grad_down_w, "dp", scatter_dimension=2, tiled=True),
    )
    grad_gate_sh = results[7]
    grad_upper_sh = results[8]
    grad_down_sh = results[9]
    return (
        layer_out,
        grad_in,
        results[4],
        results[0],
        results[1],
        results[2],
        results[3],
        results[5],
        results[6],
        grad_gate_sh,
        grad_upper_sh,
        grad_down_sh,
    )


def solution(mesh):
    return jax.shard_map(
        per_device,
        mesh=mesh,
        in_specs=(
            P(("dp", "tensor"), None),
            P("dp"),
            P("dp", None),
            P("dp", None),
            P("dp"),
            P("dp", "tensor"),
            P("dp", "tensor"),
            P("dp", "tensor"),
            P("tensor", "dp"),
            P("dp"),
            P("dp", None),
            P(None, "dp", "tensor"),
            P(None, "dp", "tensor"),
            P(None, "tensor", "dp"),
            P(("dp", "tensor"), None),
        ),
        out_specs=(
            P(("dp", "tensor"), None),
            P(("dp", "tensor"), None),
            P("dp"),
            P("dp", "tensor"),
            P("dp", "tensor"),
            P("dp", "tensor"),
            P("tensor", "dp"),
            P("dp"),
            P("dp", None),
            P(None, "dp", "tensor"),
            P(None, "dp", "tensor"),
            P(None, "tensor", "dp"),
        ),
        check_vma=False,
    )
```

profile of v0, /device:TPU:3, one launch (start us, length us, event | category | flops | bytes accessed | tf_op | source)
XLA Modules:
  0.0 2399.9 jit_solution(17227991976646640863)
XLA Ops:
  11.0 30.9 %all-reduce.9 = (bf16[1536]{0:T(1024)(128)(2,1)S(1)}, bf16[1536]{0:T(1024)(128)(2,1)S(1)}) all-reduce(bf16[1536]{0:T(1024)(128)(2,1)S(1)} %dynamic-update-slice, bf16[1536]{0:T(1024)(128)(2,1)S(1)} %dynamic-update-slice.1), channel_id=1, replica_groups=mesh['dp'=16,'tensor'=2] {'dp'}, use_global_device_ids=true, to_apply=%add.4 | all-reduce | flops 3072 | bytes 12288
  47.7 35.5 %all_gather.45 = bf16[1536,128]{1,0:T(8,128)(2,1)S(1)} all-gather(bf16[96,128]{1,0:T(8,128)(2,1)S(1)} %copy-done.55), channel_id=1, replica_groups=mesh['dp'=16,'tensor'=2] {'dp'}, dimensions={0}, use_global_device_ids=true | all-gather | bytes 417792 | tf_op jit(solution)/shard_map/all_gather | solution.py:109
  83.2 31.7 %all_gather.44 = bf16[1536,128]{1,0:T(8,128)(2,1)S(1)} all-gather(bf16[96,128]{1,0:T(8,128)(2,1)S(1)} %copy-done.56), channel_id=1, replica_groups=mesh['dp'=16,'tensor'=2] {'dp'}, dimensions={0}, use_global_device_ids=true | all-gather | bytes 417792 | tf_op jit(solution)/shard_map/all_gather | solution.py:110
  144.6 50.9 %all-gather.15.cloned.1.call-done = bf16[768,1536]{0,1:T(8,128)(2,1)} async-done(((bf16[768,96]{0,1:T(8,128)(2,1)}), bf16[768,1536]{0,1:T(8,128)(2,1)}) %all-gather.15.cloned.1.call-update) | async-done | bytes 2359312 | tf_op jit(solution)/shard_map/all_gather | solution.py:111
  215.3 29.0 %all-gather = bf16[16,96,8]{1,2,0:T(8,128)(2,1)S(1)} all-gather(bf16[1,96,8]{1,2,0:T(8,128)(2,1)S(1)} %bitcast.205), channel_id=1, replica_groups=mesh['dp'=16,'tensor'=2] {'dp'}, dimensions={0}, use_global_device_ids=true | all-gather | bytes 26112 | tf_op jit(solution)/shard_map/all_gather | solution.py:166
  253.2 11.8 gather_fusion
  268.3 11.8 gather_fusion.1
  303.2 12.5 gather_fusion.6
  333.7 26.5 %all-gather.19.cloned.1.call-done = bf16[8,1536,384]{2,1,0:T(8,128)(2,1)} async-done(((bf16[8,96,384]{2,1,0:T(8,128)(2,1)}), bf16[8,1536,384]{2,1,0:T(8,128)(2,1)}) %all-gather.19.cloned.1.call-update) | async-done | bytes 9437200 | tf_op jit(solution)/shard_map/all_gather | solution.py:167
  371.5 112.3 %all-gather.21.cloned.1.call-done = bf16[8,1536,384]{2,1,0:T(8,128)(2,1)} async-done(((bf16[8,96,384]{2,1,0:T(8,128)(2,1)}), bf16[8,1536,384]{2,1,0:T(8,128)(2,1)}) %all-gather.21.cloned.1.call-update) | async-done | bytes 9437200 | tf_op jit(solution)/shard_map/all_gather | solution.py:168
  495.1 112.4 %all-gather.23.cloned.1.call-done = bf16[8,384,1536]{1,2,0:T(8,128)(2,1)} async-done(((bf16[8,384,96]{1,2,0:T(8,128)(2,1)}), bf16[8,384,1536]{1,2,0:T(8,128)(2,1)}) %all-gather.23.cloned.1.call-update) | async-done | bytes 9437200 | tf_op jit(solution)/shard_map/all_gather | solution.py:169
  607.5 13.5 multiply_convert_fusion
  621.1 13.5 fusion.94
  646.2 19.5 gather_fusion.3
  665.7 14.8 reshape.455
  680.5 17.0 multiply_reduce_fusion
  697.6 13.3 fusion.95
  710.9 15.5 convolution_add_fusion
  737.9 19.3 gather_fusion.5
  757.2 14.7 reshape.457
  772.0 12.4 reduce_sum.141
  867.1 12.0 fusion.4
  880.5 11.8 fusion.100
  906.4 58.2 %all-reduce.8 = (f32[1536]{0:T(1024)S(1)}, f32[1536]{0:T(1024)S(1)}) all-reduce(bf16[1536]{0:T(1024)(128)(2,1)S(1)} %get-tuple-element.22, bf16[1536]{0:T(1024)(128)(2,1)S(1)} %get-tuple-element.23), channel_id=7, replica_groups=mesh['dp'=16,'tensor'=2] {'dp'}, use_global_device_ids=true, to_apply=%region_27.28.clone | all-reduce | flops 3072 | bytes 18432
  970.4 14.4 reduce-scatter.42.cloned.1.call-done
  986.2 124.9 %reduce-scatter.28.cloned.1.call-done = f32[96,128]{1,0:T(8,128)} async-done(((f32[1536,128]{1,0:T(8,128)}), f32[96,128]{1,0:T(8,128)}) %reduce-scatter.28.cloned.1.call-update) | async-done | bytes 49168 | tf_op jit(solution)/shard_map/reduce_scatter | solution.py:314
  1111.1 126.4 %reduce-scatter.30.cloned.1.call-done = f32[96,128]{1,0:T(8,128)} async-done(((f32[1536,128]{1,0:T(8,128)}), f32[96,128]{1,0:T(8,128)}) %reduce-scatter.30.cloned.1.call-update) | async-done | bytes 49168 | tf_op jit(solution)/shard_map/reduce_scatter | solution.py:315
  1237.6 141.5 %reduce-scatter.32.cloned.1.call-done = f32[768,96]{0,1:T(8,128)} async-done(((f32[768,1536]{0,1:T(8,128)}), f32[768,96]{0,1:T(8,128)}) %reduce-scatter.32.cloned.1.call-update) | async-done | bytes 294928 | tf_op jit(solution)/shard_map/reduce_scatter | solution.py:316
  1379.0 142.9 %reduce-scatter.26.cloned.1.call-done = f32[96,768]{1,0:T(8,128)} async-done(((f32[1536,768]{1,0:T(8,128)}), f32[96,768]{1,0:T(8,128)}) %reduce-scatter.26.cloned.1.call-update) | async-done | bytes 294928 | tf_op jit(solution)/shard_map/reduce_scatter | solution.py:313
  1521.9 290.4 %reduce-scatter.38.cloned.1.call-done = f32[8,384,96]{1,2,0:T(8,128)} async-done(((f32[8,384,1536]{1,2,0:T(8,128)}), f32[8,384,96]{1,2,0:T(8,128)}) %reduce-scatter.38.cloned.1.call-update) | async-done | bytes 1179664 | tf_op jit(solution)/shard_map/reduce_scatter | solution.py:322
  1812.3 290.2 %reduce-scatter.34.cloned.1.call-done = f32[8,96,384]{2,1,0:T(8,128)} async-done(((f32[8,1536,384]{2,1,0:T(8,128)}), f32[8,96,384]{2,1,0:T(8,128)}) %reduce-scatter.34.cloned.1.call-update) | async-done | bytes 1179664 | tf_op jit(solution)/shard_map/reduce_scatter | solution.py:320
  2102.5 290.1 %reduce-scatter.36.cloned.1.call-done = f32[8,96,384]{2,1,0:T(8,128)} async-done(((f32[8,1536,384]{2,1,0:T(8,128)}), f32[8,96,384]{2,1,0:T(8,128)}) %reduce-scatter.36.cloned.1.call-update) | async-done | bytes 1179664 | tf_op jit(solution)/shard_map/reduce_scatter | solution.py:321
  (304 shorter events, 260.8 us)
Async XLA Ops:
  7.2 40.5 %copy-start.55 = (bf16[96,128]{1,0:T(8,128)(2,1)S(1)}, bf16[96,128]{1,0:T(8,128)(2,1)}, u32[]{:S(2)}) copy-start(bf16[96,128]{1,0:T(8,128)(2,1)} %param.21) | copy-start | bytes 73732
  7.2 76.1 %copy-start.56 = (bf16[96,128]{1,0:T(8,128)(2,1)S(1)}, bf16[96,128]{1,0:T(8,128)(2,1)}, u32[]{:S(2)}) copy-start(bf16[96,128]{1,0:T(8,128)(2,1)} %param.22) | copy-start | bytes 73732
  7.2 107.7 %copy-start.61 = (s32[512]{0:T(512)S(1)}, s32[512]{0:T(512)}, u32[]{:S(2)}) copy-start(s32[512]{0:T(512)} %param.16) | copy-start | bytes 6148
  7.2 110.3 %all-gather.11.cloned.1.call-start = ((), (), s32[]{:S(2)}) async-start(), calls=%async_computation.13 | async-start | bytes 2359296 | tf_op jit(solution)/shard_map/all_gather | solution.py:116
  46.2 84.3 %all-gather.13.cloned.1.call-start = ((), (), s32[]{:S(2)}) async-start(), calls=%async_computation.14 | async-start | bytes 2506752 | tf_op jit(solution)/shard_map/all_gather | solution.py:108
  46.9 148.6 %all-gather.15.cloned.1.call-start = ((), (), s32[]{:S(2)}) async-start(), calls=%async_computation.15 | async-start | bytes 2506752 | tf_op jit(solution)/shard_map/all_gather | solution.py:111
  47.7 161.5 %reduce-scatter.18.cloned.1.call-start = ((), (), s32[]{:S(2)}) async-start(), calls=%async_computation.16 | async-start | bytes 2359296 | tf_op jit(solution)/shard_map/reduce_scatter | solution.py:157
  47.7 74.6 %copy-start.63 = (f32[64]{0:T(128)}, f32[64]{0:T(128)S(1)}, u32[]{:S(2)}) copy-start(f32[64]{0:T(128)S(1)} %multiply_power_fusion) | copy-start | bytes 772
  83.2 39.1 %copy-start.25 = (bf16[1536,128]{1,0:T(8,128)(2,1)}, bf16[1536,128]{1,0:T(8,128)(2,1)S(1)}, u32[]{:S(2)}) copy-start(bf16[1536,128]{1,0:T(8,128)(2,1)S(1)} %all_gather.45) | copy-start | bytes 1179652
  144.6 50.9 %copy-start.66 = (bf16[128,6,512]{2,0,1:T(8,128)(2,1)}, bf16[128,6,512]{2,0,1:T(8,128)(2,1)S(1)}, u32[]{:S(2)}) copy-start(bf16[128,6,512]{2,0,1:T(8,128)(2,1)S(1)} %fusion.36) | copy-start | bytes 2359300
  199.8 89.0 %all-gather.25.cloned.1.call-start = ((), (), s32[]{:S(2)}) async-start(), calls=%async_computation.22 | async-start | bytes 2359296 | tf_op jit(solution)/shard_map/all_gather | solution.py:193
  200.4 100.9 %all-gather.17.cloned.1.call-start = ((), (), s32[]{:S(2)}) async-start(), calls=%async_computation.17 | async-start | bytes 2359296 | tf_op jit(solution)/shard_map/all_gather | solution.py:173
  213.0 147.1 %all-gather.19.cloned.1.call-start = ((), (), s32[]{:S(2)}) async-start(), calls=%async_computation.18 | async-start | bytes 10027008 | tf_op jit(solution)/shard_map/all_gather | solution.py:167
  213.8 270.1 %all-gather.21.cloned.1.call-start = ((), (), s32[]{:S(2)}) async-start(), calls=%async_computation.19 | async-start | bytes 10027008 | tf_op jit(solution)/shard_map/all_gather | solution.py:168
  214.5 393.0 %all-gather.23.cloned.1.call-start = ((), (), s32[]{:S(2)}) async-start(), calls=%async_computation.20 | async-start | bytes 10027008 | tf_op jit(solution)/shard_map/all_gather | solution.py:169
  215.3 569.2 %reduce-scatter.40.cloned.1.call-start = ((), (), s32[]{:S(2)}) async-start(), calls=%async_computation.33 | async-start | bytes 196608
  244.5 56.8 %copy-start.48 = (bf16[1536,8]{0,1:T(8,128)(2,1)}, bf16[1536,8]{0,1:T(8,128)(2,1)S(1)}, u32[]{:S(2)}) copy-start(bf16[1536,8]{0,1:T(8,128)(2,1)S(1)} %reshape.557) | copy-start | bytes 73732
  324.8 282.7 %copy-start.38 = (f32[8,288]{1,0:T(8,128)}, f32[8,288]{1,0:T(8,128)S(1)}, u32[]{:S(2)}) copy-start(f32[8,288]{1,0:T(8,128)S(1)} %mul.494) | copy-start | bytes 27652
  697.5 95.5 %reduce-scatter.22.cloned.1.call-start = ((), (), s32[]{:S(2)}) async-start(), calls=%async_computation.23 | async-start | bytes 2359296 | tf_op jit(solution)/shard_map/reduce_scatter | solution.py:222
  784.4 25.1 %all-gather.27.cloned.1.call-start = ((), (), s32[]{:S(2)}) async-start(), calls=%async_computation.24 | async-start | bytes 2359296 | tf_op jit(solution)/shard_map/all_gather | solution.py:258
  798.3 47.4 %reduce-scatter.24.cloned.1.call-start = ((), (), s32[]{:S(2)}) async-start(), calls=%async_computation.25 | async-start | bytes 2359296 | tf_op jit(solution)/shard_map/reduce_scatter | solution.py:295
  835.4 130.3 %reduce-scatter.20.cloned.1.call-start = ((), (), s32[]{:S(2)}) async-start(), calls=%async_computation.21 | async-start | bytes 2359296 | tf_op jit(solution)/shard_map/reduce_scatter | solution.py:189
  836.0 148.8 %reduce-scatter.42.cloned.1.call-start = ((), (), s32[]{:S(2)}) async-start(), calls=%async_computation.34 | async-start | bytes 835584
  852.2 259.0 %reduce-scatter.28.cloned.1.call-start = ((), (), s32[]{:S(2)}) async-start(), calls=%async_computation.27 | async-start | bytes 835584 | tf_op jit(solution)/shard_map/reduce_scatter | solution.py:314
  853.8 383.8 %reduce-scatter.30.cloned.1.call-start = ((), (), s32[]{:S(2)}) async-start(), calls=%async_computation.28 | async-start | bytes 835584 | tf_op jit(solution)/shard_map/reduce_scatter | solution.py:315
  855.3 523.7 %reduce-scatter.32.cloned.1.call-start = ((), (), s32[]{:S(2)}) async-start(), calls=%async_computation.29 | async-start | bytes 5013504 | tf_op jit(solution)/shard_map/reduce_scatter | solution.py:316
  860.8 661.2 %reduce-scatter.26.cloned.1.call-start = ((), (), s32[]{:S(2)}) async-start(), calls=%async_computation.26 | async-start | bytes 5013504 | tf_op jit(solution)/shard_map/reduce_scatter | solution.py:313
  865.6 946.7 %reduce-scatter.38.cloned.1.call-start = ((), (), s32[]{:S(2)}) async-start(), calls=%async_computation.32 | async-start | bytes 20054016 | tf_op jit(solution)/shard_map/reduce_scatter | solution.py:322
  879.1 1223.4 %reduce-scatter.34.cloned.1.call-start = ((), (), s32[]{:S(2)}) async-start(), calls=%async_computation.30 | async-start | bytes 20054016 | tf_op jit(solution)/shard_map/reduce_scatter | solution.py:320
  892.4 1500.2 %reduce-scatter.36.cloned.1.call-start = ((), (), s32[]{:S(2)}) async-start(), calls=%async_computation.31 | async-start | bytes 20054016 | tf_op jit(solution)/shard_map/reduce_scatter | solution.py:321
  905.6 60.1 %copy-start.9 = (bf16[256,1536]{1,0:T(8,128)(2,1)S(1)}, bf16[256,1536]{1,0:T(8,128)(2,1)}, u32[]{:S(2)}) copy-start(bf16[256,1536]{1,0:T(8,128)(2,1)} %reduce-scatter.18.cloned.1.call-done) | copy-start | bytes 2359300
  905.6 60.1 %copy-start.19 = (bf16[256,1536]{1,0:T(8,128)(2,1)S(1)}, bf16[256,1536]{1,0:T(8,128)(2,1)}, u32[]{:S(2)}) copy-start(bf16[256,1536]{1,0:T(8,128)(2,1)} %param.29) | copy-start | bytes 2359300
  (59 other events, 526.0 us)
Sparse Core Ops, SparseCore 0:
  46.3 17.9 all-gather.10
  67.1 63.3 all-gather.12
  133.3 62.1 all-gather.14
  199.9 9.2 reduce-scatter.17
  210.6 11.0 all-gather.24
  223.7 10.9 all-gather.16
  237.8 122.3 all-gather.18
  363.2 120.5 all-gather.20
  486.9 120.5 all-gather.22
  697.7 6.9 reduce-scatter.39
  784.5 8.4 reduce-scatter.21
  798.5 11.0 all-gather.26
  835.5 10.2 reduce-scatter.23
  848.5 10.2 reduce-scatter.19
  863.4 121.3 reduce-scatter.41
  989.9 121.2 reduce-scatter.27
  1116.3 121.2 reduce-scatter.29
  1243.2 135.8 reduce-scatter.31
  1385.6 136.2 reduce-scatter.25
  1528.1 284.1 reduce-scatter.37
  1818.7 283.7 reduce-scatter.33
  2108.9 283.6 reduce-scatter.35
where the time goes:
time: 2410 us; the launch traced here: 2400 us
  waiting for transfers between devices  1770 us (73%)
  local copies, waits for them, and re-layouts  195 us (8%)
  blocking collectives  189 us (8%)
  matrix products  168 us (7%)
  other arithmetic  59.2 us (2%)
    reduce_scatter x1, waiting for transfers between devices, per_device(): lax.psum_scatter(grad_down_w, 'dp', scatter_dimension=2, tiled=True)  290 us
    reduce_scatter x1, waiting for transfers between devices, per_device(): lax.psum_scatter(grad_gate_w, 'dp', scatter_dimension=1, tiled=True)  290 us
    reduce_scatter x1, waiting for transfers between devices, per_device(): lax.psum_scatter(grad_upper_w, 'dp', scatter_dimension=1, tiled=True)  290 us
    reduce_scatter x1, waiting for transfers between devices, per_device(): lax.psum_scatter(grad_query_w, 'dp', scatter_dimension=0, tiled=True)  143 us
    reduce_scatter x1, waiting for transfers between devices, per_device(): lax.psum_scatter(grad_out_w, 'dp', scatter_dimension=1, tiled=True)  141 us
    reduce_scatter x1, waiting for transfers between devices, per_device(): lax.psum_scatter(grad_value_w, 'dp', scatter_dimension=0, tiled=True)  126 us
    reduce_scatter x1, waiting for transfers between devices, per_device(): lax.psum_scatter(grad_key_w, 'dp', scatter_dimension=0, tiled=True)  125 us
    all_gather x1, waiting for transfers between devices, per_device(): lax.all_gather(w_down, 'dp', axis=2, tiled=True)  112 us
  transfers between devices with their start and end apart: 22, of which 17 were waited for; matrix products, arithmetic and copies ran while one was open for 12% of the time, Pallas kernels for 0%

commit v1 on v0

v1 whole, which is shorter than its diff:
```python
import functools
import math

import jax
import jax.numpy as jnp
from jax import lax
from jax.experimental import pallas as pl
from jax.experimental.pallas import tpu as pltpu
from jax.sharding import PartitionSpec as P

HD = 128
EXTRA = 128
CUBE = 8
epsilon = 1e-06
highest = lax.Precision.HIGHEST
f32 = jnp.float32
bf16 = jnp.bfloat16
NN = (((1,), (0,)), ((), ()))
NT = (((1,), (1,)), ((), ()))


def rms_parts(values):
    inverse_root = lax.rsqrt(jnp.mean(values * values, axis=-1, keepdims=True) + epsilon)
    return (values * inverse_root, inverse_root)


def norm_backward(grad_normed, scaled, inverse_root, gain):
    grad_scaled = grad_normed * gain
    inner = jnp.mean(grad_scaled * scaled, axis=-1, keepdims=True)
    return inverse_root * (grad_scaled - scaled * inner)


def rope_tables(length, size):
    inverse = 10000.0 ** (-jnp.arange(size // 2, dtype=f32) / (size // 2))
    angle = jnp.arange(length, dtype=f32)[:, None] * inverse[None, :]
    return (jnp.cos(angle), jnp.sin(angle))


def rotate(values, cosine, sine_table):
    half_size = values.shape[-1] // 2
    first_half = values[..., :half_size]
    second = values[..., half_size:]
    cos_wide = cosine[:, None, :]
    sin_wide = sine_table[:, None, :]
    return jnp.concatenate(
        [first_half * cos_wide - second * sin_wide, second * cos_wide + first_half * sin_wide],
        axis=-1,
    )


def swap(values, bit, count):
    return lax.ppermute(values, "dp", [(i, i ^ bit) for i in range(count)])


def swap_core(values):
    return lax.ppermute(values, "tensor", [(0, 1), (1, 0)])


def thirds(rows):
    unit = 16 if rows % 16 == 0 and rows >= 48 else 1
    part = rows // unit // 3 * unit
    return ((0, rows - 2 * part), (rows - 2 * part, rows - part), (rows - part, rows))


def cut(values, span, axis):
    return lax.slice_in_dim(values, span[0], span[1], axis=axis)


def cube_gather(own, count, axis):
    got = {0: own}
    for bit in (1, 2, 4):
        got[bit] = swap(own, bit, count)
    got[3] = swap(got[2], 1, count)
    got[6] = swap(got[4], 2, count)
    got[5] = swap(got[1], 4, count)
    spans = thirds(own.shape[axis])
    got[7] = (
        swap(cut(got[6], spans[0], axis), 1, count),
        swap(cut(got[5], spans[1], axis), 2, count),
        swap(cut(got[3], spans[2], axis), 4, count),
    )
    return got


def add_round(left, right):
    return (left.astype(f32) + right.astype(f32)).astype(bf16)


def cube_sum(parts, count, axis):
    spans = thirds(parts[0].shape[axis])
    first = swap(cut(parts[7], spans[0], axis), 1, count)
    second = swap(cut(parts[7], spans[1], axis), 2, count)
    third = swap(cut(parts[7], spans[2], axis), 4, count)

    def patched(whole, extra, at):
        pieces = [cut(whole, span, axis) for span in spans]
        pieces[at] = add_round(pieces[at], extra)
        return jnp.concatenate(pieces, axis=axis)

    got2 = swap(patched(parts[3], third, 2), 1, count)
    got4 = swap(patched(parts[6], first, 0), 2, count)
    got1 = swap(patched(parts[5], second, 1), 4, count)
    last = (
        swap(add_round(parts[1], got1), 1, count),
        swap(add_round(parts[2], got2), 2, count),
        swap(add_round(parts[4], got4), 4, count),
    )
    return (
        parts[0].astype(f32) + last[0].astype(f32) + last[1].astype(f32) + last[2].astype(f32)
    )


def outer_bits(count):
    bits, bit = [], CUBE
    while bit < count:
        bits.append(bit)
        bit *= 2
    return bits


def outer_gather(own, count):
    pieces = [own[None]]
    for bit in outer_bits(count):
        pieces.append(swap(jnp.concatenate(pieces, axis=0), bit, count))
    return pieces


def place_kernel(copies, me_ref, *refs):
    out, sems = refs[-2], refs[-1]
    started = []
    for number, (source, entry, start, rows, offset, block) in enumerate(copies):
        target = pl.multiple_of((me_ref[0] ^ offset) * block + start, 16)
        copy = pltpu.make_async_copy(
            refs[source].at[entry], out.at[pl.ds(target, rows)], sems.at[number]
        )
        copy.start()
        started.append(copy)
    for copy in started:
        copy.wait()


def gather_rows(shard, me, count):
    block, width = shard.shape
    own = jnp.concatenate(outer_gather(shard, count), axis=0)
    got = cube_gather(own, count, 1)
    outer = own.shape[0]
    if block % 48:
        got[7] = jnp.concatenate(got[7], axis=1)
        stacked = jnp.stack([got[b] for b in range(CUBE)], axis=1)
        order = jnp.arange(count) ^ me
        return stacked.reshape(count, block, width)[order].reshape(count * block, width)
    sources, copies = [], []
    for b in range(CUBE):
        spans = thirds(block) if b == 7 else ((0, block),)
        for span, piece in zip(spans, got[b] if b == 7 else (got[b],)):
            for j in range(outer):
                copies.append((len(sources), j, span[0], span[1] - span[0], 8 * j + b, block))
            sources.append(piece)
    return pl.pallas_call(
        functools.partial(place_kernel, copies),
        out_shape=jax.ShapeDtypeStruct((count * block, width), shard.dtype),
        in_specs=[pl.BlockSpec(memory_space=pltpu.SMEM)]
        + [pl.BlockSpec(memory_space=pl.ANY)] * len(sources),
        out_specs=pl.BlockSpec(memory_space=pltpu.VMEM),
        scratch_shapes=[pltpu.SemaphoreType.DMA((len(copies),))],
        compiler_params=pltpu.CompilerParams(vmem_limit_bytes=24 * 1024 * 1024),
        name="place_rows",
    )(me.reshape(1), *sources)


def scatter_rows(whole, me, count):
    block = whole.shape[0] // count
    outer = count // CUBE
    offsets = jnp.arange(outer)[None, :] * CUBE + jnp.arange(CUBE)[:, None]
    parts = whole.astype(bf16).reshape(count, block, -1)[(offsets ^ me).reshape(-1)]
    parts = parts.reshape(CUBE, outer, block, -1)
    total = cube_sum([parts[b] for b in range(CUBE)], count, 1)
    for bit in reversed(outer_bits(count)):
        half = total.shape[0] // 2
        total = total[:half] + swap(total[half:].astype(bf16), bit, count).astype(f32)
    return total[0]


def gelu_parts(value):
    square = value * value
    inner = value * (0.7978845608028654 + 0.035677408136300125 * square)
    tanh = jnp.tanh(inner)
    half = 0.5 + 0.5 * tanh
    slope = half + 0.5 * value * (1.0 - tanh * tanh) * (
        0.7978845608028654 + 3.0 * 0.035677408136300125 * square
    )
    return value * half, slope


def moe_kernel(copies, hidden, me_ref, x_ref, g_ref, router_ref, *refs):
    count = len(set(c[0] for c in copies))
    sources = refs[:count]
    (branch_ref, gradn_ref, act_own, act_other, gp_own, gp_other, geo_ref) = refs[count : count + 7]
    weights, sems = refs[count + 7 :]

    @pl.when(pl.program_id(0) == 0)
    def _():
        started = []
        for number, (source, entry, rows, offset, from_col, to_col, cols) in enumerate(copies):
            row = pl.multiple_of(((me_ref[0] // CUBE) ^ offset) * rows, 16)
            copy = pltpu.make_async_copy(
                sources[source].at[entry, :, pl.ds(from_col, cols)],
                weights.at[pl.ds(row, rows), pl.ds(to_col, cols)],
                sems.at[number],
            )
            copy.start()
            started.append(copy)
        for copy in started:
            copy.wait()

    whole = 2 * hidden
    expert = me_ref[0] % CUBE
    x = x_ref[0]
    code = g_ref[0, :, x.shape[1] :].astype(f32)
    lanes = lax.broadcasted_iota(jnp.int32, code.shape, 1)
    logits = lax.dot_general(x, router_ref[...], NN, preferred_element_type=f32)
    routed = code > 0.5
    logits = jnp.where(routed, logits, -1e30)
    expo = jnp.where(routed, jnp.exp(logits - jnp.max(logits, axis=1, keepdims=True)), 0.0)
    gates = expo / jnp.sum(expo, axis=1, keepdims=True)
    kept = (lanes == expert) & (code > 1.5)
    gate = jnp.sum(jnp.where(kept, gates, 0.0), axis=1, keepdims=True)

    pre = lax.dot_general(x, weights[:, : 2 * whole], NN, preferred_element_type=f32)
    gate_pre, up_pre = pre[:, :whole], pre[:, whole:]
    gelu, slope = gelu_parts(gate_pre)
    act = (gelu * up_pre).astype(bf16)
    act_own[0] = act[:, :hidden]
    act_other[0] = act[:, hidden:]
    down = weights[:, 2 * whole :]
    expert_out = lax.dot_general(act, down, NT, preferred_element_type=f32)
    branch_ref[0] = (gate * expert_out).astype(bf16)
    g = g_ref[0, :, : x.shape[1]].astype(f32)
    grad_gate = jnp.sum(g * expert_out, axis=1, keepdims=True)
    gradn_ref[0, :, x.shape[1] :] = jnp.where(kept, grad_gate, 0.0).astype(bf16)
    geo = (gate * g).astype(bf16)
    geo_ref[0] = geo
    grad_act = lax.dot_general(geo, down, NN, preferred_element_type=f32)
    grad_gate_pre = (grad_act * up_pre * slope).astype(bf16)
    grad_up_pre = (grad_act * gelu).astype(bf16)
    gp_own[0, :, :hidden] = grad_gate_pre[:, :hidden]
    gp_own[0, :, hidden:] = grad_up_pre[:, :hidden]
    gp_other[0, :, :hidden] = grad_gate_pre[:, hidden:]
    gp_other[0, :, hidden:] = grad_up_pre[:, hidden:]
    grad_in = lax.dot_general(
        grad_gate_pre, weights[:, :whole], NT, preferred_element_type=f32
    ) + lax.dot_general(
        grad_up_pre, weights[:, whole : 2 * whole], NT, preferred_element_type=f32
    )
    gradn_ref[0, :, : x.shape[1]] = grad_in.astype(bf16)


def moe(me, x, g, router, pieces, hidden):
    blocks, rows, width = x.shape
    copies = []
    for source, (array, first, side) in enumerate(pieces):
        for entry in range(array.shape[0]):
            for kind in range(3):
                copies.append(
                    (
                        source,
                        entry,
                        array.shape[1],
                        first + entry,
                        kind * hidden,
                        (2 * kind + side) * hidden,
                        hidden,
                    )
                )

    def block(cols):
        return pl.BlockSpec((1, rows, cols), lambda b, me: (b, 0, 0))

    def out(cols):
        return jax.ShapeDtypeStruct((blocks, rows, cols), bf16)

    widths = (width, width + EXTRA, hidden, hidden, 2 * hidden, 2 * hidden, width)
    flops = 2 * blocks * rows * width * hidden * 12
    return pl.pallas_call(
        functools.partial(moe_kernel, copies, hidden),
        out_shape=[out(w) for w in widths],
        grid_spec=pltpu.PrefetchScalarGridSpec(
            num_scalar_prefetch=1,
            grid=(blocks,),
            in_specs=[
                block(width),
                block(width + EXTRA),
                pl.BlockSpec((width, EXTRA), lambda b, me: (0, 0)),
            ]
            + [pl.BlockSpec(memory_space=pl.ANY)] * len(pieces),
            out_specs=[block(w) for w in widths],
            scratch_shapes=[
                pltpu.VMEM((width, 6 * hidden), bf16),
                pltpu.SemaphoreType.DMA((len(copies),)),
            ],
        ),
        compiler_params=pltpu.CompilerParams(vmem_limit_bytes=60 * 1024 * 1024),
        cost_estimate=pl.CostEstimate(flops=flops, bytes_accessed=50_000_000, transcendentals=0),
        name="experts",
    )(me.reshape(1), x, g, router, *[p[0] for p in pieces])


def per_device(
    count,
    hidden_in,
    segment_ids,
    routes,
    slot_order,
    gain_attn,
    w_query,
    w_key,
    w_value,
    w_out,
    gain_ffn,
    w_router,
    w_gate,
    w_up,
    w_down,
    grad_out,
):
    tok_rows, width = hidden_in.shape
    seq_len = segment_ids.shape[0]
    top_count = routes.shape[1]
    experts, block, hidden = w_gate.shape
    capacity = 9 * seq_len * top_count // (8 * experts)
    me = lax.axis_index("dp").astype(jnp.int32)
    core = lax.axis_index("tensor").astype(jnp.int32)
    groups = [list(range(at, at + CUBE)) for at in range(0, count, CUBE)]

    def both_halves(mine):
        other = swap_core(mine)
        return jnp.where(
            core == 0,
            jnp.concatenate([mine, other], axis=0),
            jnp.concatenate([other, mine], axis=0),
        )

    expert_shard = jnp.concatenate([w_gate, w_up, jnp.swapaxes(w_down, 1, 2)], axis=2)
    expert_rows = lax.all_to_all(
        expert_shard.reshape(experts * block, 3 * hidden),
        "dp",
        0,
        0,
        tiled=True,
        axis_index_groups=groups,
    )

    small = jnp.concatenate([gain_attn[:, None], gain_ffn[:, None], w_router], axis=1)
    small = jnp.pad(small, ((0, 0), (0, EXTRA - small.shape[1])))
    shard_qkv = jnp.concatenate([w_query, w_key, w_value, small], axis=1)
    full_qkv = gather_rows(shard_qkv, me, count)
    out_wt = gather_rows(w_out.T, me, count)
    heads_cols, kv_cols = w_query.shape[1], w_key.shape[1]
    qkv_cols = heads_cols + 2 * kv_cols
    query_w = full_qkv[:, :heads_cols]
    key_w = full_qkv[:, heads_cols : heads_cols + kv_cols]
    value_w = full_qkv[:, heads_cols + kv_cols : qkv_cols]
    gain_af = full_qkv[:, qkv_cols].astype(f32)
    gain_ff = full_qkv[:, qkv_cols + 1].astype(f32)
    router_w = full_qkv[:, qkv_cols + 2 : qkv_cols + 2 + experts]
    router_pad = jnp.pad(router_w, ((0, 0), (0, EXTRA - experts)))

    order = jnp.min(
        jnp.where(
            routes[:, :, None] == jnp.arange(experts, dtype=jnp.int32),
            slot_order[0].reshape(seq_len, top_count)[:, :, None],
            seq_len * top_count,
        ),
        axis=1,
    )
    order_own = lax.dynamic_slice_in_dim(order, core * tok_rows, tok_rows, 0)
    ahead = jnp.sum((order[None, :, :] < order_own[:, None, :]).astype(jnp.int32), axis=1)
    routed_own = order_own < seq_len * top_count
    kept_own = routed_own & (ahead < capacity)
    code_own = routed_own.astype(bf16) + kept_own.astype(bf16)
    code_own = jnp.pad(code_own, ((0, 0), (0, EXTRA - experts)))

    hidden_full = both_halves(hidden_in).astype(f32)
    scaled_full, _ = rms_parts(hidden_full)
    scaled_in, root_in = rms_parts(hidden_in.astype(f32))
    normed = (scaled_full * gain_af).astype(bf16)
    head_count = heads_cols // HD
    kv_local = kv_cols // HD
    per_group = head_count // kv_local
    cosine, sine_table = rope_tables(seq_len, HD)
    qkv = jnp.dot(normed, full_qkv[:, :qkv_cols], preferred_element_type=f32)
    query_f = qkv[:, :heads_cols].reshape(seq_len, head_count, HD)
    key_f = qkv[:, heads_cols : heads_cols + kv_cols].reshape(seq_len, kv_local, HD)
    value_r = qkv[:, heads_cols + kv_cols :].astype(bf16).reshape(seq_len, kv_local, HD)
    query_r = rotate(query_f, cosine, sine_table).astype(bf16)
    key_r = rotate(key_f, cosine, sine_table).astype(bf16)
    query_g = query_r.reshape(seq_len, kv_local, per_group, HD)
    scale = 1.0 / math.sqrt(HD)
    positions = jnp.arange(seq_len, dtype=jnp.int32)

    def block_scores():
        raw = jnp.einsum("qgrd,kgd->grqk", query_g, key_r, preferred_element_type=f32) * scale
        allowed = (segment_ids[:, None] == segment_ids[None, :]) & (
            positions[None, :] <= positions[:, None]
        )
        return jnp.where(allowed[None, None], raw, -1e30)

    masked = block_scores()
    peak = jnp.max(masked, axis=-1, keepdims=True)
    expo_vals = jnp.exp(masked - peak)
    total = jnp.sum(expo_vals, axis=-1, keepdims=True)
    probabilities = (expo_vals / total).astype(bf16)
    mixed_block = jnp.einsum("grqk,kgd->qgrd", probabilities, value_r, preferred_element_type=f32)
    mixed = mixed_block.reshape(seq_len, head_count * HD).astype(bf16)
    lse = peak + jnp.log(total)
    attn_part = jnp.einsum("qc,dc->qd", mixed, out_wt, preferred_element_type=f32)

    def sum_cores(part):
        mine = lax.dynamic_slice_in_dim(part, core * tok_rows, tok_rows, 0)
        other = lax.dynamic_slice_in_dim(part, (1 - core) * tok_rows, tok_rows, 0)
        return mine + swap_core(other.astype(bf16)).astype(f32)

    middle = hidden_in.astype(f32) + sum_cores(attn_part)
    scaled_mid, root_mid = rms_parts(middle)
    normed2 = (scaled_mid * gain_ff).astype(bf16)

    def stacked(got):
        return jnp.stack([got[b] for b in range(7)] + [jnp.concatenate(got[7], axis=0)], axis=0)

    grads_cube = stacked(
        cube_gather(jnp.concatenate([grad_out, code_own], axis=1), count, 0)
    )
    normed_cube = stacked(cube_gather(normed2, count, 0))
    pieces, first = [], 0
    for array in outer_gather(expert_rows, count):
        pieces.append((array, first, 0))
        pieces.append((swap_core(array), first, 1))
        first += array.shape[0]
    branch, gradn, act_own, act_other, gp_own, gp_other, geo = moe(
        me, normed_cube, grads_cube, router_pad, pieces, hidden
    )
    gradn_sum = cube_sum([gradn[b] for b in range(CUBE)], count, 0)
    branch_sum = cube_sum([branch[b] for b in range(CUBE)], count, 0)
    layer_out = middle + branch_sum

    def flat(values):
        return values.reshape(-1, values.shape[-1])

    def weight_grads(gp, act):
        return jnp.concatenate(
            [
                jnp.einsum("td,th->dh", flat(normed_cube), flat(gp), preferred_element_type=f32),
                jnp.einsum("td,th->dh", flat(geo), flat(act), preferred_element_type=f32),
            ],
            axis=1,
        ).astype(bf16)

    expert_grads = weight_grads(gp_own, act_own).astype(f32) + swap_core(
        weight_grads(gp_other, act_other)
    ).astype(f32)
    for bit in reversed(outer_bits(count)):
        half = expert_grads.shape[0] // 2
        high = (me // bit) % 2
        keep = lax.dynamic_slice_in_dim(expert_grads, high * half, half, 0)
        send = lax.dynamic_slice_in_dim(expert_grads, (1 - high) * half, half, 0)
        expert_grads = keep + swap(send.astype(bf16), bit, count).astype(f32)
    expert_grads = (
        lax.all_to_all(
            expert_grads.astype(bf16), "dp", 0, 0, tiled=True, axis_index_groups=groups
        )
        .reshape(experts, block, 3 * hidden)
        .astype(f32)
    )
    grad_gate_w = expert_grads[:, :, :hidden]
    grad_up_w = expert_grads[:, :, hidden : 2 * hidden]
    grad_down_w = jnp.swapaxes(expert_grads[:, :, 2 * hidden :], 1, 2)

    logits = jnp.dot(normed2, router_w, preferred_element_type=f32)
    logits = jnp.where(routed_own, logits, -1e30)
    expo = jnp.where(routed_own, jnp.exp(logits - jnp.max(logits, axis=1, keepdims=True)), 0.0)
    gates = expo / jnp.sum(expo, axis=1, keepdims=True)
    grad_gates = gradn_sum[:, width : width + experts]
    grad_logits = gates * (grad_gates - jnp.sum(gates * grad_gates, axis=1, keepdims=True))
    grad_normed2 = gradn_sum[:, :width] + jnp.einsum(
        "te,de->td", grad_logits, router_w.astype(f32), precision=highest
    )
    grad_router = jnp.einsum("td,te->de", normed2.astype(f32), grad_logits, precision=highest)
    grad_gain_f = jnp.sum(grad_normed2 * scaled_mid, axis=0)
    grad_middle = grad_out.astype(f32) + norm_backward(
        grad_normed2, scaled_mid, root_mid, gain_ff
    )

    grad_mid_full = both_halves(grad_middle.astype(bf16))
    grad_out_wt = jnp.einsum("qd,qc->dc", grad_mid_full, mixed, preferred_element_type=f32)
    small_f = jnp.concatenate([grad_gain_f[:, None], grad_router], axis=1)
    small_f = jnp.pad(small_f, ((0, 0), (0, EXTRA - small_f.shape[1]))).astype(bf16)
    small_f = small_f.astype(f32) + swap_core(small_f).astype(f32)
    out_grads = scatter_rows(
        jnp.concatenate([grad_out_wt, small_f], axis=1).astype(bf16), me, count
    )
    grad_mixed = jnp.dot(grad_mid_full, out_wt, preferred_element_type=f32)
    grad_mixed = grad_mixed.astype(bf16).reshape(seq_len, kv_local, per_group, HD)
    probs_float = jnp.exp(block_scores() - lse)
    probs_r = probs_float.astype(bf16)
    grad_probs = jnp.einsum("qgrd,kgd->grqk", grad_mixed, value_r, preferred_element_type=f32)
    inner = jnp.sum(grad_probs * probs_float, axis=-1, keepdims=True)
    grad_scores = (probs_float * (grad_probs - inner)).astype(bf16)
    grad_query = (
        jnp.einsum("grqk,kgd->qgrd", grad_scores, key_r, preferred_element_type=f32) * scale
    )
    grad_key = (
        jnp.einsum("grqk,qgrd->kgd", grad_scores, query_g, preferred_element_type=f32) * scale
    )
    grad_value = jnp.einsum("grqk,qgrd->kgd", probs_r, grad_mixed, preferred_element_type=f32)
    grad_query = rotate(grad_query.reshape(seq_len, head_count, HD), cosine, -sine_table)
    grad_key = rotate(grad_key, cosine, -sine_table)
    grad_qkv = jnp.concatenate(
        [
            grad_query.astype(bf16).reshape(seq_len, heads_cols),
            grad_key.astype(bf16).reshape(seq_len, kv_cols),
            grad_value.astype(bf16).reshape(seq_len, kv_cols),
        ],
        axis=1,
    )
    grad_qkv_w = jnp.einsum("qd,qc->dc", normed, grad_qkv, preferred_element_type=f32)
    grad_normed_part = jnp.einsum(
        "qc,dc->qd", grad_qkv, full_qkv[:, :qkv_cols], preferred_element_type=f32
    )
    grad_gain_a = jnp.sum(grad_normed_part * scaled_full, axis=0)
    grad_gain_a = grad_gain_a + swap_core(grad_gain_a)
    small_a = jnp.pad(grad_gain_a[:, None], ((0, 0), (0, EXTRA - 1)))
    qkv_grads = scatter_rows(
        jnp.concatenate([grad_qkv_w, small_a], axis=1).astype(bf16), me, count
    )
    grad_normed = sum_cores(grad_normed_part)
    grad_in = grad_middle + norm_backward(grad_normed, scaled_in, root_in, gain_af)
    return (
        layer_out,
        grad_in,
        qkv_grads[:, qkv_cols],
        qkv_grads[:, :heads_cols],
        qkv_grads[:, heads_cols : heads_cols + kv_cols],
        qkv_grads[:, heads_cols + kv_cols : qkv_cols],
        out_grads[:, :heads_cols].T,
        out_grads[:, heads_cols],
        out_grads[:, heads_cols + 1 : heads_cols + 1 + experts],
        grad_gate_w,
        grad_up_w,
        grad_down_w,
    )


def solution(mesh):
    return jax.shard_map(
        functools.partial(per_device, mesh.shape["dp"]),
        mesh=mesh,
        in_specs=(
            P(("dp", "tensor"), None),
            P("dp"),
            P("dp", None),
            P("dp", None),
            P("dp"),
            P("dp", "tensor"),
            P("dp", "tensor"),
            P("dp", "tensor"),
            P("tensor", "dp"),
            P("dp"),
            P("dp", None),
            P(None, "dp", "tensor"),
            P(None, "dp", "tensor"),
            P(None, "tensor", "dp"),
            P(("dp", "tensor"), None),
        ),
        out_specs=(
            P(("dp", "tensor"), None),
            P(("dp", "tensor"), None),
            P("dp"),
            P("dp", "tensor"),
            P("dp", "tensor"),
            P("dp", "tensor"),
            P("tensor", "dp"),
            P("dp"),
            P("dp", None),
            P(None, "dp", "tensor"),
            P(None, "dp", "tensor"),
            P(None, "tensor", "dp"),
        ),
        check_vma=False,
    )
```

time: 2410 us -> 683 us (0.28)
  waiting for transfers between devices: 1770 us -> 294 us
  blocking collectives: 189 us -> 0 us
  local copies, waits for them, and re-layouts: 195 us -> 92.6 us
  matrix products: 168 us -> 66.6 us
  starting transfers between devices: 1.78 us -> 91.1 us
  Pallas kernels: 0 us -> 54 us
    reduce_scatter x11 -> x0, waiting for transfers between devices: 1430 us -> none  [the longest x1 290 us: per_device(): lax.psum_scatter(grad_down_w, 'dp', scatter_dimension=2, tiled=True)]
    all_gather x9 -> x0, waiting for transfers between devices: 321 us -> none  [the longest x1 112 us: per_device(): lax.all_gather(w_down, 'dp', axis=2, tiled=True)]
    ppermute x0 -> x87, waiting for transfers between devices: none -> 294 us  [the longest x78 294 us: swap(): return lax.ppermute(values, 'dp', [(i, i ^ bit) for i in range(count)])]
    dot_general x28 -> x17, matrix products: 162 us -> 59 us  [the longest x2 14.8 us: weight_grads(): jnp.einsum('td,th->dh', flat(normed_cube), flat(gp), preferred_element_ty...]
    all_gather x3 -> x0, blocking collectives: 96.2 us -> none  [the longest x1 35.5 us: per_device(): lax.all_gather(w_key, 'dp', axis=0, tiled=True)]
    unnamed x2 -> x0, blocking collectives: 89.1 us -> none
    gather x11 -> x2, local copies, waits for them, and re-layouts: 93.1 us -> 7.16 us  [scatter_rows(): whole.astype(bf16).reshape(count, block, -1)[(offsets ^ me).reshape(-1)]]
    ppermute x0 -> x87, starting transfers between devices: none -> 81 us  [the longest x78 53 us: swap(): return lax.ppermute(values, 'dp', [(i, i ^ bit) for i in range(count)])]
  transfers between devices with their start and end apart: 22 -> 89, of which waited for: 17 -> 34; matrix products, arithmetic and copies ran while one was open for 12% -> 28% of each run, Pallas kernels for 0% -> 1%
where the time goes in v1:
time: 683 us; the launch traced here: 672 us
  waiting for transfers between devices  294 us (43%)
  local copies, waits for them, and re-layouts  92.6 us (14%)
  starting transfers between devices  91.1 us (13%)
  other arithmetic  70.8 us (10%)
  matrix products  66.6 us (10%)
  Pallas kernels  54 us (8%)
    ppermute x78, waiting for transfers between devices, swap(): return lax.ppermute(values, 'dp', [(i, i ^ bit) for i in range(count)])  294 us
    ppermute x78, starting transfers between devices, swap(): return lax.ppermute(values, 'dp', [(i, i ^ bit) for i in range(count)])  53 us
    pallas_call x1, Pallas kernels, moe(): pl.pallas_call(functools.partial(moe_kernel, copies, hidden), out_shape=[...  45.8 us
    unnamed x225, local copies, waits for them, and re-layouts  41.9 us
    ppermute x9, starting transfers between devices, swap_core(): return lax.ppermute(values, 'tensor', [(0, 1), (1, 0)])  27.9 us
    dot_general x2, matrix products, weight_grads(): jnp.einsum('td,th->dh', flat(normed_cube), flat(gp), preferred_element_ty...  14.8 us
  transfers between devices with their start and end apart: 89, of which 34 were waited for; matrix products, arithmetic and copies ran while one was open for 28% of the time, Pallas kernels for 1%

profile of v1, /device:TPU:3, one launch (start us, length us, event | category | flops | bytes accessed | tf_op | source)
XLA Modules:
  0.0 671.8 jit_solution(1064001148681376130)
XLA Ops:
  6.9 4.8 convert_reduce_fusion
  16.1 5.6 all-to-all-start
  28.4 20.4 %collective-permute-done.15.refs_4_ = bf16[2,96,768]{2,1,0:T(8,128)(2,1)S(1)} collective-permute-done((bf16[2,96,768]{2,1,0:T(8,128)(2,1)S(1)}, bf16[2,96,768]{2,1,0:T(8,128)(2,1)S(1)}, u32[]{:S(2)}, u32[]{:S(2)}) %collective-permute-start.15) | collective-permute-done | bytes 294944 | tf_op jit(solution)/shard_map/ppermute | solution.py:52
  50.0 10.1 %collective-permute-done.12.refs_1_ = bf16[2,96,768]{2,1,0:T(8,128)(2,1)S(1)} collective-permute-done((bf16[2,96,768]{2,1,0:T(8,128)(2,1)S(1)}, bf16[2,96,768]{2,1,0:T(8,128)(2,1)S(1)}, u32[]{:S(2)}, u32[]{:S(2)}) %collective-permute-start.12) | collective-permute-done | bytes 294944 | tf_op jit(solution)/shard_map/ppermute | solution.py:52
  68.9 10.5 %collective-permute-done.1 = bf16[1,96,1152]{2,1,0:T(8,128)(2,1)S(1)} collective-permute-done((bf16[1,96,1152]{2,1,0:T(8,128)(2,1)S(1)}, bf16[1,96,1152]{2,1,0:T(8,128)(2,1)S(1)}, u32[]{:S(2)}, u32[]{:S(2)}) %collective-permute-start.1) | collective-permute-done | bytes 221216 | tf_op jit(solution)/shard_map/ppermute | solution.py:52
  107.3 14.6 %collective-permute-done.6.refs_5_ = bf16[2,96,1152]{2,1,0:T(8,128)(2,1)S(1)} collective-permute-done((bf16[2,96,1152]{2,1,0:T(8,128)(2,1)S(1)}, bf16[2,96,1152]{2,1,0:T(8,128)(2,1)S(1)}, u32[]{:S(2)}, u32[]{:S(2)}) %collective-permute-start.6) | collective-permute-done | bytes 442400 | tf_op jit(solution)/shard_map/ppermute | solution.py:52
  130.0 4.8 place_rows.2
  166.2 9.2 %collective-permute-start.21 = (bf16[256,1536]{1,0:T(8,128)(2,1)S(1)}, bf16[256,1536]{1,0:T(8,128)(2,1)S(1)}, u32[]{:S(2)}, u32[]{:S(2)}) collective-permute-start(bf16[256,1536]{1,0:T(8,128)(2,1)S(1)} %dynamic-slice_convert_fusion.2), channel_id=1, source_target_pairs={{0,1},{1,0},{2,3},{3,2},{4,5},{5,4},{6,7},{7,6},{8,9},{9,8},{10,11... | collective-permute-start | bytes 2359304 | tf_op jit(solution)/shard_map/ppermute | solution.py:56
  202.8 12.7 %collective-permute-done.23 = bf16[256,1536]{1,0:T(8,128)(2,1)} collective-permute-done((bf16[256,1536]{1,0:T(8,128)(2,1)}, bf16[256,1536]{1,0:T(8,128)(2,1)}, u32[]{:S(2)}, u32[]{:S(2)}) %collective-permute-start.23) | collective-permute-done | bytes 786464 | tf_op jit(solution)/shard_map/ppermute | solution.py:52
  215.9 15.9 %collective-permute-done.25 = bf16[256,1536]{1,0:T(8,128)(2,1)} collective-permute-done((bf16[256,1536]{1,0:T(8,128)(2,1)}, bf16[256,1536]{1,0:T(8,128)(2,1)}, u32[]{:S(2)}, u32[]{:S(2)}) %collective-permute-start.25) | collective-permute-done | bytes 786464 | tf_op jit(solution)/shard_map/ppermute | solution.py:52
  239.5 8.7 %collective-permute-done.27 = bf16[256,1536]{1,0:T(8,128)(2,1)S(1)} collective-permute-done((bf16[256,1536]{1,0:T(8,128)(2,1)}, bf16[256,1536]{1,0:T(8,128)(2,1)S(1)}, u32[]{:S(2)}, u32[]{:S(2)}) %collective-permute-start.27) | collective-permute-done | bytes 786464 | tf_op jit(solution)/shard_map/ppermute | solution.py:52
  249.4 19.8 %collective-permute-done.26 = bf16[256,1536]{1,0:T(8,128)(2,1)S(1)} collective-permute-done((bf16[256,1536]{1,0:T(8,128)(2,1)}, bf16[256,1536]{1,0:T(8,128)(2,1)S(1)}, u32[]{:S(2)}, u32[]{:S(2)}) %collective-permute-start.26) | collective-permute-done | bytes 786464 | tf_op jit(solution)/shard_map/ppermute | solution.py:52
  284.3 45.8 %experts.1 = (bf16[8,256,1536]{2,1,0:T(8,128)(2,1)}, bf16[8,256,1664]{2,1,0:T(8,128)(2,1)}, bf16[8,256,384]{2,1,0:T(8,128)(2,1)}, bf16[8,256,384]{2,1,0:T(8,128)...) custom-call(s32[1]{0:T(128)} %bitcast.me_ref, ...), custom_call_target="tpu_custom_call" | custom-call | flops 28991029248 | bytes 50000000 | tf_op jit(solution)/shard_map/experts/pallas_call | solution.py:284
  333.2 8.3 %bitcast_convert_fusion = bf16[1536,768]{0,1:T(8,128)(2,1)S(1)} fusion(bf16[8,256,1536]{2,1,0:T(8,128)(2,1)} %fusion.61.x_ref, bf16[8,256,768]{2,1,0:T(8,128)(2,1)S(1)} %copy-done.93), kind=kOutput, calls=%fused_computation.14 | convolution fusion | flops 4833017856 | bytes 11796480 | tf_op jit(solution)/shard_map/td,th->dh/dot_general | solution.py:452
  345.2 5.6 fusion.18
  350.8 6.5 bitcast_convert_fusion.1
  372.3 12.4 %collective-permute-done.56 = bf16[256,1664]{1,0:T(8,128)(2,1)S(1)} collective-permute-done((bf16[256,1664]{1,0:T(8,128)(2,1)S(1)}, bf16[256,1664]{1,0:T(8,128)(2,1)S(1)}, u32[]{:S(2)}, u32[]{:S(2)}) %collective-permute-start.56) | collective-permute-done | bytes 852000 | tf_op jit(solution)/shard_map/ppermute | solution.py:52
  384.7 5.1 collective-permute-done.53
  392.6 18.2 %collective-permute-done.54 = bf16[256,1664]{1,0:T(8,128)(2,1)S(1)} collective-permute-done((bf16[256,1664]{1,0:T(8,128)(2,1)S(1)}, bf16[256,1664]{1,0:T(8,128)(2,1)S(1)}, u32[]{:S(2)}, u32[]{:S(2)}) %collective-permute-start.54) | collective-permute-done | bytes 852000 | tf_op jit(solution)/shard_map/ppermute | solution.py:52
  419.7 7.9 %collective-permute-done.47 = bf16[256,1536]{1,0:T(8,128)(2,1)S(1)} collective-permute-done((bf16[256,1536]{1,0:T(8,128)(2,1)S(1)}, bf16[256,1536]{1,0:T(8,128)(2,1)S(1)}, u32[]{:S(2)}, u32[]{:S(2)}) %collective-permute-start.47) | collective-permute-done | bytes 786464 | tf_op jit(solution)/shard_map/ppermute | solution.py:52
  453.2 4.9 convolution_convert_fusion.3
  460.4 5.1 fusion
  485.6 6.3 fusion.8
  530.5 35.9 %collective-permute-done.65 = bf16[2,96,1152]{2,1,0:T(8,128)(2,1)S(1)} collective-permute-done((bf16[2,96,1152]{2,1,0:T(8,128)(2,1)S(1)}, bf16[2,96,1152]{2,1,0:T(8,128)(2,1)S(1)}, u32[]{:S(2)}, u32[]{:S(2)}) %collective-permute-start.65) | collective-permute-done | bytes 442400 | tf_op jit(solution)/shard_map/ppermute | solution.py:52
  571.8 5.3 collective-permute-done.77
  577.2 19.1 %collective-permute-done.86 = bf16[768,1152]{0,1:T(8,128)(2,1)S(1)} collective-permute-done((bf16[768,1152]{0,1:T(8,128)(2,1)S(1)}, bf16[768,1152]{0,1:T(8,128)(2,1)S(1)}, u32[]{:S(2)}, u32[]{:S(2)}) %collective-permute-start.86) | collective-permute-done | bytes 1769504 | tf_op jit(solution)/shard_map/ppermute | solution.py:52
  599.1 4.5 all-to-all-start.1
  603.8 17.8 %collective-permute-done.83 = bf16[2,96,896]{2,1,0:T(8,128)(2,1)} collective-permute-done((bf16[2,96,896]{2,1,0:T(8,128)(2,1)}, bf16[2,96,896]{2,1,0:T(8,128)(2,1)}, u32[]{:S(2)}, u32[]{:S(2)}) %collective-permute-start.83) | collective-permute-done | bytes 344096 | tf_op jit(solution)/shard_map/ppermute | solution.py:52
  624.7 5.6 fusion.34
  630.3 5.7 collective-permute-done.84
  640.1 13.7 %collective-permute-done.72 = bf16[2,96,1152]{2,1,0:T(8,128)(2,1)} collective-permute-done((bf16[2,96,1152]{2,1,0:T(8,128)(2,1)}, bf16[2,96,1152]{2,1,0:T(8,128)(2,1)}, u32[]{:S(2)}, u32[]{:S(2)}) %collective-permute-start.72) | collective-permute-done | bytes 442400 | tf_op jit(solution)/shard_map/ppermute | solution.py:52
  656.3 11.2 %collective-permute-done.73 = bf16[1,96,1152]{2,1,0:T(8,128)(2,1)S(1)} collective-permute-done((bf16[1,96,1152]{2,1,0:T(8,128)(2,1)S(1)}, bf16[1,96,1152]{2,1,0:T(8,128)(2,1)S(1)}, u32[]{:S(2)}, u32[]{:S(2)}) %collective-permute-start.73) | collective-permute-done | bytes 221216 | tf_op jit(solution)/shard_map/ppermute | solution.py:52
  (532 shorter events, 287.1 us)
Async XLA Ops:
  0.7 80.0 %collective-permute-start = (bf16[256,1536]{1,0:T(8,128)(2,1)}, bf16[256,1536]{1,0:T(8,128)(2,1)}, u32[]{:S(2)}, u32[]{:S(2)}) collective-permute-start(bf16[256,1536]{1,0:T(8,128)(2,1)} %param.15), channel_id=1, source_target_pairs={{0,1},{1,0},{2,3},{3,2},{4,5},{5,4},{6,7},{7,6},{8,9},{9,8},{10,11... | collective-permute-start | bytes 2359304 | tf_op jit(solution)/shard_map/ppermute | solution.py:56
  14.4 85.5 %collective-permute-start.31 = (bf16[256,1664]{1,0:T(8,128)(2,1)}, bf16[256,1664]{1,0:T(8,128)(2,1)}, u32[]{:S(2)}, u32[]{:S(2)}) collective-permute-start(bf16[256,1664]{1,0:T(8,128)(2,1)} %fusion.57), channel_id=1, source_target_pairs={{0,2},{2,0},{4,6},{6,4},{8,10},{10,8},{12,14},{14,12},{16,18},{18,... | collective-permute-start | bytes 2555912 | tf_op jit(solution)/shard_map/ppermute | solution.py:52
  16.1 182.0 %all-to-all-start = ((bf16[8,96,1152]{2,1,0:T(8,128)(2,1)}), bf16[8,96,1152]{2,1,0:T(8,128)(2,1)}, u32[]{:S(2)}, u32[]{:S(2)}) async-start(bf16[8,96,1152]{2,1,0:T(8,128)(2,1)} %pad_maximum_fusion.3), calls=%async_computation | async-start | bytes 3538944 | tf_op jit(solution)/shard_map/all_to_all | solution.py:344
  25.9 34.2 %collective-permute-start.12 = (bf16[2,96,768]{2,1,0:T(8,128)(2,1)S(1)}, bf16[2,96,768]{2,1,0:T(8,128)(2,1)S(1)}, u32[]{:S(2)}, u32[]{:S(2)}) collective-permute-start(bf16[2,96,768]{2,1,0:T(8,128)(2,1)S(1)} %pad_maximum_fusion.20.refs_0_), channel_id=1, source_target_pairs={{0,2},{2,0},{4,6},{6,4},{8,10},{10,8},{12,14},{14,12},{16,18},{18,... | collective-permute-start | bytes 884744 | tf_op jit(solution)/shard_map/ppermute | solution.py:52
  26.2 35.2 %collective-permute-start.13 = (bf16[2,96,768]{2,1,0:T(8,128)(2,1)S(1)}, bf16[2,96,768]{2,1,0:T(8,128)(2,1)S(1)}, u32[]{:S(2)}, u32[]{:S(2)}) collective-permute-start(bf16[2,96,768]{2,1,0:T(8,128)(2,1)S(1)} %pad_maximum_fusion.20.refs_0_), channel_id=1, source_target_pairs={{0,4},{2,6},{4,0},{6,2},{8,12},{10,14},{12,8},{14,10},{16,20},{18,... | collective-permute-start | bytes 884744 | tf_op jit(solution)/shard_map/ppermute | solution.py:52
  61.9 38.2 %collective-permute-start.32 = (bf16[256,1664]{1,0:T(8,128)(2,1)}, bf16[256,1664]{1,0:T(8,128)(2,1)}, u32[]{:S(2)}, u32[]{:S(2)}) collective-permute-start(bf16[256,1664]{1,0:T(8,128)(2,1)} %fusion.57), channel_id=1, source_target_pairs={{0,4},{2,6},{4,0},{6,2},{8,12},{10,14},{12,8},{14,10},{16,20},{18,... | collective-permute-start | bytes 2555912 | tf_op jit(solution)/shard_map/ppermute | solution.py:52
  96.1 29.1 %collective-permute-start.34 = (bf16[256,1664]{1,0:T(8,128)(2,1)}, bf16[256,1664]{1,0:T(8,128)(2,1)}, u32[]{:S(2)}, u32[]{:S(2)}) collective-permute-start(bf16[256,1664]{1,0:T(8,128)(2,1)} %fusion.57), channel_id=1, source_target_pairs={{0,8},{2,10},{4,12},{6,14},{8,0},{10,2},{12,4},{14,6},{16,24},{18,... | collective-permute-start | bytes 2555912 | tf_op jit(solution)/shard_map/ppermute | solution.py:52
  100.1 80.9 %collective-permute-start.33 = (bf16[256,1664]{1,0:T(8,128)(2,1)}, bf16[256,1664]{1,0:T(8,128)(2,1)}, u32[]{:S(2)}, u32[]{:S(2)}) collective-permute-start(bf16[256,1664]{1,0:T(8,128)(2,1)} %collective-permute-done.32), channel_id=1, source_target_pairs={{0,2},{2,0},{4,6},{6,4},{8,10},{10,8},{12,14},{14,12},{16,18},{18,... | collective-permute-start | bytes 2555912 | tf_op jit(solution)/shard_map/ppermute | solution.py:52
  125.2 53.3 %collective-permute-start.35 = (bf16[256,1664]{1,0:T(8,128)(2,1)}, bf16[256,1664]{1,0:T(8,128)(2,1)}, u32[]{:S(2)}, u32[]{:S(2)}) collective-permute-start(bf16[256,1664]{1,0:T(8,128)(2,1)} %collective-permute-done.31), channel_id=1, source_target_pairs={{0,8},{2,10},{4,12},{6,14},{8,0},{10,2},{12,4},{14,6},{16,24},{18,... | collective-permute-start | bytes 2555912 | tf_op jit(solution)/shard_map/ppermute | solution.py:52
  126.7 49.6 %collective-permute-start.36 = (bf16[256,1664]{1,0:T(8,128)(2,1)}, bf16[256,1664]{1,0:T(8,128)(2,1)}, u32[]{:S(2)}, u32[]{:S(2)}) collective-permute-start(bf16[256,1664]{1,0:T(8,128)(2,1)} %collective-permute-done.34), channel_id=1, source_target_pairs={{0,4},{2,6},{4,0},{6,2},{8,12},{10,14},{12,8},{14,10},{16,20},{18,... | collective-permute-start | bytes 2555912 | tf_op jit(solution)/shard_map/ppermute | solution.py:52
  166.2 26.0 %collective-permute-start.21 = (bf16[256,1536]{1,0:T(8,128)(2,1)S(1)}, bf16[256,1536]{1,0:T(8,128)(2,1)S(1)}, u32[]{:S(2)}, u32[]{:S(2)}) collective-permute-start(bf16[256,1536]{1,0:T(8,128)(2,1)S(1)} %dynamic-slice_convert_fusion.2), channel_id=1, source_target_pairs={{0,1},{1,0},{2,3},{3,2},{4,5},{5,4},{6,7},{7,6},{8,9},{9,8},{10,11... | collective-permute-start | bytes 2359304 | tf_op jit(solution)/shard_map/ppermute | solution.py:56
  198.0 33.7 %collective-permute-start.25 = (bf16[256,1536]{1,0:T(8,128)(2,1)}, bf16[256,1536]{1,0:T(8,128)(2,1)}, u32[]{:S(2)}, u32[]{:S(2)}) collective-permute-start(bf16[256,1536]{1,0:T(8,128)(2,1)} %get-tuple-element.93), channel_id=1, source_target_pairs={{0,8},{2,10},{4,12},{6,14},{8,0},{10,2},{12,4},{14,6},{16,24},{18,... | collective-permute-start | bytes 2359304 | tf_op jit(solution)/shard_map/ppermute | solution.py:52
  198.1 78.2 %collective-permute-start.41 = (bf16[1,768,1152]{2,1,0:T(8,128)(2,1)}, bf16[1,768,1152]{2,1,0:T(8,128)(2,1)S(1)}, u32[]{:S(2)}, u32[]{:S(2)}) collective-permute-start(bf16[1,768,1152]{2,1,0:T(8,128)(2,1)} %bitcast.36.refs_0_), channel_id=1, source_target_pairs={{0,16},{2,18},{4,20},{6,22},{8,24},{10,26},{12,28},{14,30},{16,0},... | collective-permute-start | bytes 5308424 | tf_op jit(solution)/shard_map/ppermute | solution.py:52
  215.5 54.9 %collective-permute-start.24 = (bf16[256,1536]{1,0:T(8,128)(2,1)}, bf16[256,1536]{1,0:T(8,128)(2,1)S(1)}, u32[]{:S(2)}, u32[]{:S(2)}) collective-permute-start(bf16[256,1536]{1,0:T(8,128)(2,1)} %collective-permute-done.23), channel_id=1, source_target_pairs={{0,2},{2,0},{4,6},{6,4},{8,10},{10,8},{12,14},{14,12},{16,18},{18,... | collective-permute-start | bytes 2359304 | tf_op jit(solution)/shard_map/ppermute | solution.py:52
  215.7 53.5 %collective-permute-start.26 = (bf16[256,1536]{1,0:T(8,128)(2,1)}, bf16[256,1536]{1,0:T(8,128)(2,1)S(1)}, u32[]{:S(2)}, u32[]{:S(2)}) collective-permute-start(bf16[256,1536]{1,0:T(8,128)(2,1)} %collective-permute-done.22), channel_id=1, source_target_pairs={{0,8},{2,10},{4,12},{6,14},{8,0},{10,2},{12,4},{14,6},{16,24},{18,... | collective-permute-start | bytes 2359304 | tf_op jit(solution)/shard_map/ppermute | solution.py:52
  236.4 47.8 %collective-permute-start.40 = (bf16[1,768,1152]{2,1,0:T(8,128)(2,1)}, bf16[1,768,1152]{2,1,0:T(8,128)(2,1)}, u32[]{:S(2)}, u32[]{:S(2)}) collective-permute-start(bf16[1,768,1152]{2,1,0:T(8,128)(2,1)} %bitcast.36.refs_0_), channel_id=1, source_target_pairs={{0,1},{1,0},{2,3},{3,2},{4,5},{5,4},{6,7},{7,6},{8,9},{9,8},{10,11... | collective-permute-start | bytes 5308424 | tf_op jit(solution)/shard_map/ppermute | solution.py:56
  248.2 35.1 %collective-permute-start.28 = (bf16[96,1536]{1,0:T(8,128)(2,1)S(1)}, bf16[96,1536]{1,0:T(8,128)(2,1)S(1)}, u32[]{:S(2)}, u32[]{:S(2)}) collective-permute-start(bf16[96,1536]{1,0:T(8,128)(2,1)S(1)} %slice.602), channel_id=1, source_target_pairs={{0,2},{2,0},{4,6},{6,4},{8,10},{10,8},{12,14},{14,12},{16,18},{18,... | collective-permute-start | bytes 884744 | tf_op jit(solution)/shard_map/ppermute | solution.py:52
  370.4 144.1 %collective-permute-start.85 = (bf16[1536,1152]{0,1:T(8,128)(2,1)}, bf16[1536,1152]{0,1:T(8,128)(2,1)}, u32[]{:S(2)}, u32[]{:S(2)}) collective-permute-start(bf16[1536,1152]{0,1:T(8,128)(2,1)} %pad_maximum_fusion.1), channel_id=1, source_target_pairs={{0,1},{1,0},{2,3},{3,2},{4,5},{5,4},{6,7},{7,6},{8,9},{9,8},{10,11... | collective-permute-start | bytes 10616840 | tf_op jit(solution)/shard_map/ppermute | solution.py:56
  391.0 36.7 %collective-permute-start.47 = (bf16[256,1536]{1,0:T(8,128)(2,1)S(1)}, bf16[256,1536]{1,0:T(8,128)(2,1)S(1)}, u32[]{:S(2)}, u32[]{:S(2)}) collective-permute-start(bf16[256,1536]{1,0:T(8,128)(2,1)S(1)} %pad_maximum_fusion.10), channel_id=1, source_target_pairs={{0,2},{2,0},{4,6},{6,4},{8,10},{10,8},{12,14},{14,12},{16,18},{18,... | collective-permute-start | bytes 2359304 | tf_op jit(solution)/shard_map/ppermute | solution.py:52
  474.4 31.8 %collective-permute-start.75 = (bf16[2,32,896]{2,1,0:T(8,128)(2,1)}, bf16[2,32,896]{2,1,0:T(8,128)(2,1)}, u32[]{:S(2)}, u32[]{:S(2)}) collective-permute-start(bf16[2,32,896]{2,1,0:T(8,128)(2,1)} %get-tuple-element.146), channel_id=1, source_target_pairs={{0,4},{2,6},{4,0},{6,2},{8,12},{10,14},{12,8},{14,10},{16,20},{18,... | collective-permute-start | bytes 344072 | tf_op jit(solution)/shard_map/ppermute | solution.py:52
  474.8 32.5 %collective-permute-start.78 = (bf16[2,32,896]{2,1,0:T(8,128)(2,1)}, bf16[2,32,896]{2,1,0:T(8,128)(2,1)}, u32[]{:S(2)}, u32[]{:S(2)}) collective-permute-start(bf16[2,32,896]{2,1,0:T(8,128)(2,1)} %get-tuple-element.144), channel_id=1, source_target_pairs={{0,8},{2,10},{4,12},{6,14},{8,0},{10,2},{12,4},{14,6},{16,24},{18,... | collective-permute-start | bytes 344072 | tf_op jit(solution)/shard_map/ppermute | solution.py:52
  475.0 33.7 %collective-permute-start.81 = (bf16[2,32,896]{2,1,0:T(8,128)(2,1)}, bf16[2,32,896]{2,1,0:T(8,128)(2,1)}, u32[]{:S(2)}, u32[]{:S(2)}) collective-permute-start(bf16[2,32,896]{2,1,0:T(8,128)(2,1)} %get-tuple-element.143), channel_id=1, source_target_pairs={{0,2},{2,0},{4,6},{6,4},{8,10},{10,8},{12,14},{14,12},{16,18},{18,... | collective-permute-start | bytes 344072 | tf_op jit(solution)/shard_map/ppermute | solution.py:52
  517.8 78.4 %collective-permute-start.86 = (bf16[768,1152]{0,1:T(8,128)(2,1)S(1)}, bf16[768,1152]{0,1:T(8,128)(2,1)S(1)}, u32[]{:S(2)}, u32[]{:S(2)}) collective-permute-start(bf16[768,1152]{0,1:T(8,128)(2,1)S(1)} %dynamic-slice_convert_fusion), channel_id=1, source_target_pairs={{0,16},{2,18},{4,20},{6,22},{8,24},{10,26},{12,28},{14,30},{16,0},... | collective-permute-start | bytes 5308424 | tf_op jit(solution)/shard_map/ppermute | solution.py:52
  519.7 46.8 %collective-permute-start.65 = (bf16[2,96,1152]{2,1,0:T(8,128)(2,1)S(1)}, bf16[2,96,1152]{2,1,0:T(8,128)(2,1)S(1)}, u32[]{:S(2)}, u32[]{:S(2)}) collective-permute-start(bf16[2,96,1152]{2,1,0:T(8,128)(2,1)S(1)} %pad_maximum_fusion.14), channel_id=1, source_target_pairs={{0,8},{2,10},{4,12},{6,14},{8,0},{10,2},{12,4},{14,6},{16,24},{18,... | collective-permute-start | bytes 1327112 | tf_op jit(solution)/shard_map/ppermute | solution.py:52
  520.6 49.2 %collective-permute-start.62 = (bf16[256,1536]{1,0:T(8,128)(2,1)S(1)}, bf16[256,1536]{1,0:T(8,128)(2,1)S(1)}, u32[]{:S(2)}, u32[]{:S(2)}) collective-permute-start(bf16[256,1536]{1,0:T(8,128)(2,1)S(1)} %dynamic-slice_convert_fusion.1), channel_id=1, source_target_pairs={{0,1},{1,0},{2,3},{3,2},{4,5},{5,4},{6,7},{7,6},{8,9},{9,8},{10,11... | collective-permute-start | bytes 2359304 | tf_op jit(solution)/shard_map/ppermute | solution.py:56
  528.9 94.2 %collective-permute-start.45 = (bf16[256,1536]{1,0:T(8,128)(2,1)}, bf16[256,1536]{1,0:T(8,128)(2,1)}, u32[]{:S(2)}, u32[]{:S(2)}) collective-permute-start(bf16[256,1536]{1,0:T(8,128)(2,1)} %get-tuple-element.110), channel_id=1, source_target_pairs={{0,2},{2,0},{4,6},{6,4},{8,10},{10,8},{12,14},{14,12},{16,18},{18,... | collective-permute-start | bytes 2359304 | tf_op jit(solution)/shard_map/ppermute | solution.py:52
  530.4 92.8 %collective-permute-start.48 = (bf16[256,1536]{1,0:T(8,128)(2,1)}, bf16[256,1536]{1,0:T(8,128)(2,1)}, u32[]{:S(2)}, u32[]{:S(2)}) collective-permute-start(bf16[256,1536]{1,0:T(8,128)(2,1)} %get-tuple-element.112), channel_id=1, source_target_pairs={{0,4},{2,6},{4,0},{6,2},{8,12},{10,14},{12,8},{14,10},{16,20},{18,... | collective-permute-start | bytes 2359304 | tf_op jit(solution)/shard_map/ppermute | solution.py:52
  566.4 58.2 %collective-permute-start.51 = (bf16[256,1536]{1,0:T(8,128)(2,1)}, bf16[256,1536]{1,0:T(8,128)(2,1)}, u32[]{:S(2)}, u32[]{:S(2)}) collective-permute-start(bf16[256,1536]{1,0:T(8,128)(2,1)} %get-tuple-element.111), channel_id=1, source_target_pairs={{0,8},{2,10},{4,12},{6,14},{8,0},{10,2},{12,4},{14,6},{16,24},{18,... | collective-permute-start | bytes 2359304 | tf_op jit(solution)/shard_map/ppermute | solution.py:52
  577.2 26.5 %collective-permute-start.80 = (bf16[2,96,896]{2,1,0:T(8,128)(2,1)}, bf16[2,96,896]{2,1,0:T(8,128)(2,1)}, u32[]{:S(2)}, u32[]{:S(2)}) collective-permute-start(bf16[2,96,896]{2,1,0:T(8,128)(2,1)} %get-tuple-element.141), channel_id=1, source_target_pairs={{0,4},{2,6},{4,0},{6,2},{8,12},{10,14},{12,8},{14,10},{16,20},{18,... | collective-permute-start | bytes 1032200 | tf_op jit(solution)/shard_map/ppermute | solution.py:52
  599.1 70.4 %all-to-all-start.1 = ((bf16[8,96,1152]{2,1,0:T(8,128)(2,1)}), bf16[8,96,1152]{2,1,0:T(8,128)(2,1)S(1)}, u32[]{:S(2)}, u32[]{:S(2)}) async-start(bf16[8,96,1152]{2,1,0:T(8,128)(2,1)} %bitcast.269), calls=%async_computation.1 | async-start | bytes 3538944 | tf_op jit(solution)/shard_map/all_to_all | solution.py:468
  603.7 33.7 %collective-permute-start.66 = (bf16[2,96,1152]{2,1,0:T(8,128)(2,1)}, bf16[2,96,1152]{2,1,0:T(8,128)(2,1)}, u32[]{:S(2)}, u32[]{:S(2)}) collective-permute-start(bf16[2,96,1152]{2,1,0:T(8,128)(2,1)} %get-tuple-element.126), channel_id=1, source_target_pairs={{0,2},{2,0},{4,6},{6,4},{8,10},{10,8},{12,14},{14,12},{16,18},{18,... | collective-permute-start | bytes 1327112 | tf_op jit(solution)/shard_map/ppermute | solution.py:52
  623.1 30.7 %collective-permute-start.72 = (bf16[2,96,1152]{2,1,0:T(8,128)(2,1)}, bf16[2,96,1152]{2,1,0:T(8,128)(2,1)}, u32[]{:S(2)}, u32[]{:S(2)}) collective-permute-start(bf16[2,96,1152]{2,1,0:T(8,128)(2,1)} %get-tuple-element.127), channel_id=1, source_target_pairs={{0,8},{2,10},{4,12},{6,14},{8,0},{10,2},{12,4},{14,6},{16,24},{18,... | collective-permute-start | bytes 1327112 | tf_op jit(solution)/shard_map/ppermute | solution.py:52
  (161 other events, 1927.1 us)

commit v2 on v0

v2 whole, which is shorter than its diff:
```python
import functools
import math

import jax
import jax.numpy as jnp
from jax import lax
from jax.experimental import pallas as pl
from jax.experimental.pallas import tpu as pltpu
from jax.sharding import PartitionSpec as P

HD = 128
EXTRA = 128
GAIN_A, GAIN_F = 8, 9
CUBE = 8
BRIEF = pl.CostEstimate(flops=0, bytes_accessed=3_000_000, transcendentals=0)
epsilon = 1e-06
highest = lax.Precision.HIGHEST
f32 = jnp.float32
bf16 = jnp.bfloat16
NN = (((1,), (0,)), ((), ()))
NT = (((1,), (1,)), ((), ()))
TN = (((0,), (0,)), ((), ()))


def rms_parts(values):
    inverse_root = lax.rsqrt(jnp.mean(values * values, axis=-1, keepdims=True) + epsilon)
    return (values * inverse_root, inverse_root)


def norm_backward(grad_normed, scaled, inverse_root, gain):
    grad_scaled = grad_normed * gain
    inner = jnp.mean(grad_scaled * scaled, axis=-1, keepdims=True)
    return inverse_root * (grad_scaled - scaled * inner)


def rope_tables(length, size):
    inverse = 10000.0 ** (-jnp.arange(size // 2, dtype=f32) / (size // 2))
    angle = jnp.arange(length, dtype=f32)[:, None] * inverse[None, :]
    return (jnp.cos(angle), jnp.sin(angle))


def swap(values, bit, count):
    return lax.ppermute(values, "dp", [(i, i ^ bit) for i in range(count)])


def swap_core(values):
    return lax.ppermute(values, "tensor", [(0, 1), (1, 0)])


def gate(values, *events):
    values = list(values)
    flat = jax.tree.leaves(events)
    return pl.pallas_call(
        lambda *refs: None,
        out_shape=[jax.ShapeDtypeStruct(v.shape, v.dtype) for v in values],
        in_specs=[pl.BlockSpec(memory_space=pl.ANY)] * (len(values) + len(flat)),
        out_specs=[pl.BlockSpec(memory_space=pl.ANY)] * len(values),
        input_output_aliases={i: i for i in range(len(values))},
        compiler_params=pltpu.CompilerParams(vmem_limit_bytes=60 * 1024 * 1024),
        cost_estimate=BRIEF,
        name="gate",
    )(*values, *flat)


def gate_dict(got, keys, *events):
    return got | dict(zip(keys, gate([got[k] for k in keys], *events)))


def halves(rows):
    part = rows // 2
    return ((0, part), (part, rows))


def cut(values, span, axis):
    return lax.slice_in_dim(values, span[0], span[1], axis=axis)


NEAR, FAR, LAST = (1, 2, 4), (3, 6, 5), (7, 8)


def add_round(left, right):
    return (left.astype(f32) + right.astype(f32)).astype(bf16)


def sum_last(parts, count):
    return {7: swap(parts[7], 1, count), 8: swap(parts[8], 2, count)}


def patch_kernel(first, second, low, high, first_out, second_out):
    first_out[...] = (first[...].astype(f32) + low[...].astype(f32)).astype(bf16)
    second_out[...] = (second[...].astype(f32) + high[...].astype(f32)).astype(bf16)


def patch(first, second, low, high):
    shape = first.shape
    half = low.shape
    if half[-2] % 16:
        return (
            jnp.concatenate([add_round(first[..., : half[-2], :], low), first[..., half[-2] :, :]], -2),
            jnp.concatenate([second[..., : half[-2], :], add_round(second[..., half[-2] :, :], high)], -2),
        )
    lead = (0,) * (len(shape) - 2)
    top = pl.BlockSpec(half, lambda i: lead + (0, 0))
    bottom = pl.BlockSpec(half, lambda i: lead + (1, 0))
    return pl.pallas_call(
        patch_kernel,
        grid=(1,),
        out_shape=[jax.ShapeDtypeStruct(shape, bf16)] * 2,
        in_specs=[top, bottom, top, top],
        out_specs=[top, bottom],
        input_output_aliases={0: 0, 1: 1},
        compiler_params=pltpu.CompilerParams(vmem_limit_bytes=60 * 1024 * 1024),
        cost_estimate=BRIEF,
        name="patch",
    )(first, second, low, high)


def far_terms(parts, got):
    return patch(parts[6], parts[5], got[7], got[8])


def sum_far(parts, terms, count):
    first, second = terms
    return {4: swap(first, 2, count), 1: swap(second, 4, count), 2: swap(parts[3], 1, count)}


def terms_kernel(*refs):
    for k in range(3):
        refs[6 + k][...] = (refs[k][...].astype(f32) + refs[3 + k][...].astype(f32)).astype(bf16)


def near_terms(parts, got):
    args = [parts[bit] for bit in NEAR] + [got[bit] for bit in NEAR]
    shape = parts[1].shape
    grid = 4 if shape[-2] % 64 == 0 else 1
    block = shape[:-2] + (shape[-2] // grid, shape[-1])
    lead = (0,) * (len(shape) - 2)
    spec = pl.BlockSpec(block, lambda i: lead + (i, 0))
    outs = pl.pallas_call(
        terms_kernel,
        grid=(grid,),
        out_shape=[jax.ShapeDtypeStruct(shape, bf16)] * 3,
        in_specs=[spec] * 6,
        out_specs=[spec] * 3,
        compiler_params=pltpu.CompilerParams(vmem_limit_bytes=60 * 1024 * 1024),
        cost_estimate=BRIEF,
        name="terms",
    )(*args)
    return dict(zip(NEAR, outs))


def sum_near(terms, count):
    return {bit: swap(terms[bit], bit, count) for bit in NEAR}


def sum_own(parts, got):
    return parts[0].astype(f32) + (
        got[1].astype(f32) + (got[2].astype(f32) + got[4].astype(f32))
    )


def outer_bits(count):
    bits, bit = [], CUBE
    while bit < count:
        bits.append(bit)
        bit *= 2
    return bits


def outer_gather(own, count):
    pieces = [own[None]]
    for bit in outer_bits(count):
        pieces.append(swap(jnp.concatenate(pieces, axis=0), bit, count))
    return pieces


def outer_pair(shard, count):
    return jnp.concatenate(outer_gather(shard, count), axis=0)


def piece_copies(got, block, me, count):
    if block % 32:
        stacked = jnp.stack(
            [got[b] for b in range(7)] + [jnp.concatenate([got[b] for b in LAST], axis=1)],
            axis=1,
        )
        whole = stacked.reshape(count, block, -1)[jnp.arange(count) ^ me]
        return [whole.reshape(1, count * block, -1)], [(0, 0, 0, count * block, None, block)]
    sources, copies = [], []
    spans = [(0, block)] * 7 + list(halves(block))
    for b, span in enumerate(spans):
        for j in range(got[b].shape[0]):
            copies.append((b, j, span[0], span[1] - span[0], 8 * j + min(b, 7), block))
        sources.append(got[b])
    return sources, copies


def lay_rows(copies, sources, targets, sems, me):
    started = []
    for number, (source, entry, start, rows, offset, block) in enumerate(copies):
        row = 0 if offset is None else pl.multiple_of((me ^ offset) * block + start, 16)
        column = 0
        for k, target in enumerate(targets):
            cols = target.shape[1]
            copy = pltpu.make_async_copy(
                sources[source].at[entry, :, pl.ds(column, cols)],
                target.at[pl.ds(row, rows)],
                sems.at[len(targets) * number + k],
            )
            copy.start()
            started.append(copy)
            column += cols
    for copy in started:
        copy.wait()


def part_order(block):
    return [(b, (0, block)) for b in range(7)] + [(7, span) for span in halves(block)]


def part_shapes(count, block, width):
    if block % 32:
        return [jax.ShapeDtypeStruct((count * block, width), bf16)]
    return [
        jax.ShapeDtypeStruct((count // CUBE, span[1] - span[0], width), bf16)
        for _, span in part_order(block)
    ]


def store_parts(whole, parts, me, block, at):
    cols = pl.ds(at, whole.shape[1])
    if len(parts) == 1:
        parts[0][:, cols] = whole[...].astype(bf16)
        return
    for part, (offset, span) in zip(parts, part_order(block)):
        for j in range(part.shape[0]):
            row = pl.multiple_of((me ^ (8 * j + offset)) * block + span[0], 16)
            part[j, :, cols] = whole[pl.ds(row, span[1] - span[0])].astype(bf16)


def spread_parts(parts, me, count):
    if len(parts) > 1:
        return dict(enumerate(parts))
    block = parts[0].shape[0] // count
    outer = jnp.arange(count // CUBE) * CUBE
    blocks = parts[0].reshape(count, block, -1)
    return {
        k: cut(blocks[(offset + outer) ^ me], span, 1)
        for k, (offset, span) in enumerate(part_order(block))
    }


def outer_sum(total, count):
    for bit in reversed(outer_bits(count)):
        half = total.shape[0] // 2
        total = total[:half] + swap(total[half:].astype(bf16), bit, count).astype(f32)
    return total[0]


def vmem_call(kernel, out_shapes, scratch, args, name, smem=(), flops=0):
    spaces = {0: pltpu.VMEM, 1: pltpu.SMEM, 2: pl.ANY}
    moved = sum(math.prod(o.shape) * o.dtype.itemsize for o in out_shapes)
    moved += sum(math.prod(a.shape) * a.dtype.itemsize for a, _ in args)
    return pl.pallas_call(
        kernel,
        out_shape=out_shapes,
        in_specs=[pl.BlockSpec(memory_space=spaces[space]) for _, space in args],
        out_specs=[pl.BlockSpec(memory_space=pltpu.VMEM)] * len(out_shapes),
        scratch_shapes=scratch,
        compiler_params=pltpu.CompilerParams(vmem_limit_bytes=60 * 1024 * 1024),
        cost_estimate=BRIEF,
        name=name,
    )(*[a for a, _ in args])


def turn(values, cosine, sine):
    return values * cosine + pltpu.roll(values, values.shape[1] // 2, 1) * sine


def masks(seg_col, seg_row, splits):
    out = []
    for low, high in splits:
        shape = (high - low, high)
        query_at = lax.broadcasted_iota(jnp.int32, shape, 0) + low
        key_at = lax.broadcasted_iota(jnp.int32, shape, 1)
        allowed = (seg_col[low:high] == seg_row[:, :high]) & (key_at <= query_at)
        out.append(jnp.where(allowed, 0.0, -1e30))
    return out


def row_splits(length):
    return [(at, at + length // 2) for at in (0, length // 2)]


def attend_kernel(
    copies, sizes, at_ref, own_ref, other_ref, seg_col, seg_row, cos_ref, sin_ref, *refs
):
    heads, kv_heads, sources = sizes
    pieces = refs[:sources]
    hid, normed, qs, ks, vs, mixed, lse, weights, small, out_weights, gains = refs[sources:-3]
    own, other, sems = refs[-3:]
    me, core = at_ref[0], at_ref[1]
    rows = own_ref.shape[0]
    length = 2 * rows
    hid[pl.ds(pl.multiple_of(core * rows, rows), rows)] = own_ref[...]
    hid[pl.ds(pl.multiple_of((1 - core) * rows, rows), rows)] = other_ref[...]
    lay_rows(copies, pieces, (weights, small, out_weights), sems, me)
    gains[...] = jnp.transpose(small[...].astype(f32))[: gains.shape[0]]
    value = hid[...].astype(f32)
    root = lax.rsqrt(jnp.mean(value * value, axis=1, keepdims=True) + epsilon)
    normed[...] = (value * root * gains[GAIN_A : GAIN_A + 1]).astype(bf16)
    qkv = lax.dot_general(normed[...], weights[...], NN, preferred_element_type=f32)
    cosine, sine = cos_ref[...], sin_ref[...]
    for head in range(heads):
        at = slice(head * HD, (head + 1) * HD)
        qs[:, at] = turn(qkv[:, at], cosine, sine).astype(bf16)
    for head in range(kv_heads):
        at = slice(head * HD, (head + 1) * HD)
        ks[:, at] = turn(qkv[:, heads * HD :][:, at], cosine, sine).astype(bf16)
    vs[...] = qkv[:, (heads + kv_heads) * HD :].astype(bf16)
    splits = row_splits(length)
    scale = 1.0 / math.sqrt(HD)
    for (low, high), mask in zip(splits, masks(seg_col[...], seg_row[...], splits)):
        for head in range(heads):
            at = slice(head * HD, (head + 1) * HD)
            kv = head // (heads // kv_heads)
            kv = slice(kv * HD, (kv + 1) * HD)
            scores = lax.dot_general(
                qs[low:high, at], ks[:high, kv], NT, preferred_element_type=f32
            )
            scores = scores * scale + mask
            peak = jnp.max(scores, axis=1, keepdims=True)
            expo = jnp.exp(scores - peak)
            total = jnp.sum(expo, axis=1, keepdims=True)
            lse[low:high, head : head + 1] = peak + jnp.log(total)
            probs = (expo * (1.0 / total)).astype(bf16)
            mixed[low:high, at] = lax.dot_general(
                probs, vs[:high, kv], NN, preferred_element_type=f32
            ).astype(bf16)
    for target, half in ((other, 1 - core), (own, core)):
        part = mixed[pl.ds(pl.multiple_of(half * rows, rows), rows)]
        target[...] = lax.dot_general(
            part, out_weights[...], NT, preferred_element_type=f32
        ).astype(target.dtype)


def middle_kernel(hidden, own, other, gains, middle, normed):
    value = hidden[...].astype(f32) + own[...] + other[...].astype(f32)
    middle[...] = value
    root = lax.rsqrt(jnp.mean(value * value, axis=1, keepdims=True) + epsilon)
    normed[...] = (value * root * gains[GAIN_F : GAIN_F + 1]).astype(bf16)


def middle_back_kernel(
    middle, normed, grad_out, code, router, gains, own, *refs
):
    others, (grad_middle, grad_round, small) = refs[:-3], refs[-3:]
    width = middle.shape[1]
    total = own[...].astype(f32)
    for other in others:
        total += other[...].astype(f32)
    routed = code[...].astype(f32) > 0.5
    logits = lax.dot_general(normed[...], router[...], NN, preferred_element_type=f32)
    logits = jnp.where(routed, logits, -1e30)
    expo = jnp.where(routed, jnp.exp(logits - jnp.max(logits, axis=1, keepdims=True)), 0.0)
    gates = expo / jnp.sum(expo, axis=1, keepdims=True)
    grad_gates = total[:, width:]
    grad_logits = gates * (grad_gates - jnp.sum(gates * grad_gates, axis=1, keepdims=True))
    high = grad_logits.astype(bf16)
    low = (grad_logits - high.astype(f32)).astype(bf16)
    grad_normed = total[:, :width]
    router_grad = jnp.zeros(small.shape, f32)
    for part in (high, low):
        grad_normed += lax.dot_general(part, router[...], NT, preferred_element_type=f32)
        router_grad += lax.dot_general(normed[...], part, TN, preferred_element_type=f32)
    value = middle[...]
    root = lax.rsqrt(jnp.mean(value * value, axis=1, keepdims=True) + epsilon)
    scaled = value * root
    column = jnp.sum(grad_normed * scaled, axis=0, keepdims=True)
    column = jnp.transpose(jnp.broadcast_to(column, (EXTRA, width)))
    lanes = lax.broadcasted_iota(jnp.int32, small.shape, 1)
    small[...] = jnp.where(lanes == GAIN_F, column, router_grad)
    grad_scaled = grad_normed * gains[GAIN_F : GAIN_F + 1]
    inner = jnp.mean(grad_scaled * scaled, axis=1, keepdims=True)
    result = grad_out[...].astype(f32) + root * (grad_scaled - scaled * inner)
    grad_middle[...] = result
    grad_round[...] = result.astype(bf16)


def attend_back_kernel(
    block,
    sizes,
    at_ref,
    own_ref,
    other_ref,
    mixed,
    out_weights,
    small_ref,
    qs,
    ks,
    vs,
    lse,
    seg_col,
    seg_row,
    cos_ref,
    sin_ref,
    hid,
    normed,
    weights,
    *refs,
):
    heads, kv_heads = sizes
    own, other, parts = refs[0], refs[1], refs[2:-6]
    acc, small, grads, whole, grad_mixed, out_acc = refs[-6:]
    me, core = at_ref[0], at_ref[1]
    length, width = hid.shape
    rows = own.shape[0]
    cols = grads.shape[1]
    whole[pl.ds(pl.multiple_of(core * rows, rows), rows)] = own_ref[...]
    whole[pl.ds(pl.multiple_of((1 - core) * rows, rows), rows)] = other_ref[...]
    grad_mixed[...] = lax.dot_general(
        whole[...], out_weights[...], NN, preferred_element_type=f32
    ).astype(bf16)
    out_acc[...] = lax.dot_general(whole[...], mixed[...], TN, preferred_element_type=f32)
    store_parts(out_acc, parts, me, block, cols + EXTRA)
    cosine, sine = cos_ref[...], -sin_ref[...]
    splits = row_splits(length)
    scale = 1.0 / math.sqrt(HD)
    per_group = heads // kv_heads
    bias = masks(seg_col[...], seg_row[...], splits)
    for kv_head in range(kv_heads):
        kv = slice(kv_head * HD, (kv_head + 1) * HD)
        grad_key = jnp.zeros((length, HD), f32)
        grad_value = jnp.zeros((length, HD), f32)
        for (low, high), mask in zip(splits, bias):
            key_sum = jnp.zeros((high, HD), f32)
            value_sum = jnp.zeros((high, HD), f32)
            for head in range(kv_head * per_group, (kv_head + 1) * per_group):
                at = slice(head * HD, (head + 1) * HD)
                query, grad = qs[low:high, at], grad_mixed[low:high, at]
                scores = lax.dot_general(query, ks[:high, kv], NT, preferred_element_type=f32)
                probs = jnp.exp(scores * scale + mask - lse[low:high, head : head + 1])
                grad_probs = lax.dot_general(
                    grad, vs[:high, kv], NT, preferred_element_type=f32
                )
                inner = jnp.sum(grad_probs * probs, axis=1, keepdims=True)
                grad_scores = (probs * (grad_probs - inner)).astype(bf16)
                grad_query = lax.dot_general(
                    grad_scores, ks[:high, kv], NN, preferred_element_type=f32
                )
                grads[low:high, at] = turn(
                    grad_query * scale, cosine[low:high], sine[low:high]
                ).astype(bf16)
                key_sum += lax.dot_general(grad_scores, query, TN, preferred_element_type=f32)
                value_sum += lax.dot_general(
                    probs.astype(bf16), grad, TN, preferred_element_type=f32
                )
            if high < length:
                pad = jnp.zeros((length - high, HD), f32)
                key_sum = jnp.concatenate([key_sum, pad], axis=0)
                value_sum = jnp.concatenate([value_sum, pad], axis=0)
            grad_key += key_sum
            grad_value += value_sum
        at = (heads + kv_head) * HD
        grads[:, at : at + HD] = turn(grad_key * scale, cosine, sine).astype(bf16)
        at += kv_heads * HD
        grads[:, at : at + HD] = grad_value.astype(bf16)
    acc[...] = lax.dot_general(normed[...], grads[...], TN, preferred_element_type=f32)
    store_parts(acc, parts, me, block, 0)
    value = hid[...].astype(f32)
    root = lax.rsqrt(jnp.mean(value * value, axis=1, keepdims=True) + epsilon)
    column = jnp.zeros((1, width), f32)
    for target, half in ((other, 1 - core), (own, core)):
        at = pl.ds(pl.multiple_of(half * rows, rows), rows)
        part = lax.dot_general(grads[at], weights[...], NT, preferred_element_type=f32)
        target[...] = part.astype(target.dtype)
        half_value = hid[at].astype(f32)
        half_root = lax.rsqrt(jnp.mean(half_value * half_value, axis=1, keepdims=True) + epsilon)
        column += jnp.sum(part * (half_value * half_root), axis=0, keepdims=True)
    lanes = lax.broadcasted_iota(jnp.int32, small.shape, 1)
    column = jnp.transpose(jnp.broadcast_to(column, (EXTRA, width)))
    small[...] = jnp.where(lanes == GAIN_A, column, small_ref[...])
    store_parts(small, parts, me, block, cols)


def slots_kernel(parts, at_ref, order_col, order_row, own, other, code, *refs):
    picks, rows_out, whole = refs[: len(parts)], refs[-2], refs[-1]
    core = at_ref[1]
    rows = own.shape[0]
    width = own.shape[1]
    whole[pl.ds(pl.multiple_of(core * rows, rows), rows), :width] = own[...]
    whole[pl.ds(pl.multiple_of((1 - core) * rows, rows), rows), :width] = other[...]
    whole[:, width:] = code[...]
    none = order_row.shape[0] // 2 * order_row.shape[1]
    first = core * sum(parts)
    for expert in range(order_row.shape[0]):
        row = order_row[expert : expert + 1, :]
        ahead = (order_col[:, expert : expert + 1] < row).astype(f32)
        position = jnp.sum(ahead, axis=0, keepdims=True).astype(jnp.int32)
        position = jnp.where(row < none, position, -1)
        low = first
        for pick, count in zip(picks, parts):
            slot = lax.broadcasted_iota(jnp.int32, (count, row.shape[1]), 0) + low
            pick[expert * count : (expert + 1) * count, :] = (slot == position).astype(bf16)
            low = low + count
    low = 0
    for pick, count in zip(picks, parts):
        taken = lax.dot_general(pick[...], whole[...], NN, preferred_element_type=f32)
        rows_out[:, low : low + count] = taken.astype(bf16).reshape(
            order_row.shape[0], count, whole.shape[1]
        )
        low += count


def take_kernel(at_ref, own, other, *refs):
    count = (len(refs) - 1) // 2
    picks, outs, whole = refs[:count], refs[count:-1], refs[-1]
    core = at_ref[1]
    rows = own.shape[0]
    whole[pl.ds(pl.multiple_of(core * rows, rows), rows)] = own[...]
    whole[pl.ds(pl.multiple_of((1 - core) * rows, rows), rows)] = other[...]
    for pick, out in zip(picks, outs):
        out[...] = lax.dot_general(
            pick[...], whole[...], NN, preferred_element_type=f32
        ).astype(bf16)


def give_kernel(count, at_ref, *refs):
    picks, values, (own, other) = refs[:count], refs[count:-2], refs[-2:]
    rows = own.shape[0]
    if len(values) < count:
        whole, values, low = values[0][...], [], 0
        for pick in picks:
            each = pick.shape[0] // whole.shape[0]
            values.append(whole[:, low : low + each].reshape(pick.shape[0], whole.shape[2]))
            low += each
    for target, half in ((other, 1 - at_ref[1]), (own, at_ref[1])):
        columns = pl.ds(pl.multiple_of(half * rows, rows), rows)
        total = None
        for pick, value in zip(picks, values):
            part = lax.dot_general(
                pick[:, columns], value[...], TN, preferred_element_type=f32
            )
            total = part if total is None else total + part
        target[...] = total.astype(target.dtype)


def gelu_parts(value):
    square = value * value
    inner = value * (0.7978845608028654 + 0.035677408136300125 * square)
    tanh = jnp.tanh(inner)
    half = 0.5 + 0.5 * tanh
    slope = half + 0.5 * value * (1.0 - tanh * tanh) * (
        0.7978845608028654 + 3.0 * 0.035677408136300125 * square
    )
    return value * half, slope


def moe_kernel(plan, at_ref, router_ref, x_in, g_in, *refs):
    copies, hidden, blocks, outer, first, groups = plan
    weight_count = len(set(c[0] for c in copies))
    if first:
        refs = refs[1:]
    sources, outs, refs = refs[:weight_count], refs[weight_count:][:5], refs[weight_count + 5 :]
    weights, xs, gs = refs[:3]
    buffers = refs[3:8]
    weight_sems, in_sems, out_sems = refs[8:]
    branch, gradn, act_all, gp_all, geo_all = buffers
    _, rows, width = xs.shape
    whole = 2 * hidden
    expert = at_ref[0] % CUBE

    weight_copies = []
    block_rows = weights.shape[0] // outer
    for number, (source, entry, low, length, offset, from_col, to_col, cols) in enumerate(copies):
        row = pl.multiple_of(((at_ref[0] // CUBE) ^ offset) * block_rows + low, 16)
        weight_copies.append(
            pltpu.make_async_copy(
                sources[source].at[entry, :, pl.ds(from_col, cols)],
                weights.at[pl.ds(row, length), pl.ds(to_col, cols)],
                weight_sems.at[number],
            )
        )
    weight_order = sorted(range(len(copies)), key=lambda k: copies[k][5] // hidden)
    in_copies = []
    for block in range(blocks):
        span = pl.ds(block * rows, rows)
        for kind, (source, target) in enumerate(((x_in, xs), (g_in, gs))):
            held = (span,)
            if kind == 1:
                held = pl.ds(block * groups, groups), pl.ds(first, rows // groups)
            in_copies.append(
                pltpu.make_async_copy(
                    source.at[held], target.at[block], in_sems.at[2 * block + kind]
                )
            )
    in_copies[0].start()
    for k in weight_order:
        weight_copies[k].start()
    for copy in in_copies[1:]:
        copy.start()
    out_copies = []
    for block in range(blocks):
        in_copies[2 * block].wait()
        x = xs[block]
        logits = lax.dot_general(x, router_ref[...], NN, preferred_element_type=f32)
        if block == 0:
            for k in weight_order:
                if copies[k][5] < 2 * hidden:
                    weight_copies[k].wait()
        pre = lax.dot_general(x, weights[:, : 2 * whole], NN, preferred_element_type=f32)
        in_copies[2 * block + 1].wait()
        both = gs[block].reshape(rows, gs.shape[3])
        routed = both[:, width:].astype(f32) > 0.5
        lanes = lax.broadcasted_iota(jnp.int32, routed.shape, 1)
        logits = jnp.where(routed, logits, -1e30)
        expo = jnp.where(routed, jnp.exp(logits - jnp.max(logits, axis=1, keepdims=True)), 0.0)
        total = jnp.sum(expo, axis=1, keepdims=True)
        gate = jnp.sum(jnp.where(lanes == expert, expo, 0.0), axis=1, keepdims=True)
        gate = gate / jnp.where(total > 0.0, total, 1.0)

        gate_pre, up_pre = pre[:, :whole], pre[:, whole:]
        gelu, slope = gelu_parts(gate_pre)
        act = (gelu * up_pre).astype(bf16)
        act_all[block] = act
        if block == 0:
            for k in weight_order:
                if copies[k][5] == 2 * hidden:
                    weight_copies[k].wait()
        down = weights[:, 2 * whole :]
        expert_out = lax.dot_general(act, down, NT, preferred_element_type=f32)
        branch[block] = (gate * expert_out).astype(bf16).reshape(branch.shape[1:])
        g = both[:, :width].astype(f32)
        grad_gate = jnp.sum(g * expert_out, axis=1, keepdims=True)
        gradn[block, :, width:] = jnp.where(lanes == expert, grad_gate, 0.0).astype(bf16)
        geo = (gate * g).astype(bf16)
        geo_all[block] = geo
        grad_act = lax.dot_general(geo, down, NN, preferred_element_type=f32)
        grad_gate_pre = (grad_act * up_pre * slope).astype(bf16)
        grad_up_pre = (grad_act * gelu).astype(bf16)
        for side in range(2):
            cols = slice(side * hidden, (side + 1) * hidden)
            for kind, part in enumerate((grad_gate_pre, grad_up_pre)):
                at = (2 * side + kind) * hidden
                gp_all[block, :, at : at + hidden] = part[:, cols]
        grad_in = lax.dot_general(
            grad_gate_pre, weights[:, :whole], NT, preferred_element_type=f32
        ) + lax.dot_general(
            grad_up_pre, weights[:, whole : 2 * whole], NT, preferred_element_type=f32
        )
        gradn[block, :, :width] = grad_in.astype(bf16)
        for number, (source, target) in enumerate(zip(buffers, outs)):
            if number == 0:
                held = pl.ds(block * groups, groups), pl.ds(first, rows // groups)
            else:
                held = (pl.ds(block * rows, rows),)
            copy = pltpu.make_async_copy(
                source.at[block], target.at[held], out_sems.at[5 * block + number]
            )
            copy.start()
            out_copies.append(copy)
    for copy in out_copies:
        copy.wait()


def moe(at, x, g, router, pieces, hidden, outer, sequences, capacity, branch=None):
    copies = []
    for source, (array, first, low, side) in enumerate(pieces):
        for entry in range(array.shape[0]):
            for kind in range(3):
                copies.append(
                    (source, entry, low, array.shape[1], first + entry, kind * hidden)
                    + ((2 * kind + side) * hidden, hidden)
                )
    total, width = x.shape
    blocks = 2
    rows = total // blocks
    widths = (width, width + EXTRA, 2 * hidden, 4 * hidden, width)
    each = total // sequences
    first = 0 if branch is None else capacity - each
    args = [x, g] + ([] if branch is None else [branch]) + [p[0] for p in pieces]
    groups = sequences // blocks
    buffers = [(blocks, rows, w) for w in widths]
    buffers[0] = (blocks, groups, each, width)
    return pl.pallas_call(
        functools.partial(moe_kernel, (copies, hidden, blocks, outer, first, groups)),
        out_shape=[jax.ShapeDtypeStruct((sequences, capacity, width), bf16)]
        + [jax.ShapeDtypeStruct((total, w), bf16) for w in widths[1:]],
        in_specs=[pl.BlockSpec(memory_space=pltpu.SMEM), pl.BlockSpec(memory_space=pltpu.VMEM)]
        + [pl.BlockSpec(memory_space=pl.ANY)] * len(args),
        out_specs=[pl.BlockSpec(memory_space=pl.ANY)] * 5,
        scratch_shapes=[
            pltpu.VMEM((width, 6 * hidden), bf16),
            pltpu.VMEM((blocks, rows, width), bf16),
            pltpu.VMEM((blocks, groups, each, width + EXTRA), bf16),
        ]
        + [pltpu.VMEM(dims, bf16) for dims in buffers]
        + [
            pltpu.SemaphoreType.DMA((len(copies),)),
            pltpu.SemaphoreType.DMA((2 * blocks,)),
            pltpu.SemaphoreType.DMA((5 * blocks,)),
        ],
        input_output_aliases={} if branch is None else {4: 0},
        compiler_params=pltpu.CompilerParams(vmem_limit_bytes=60 * 1024 * 1024),
        cost_estimate=BRIEF,
        name="experts",
    )(at, router, *args)


def weight_grads_kernel(calls, pre, down, at_ref, *refs):
    kinds = int(pre) + int(down)
    pairs = []
    for _ in range(kinds):
        pairs.append((refs[:calls], refs[calls : 2 * calls]))
        refs = refs[2 * calls :]
    outs, buffers, sems = refs[: 2 * kinds], refs[2 * kinds : -1], refs[-1]
    cols = buffers[0].shape[1]
    columns = pl.ds(pl.multiple_of(at_ref[2] * cols, cols), cols)
    copies = []
    for number, (lefts, rights) in enumerate(pairs):
        row = 0
        for left, right in zip(lefts, rights):
            rows = pl.ds(row, left.shape[0])
            for source, target in (
                (left.at[:, columns], buffers[2 * number].at[rows]),
                (right, buffers[2 * number + 1].at[rows]),
            ):
                copies.append(pltpu.make_async_copy(source, target, sems.at[len(copies)]))
                copies[-1].start()
            row += left.shape[0]
    for number in range(kinds):
        for copy in copies[2 * calls * number : 2 * calls * (number + 1)]:
            copy.wait()
        total = lax.dot_general(
            buffers[2 * number][...],
            buffers[2 * number + 1][...],
            TN,
            preferred_element_type=f32,
        )
        width = total.shape[1]
        outs[2 * number][...] = total[:, : width // 2]
        outs[2 * number + 1][...] = total[:, width // 2 :].astype(bf16)


def weight_grads(at, half, pre, down):
    args, outs, scratch = [], [], []
    for pairs in (pre, down):
        if not pairs:
            continue
        args += [p[0] for p in pairs] + [p[1] for p in pairs]
        rows = sum(p[0].shape[0] for p in pairs)
        left, right = pairs[0][0].shape[1] // 2, pairs[0][1].shape[1]
        outs += [((left, right // 2), f32), ((left, right // 2), bf16)]
        scratch += [(rows, left), (rows, right)]
    return pl.pallas_call(
        functools.partial(weight_grads_kernel, len(pre or down), bool(pre), bool(down)),
        out_shape=[jax.ShapeDtypeStruct(dims, kind) for dims, kind in outs],
        in_specs=[pl.BlockSpec(memory_space=pltpu.SMEM)]
        + [pl.BlockSpec(memory_space=pl.ANY)] * len(args),
        out_specs=[pl.BlockSpec(memory_space=pltpu.VMEM)] * len(outs),
        scratch_shapes=[pltpu.VMEM(dims, bf16) for dims in scratch]
        + [pltpu.SemaphoreType.DMA((len(args),))],
        compiler_params=pltpu.CompilerParams(vmem_limit_bytes=60 * 1024 * 1024),
        cost_estimate=BRIEF,
        name="weight_grads",
    )(jnp.concatenate([at, half.reshape(1)]), *args)


def per_device(
    count,
    hidden_in,
    segment_ids,
    routes,
    slot_order,
    gain_attn,
    w_query,
    w_key,
    w_value,
    w_out,
    gain_ffn,
    w_router,
    w_gate,
    w_up,
    w_down,
    grad_out,
):
    tok_rows, width = hidden_in.shape
    seq_len = segment_ids.shape[0]
    top_count = routes.shape[1]
    experts, block, hidden = w_gate.shape
    capacity = 9 * seq_len * top_count // (8 * experts)
    me = lax.axis_index("dp").astype(jnp.int32)
    core = lax.axis_index("tensor").astype(jnp.int32)
    at = jnp.stack([me, core])
    groups = [list(range(first, first + CUBE)) for first in range(0, count, CUBE)]
    heads_cols, kv_cols = w_query.shape[1], w_key.shape[1]
    qkv_cols = heads_cols + 2 * kv_cols
    heads, kv_heads = heads_cols // HD, kv_cols // HD

    def shape(rows, cols, dtype=bf16):
        return jax.ShapeDtypeStruct((rows, cols), dtype)

    def near(own):
        return {0: own} | {bit: swap(own, bit, count) for bit in NEAR}

    def far(got):
        return got | {
            3: swap(got[2], 1, count),
            6: swap(got[4], 2, count),
            5: swap(got[1], 4, count),
        }

    def last(got, axis):
        spans = halves(got[0].shape[axis])
        return got | {
            7: swap(cut(got[6], spans[0], axis), 1, count),
            8: swap(cut(got[5], spans[1], axis), 2, count),
        }

    small = jnp.concatenate([w_router, gain_attn[:, None], gain_ffn[:, None]], axis=1)
    small = jnp.pad(small, ((0, 0), (0, EXTRA - small.shape[1])))
    pair = outer_pair(
        jnp.concatenate([w_query, w_key, w_value, small, w_out.T], axis=1), count
    )
    hidden_other = swap_core(hidden_in)

    expert_shard = jnp.concatenate([w_gate, w_up, jnp.swapaxes(w_down, 1, 2)], axis=2)
    expert_rows = lax.all_to_all(
        expert_shard.reshape(experts * block, 3 * hidden),
        "dp",
        0,
        0,
        tiled=True,
        axis_index_groups=groups,
    )

    order = jnp.min(
        jnp.where(
            routes[:, :, None] == jnp.arange(experts, dtype=jnp.int32),
            slot_order[0].reshape(seq_len, top_count)[:, :, None],
            seq_len * top_count,
        ),
        axis=1,
    )
    code = (order < seq_len * top_count).astype(bf16)
    code = jnp.pad(code, ((0, 0), (0, EXTRA - experts)))
    code_own = lax.dynamic_slice_in_dim(code, core * tok_rows, tok_rows, 0)
    first_part = (capacity // 4 + 15) // 16 * 16
    slot_parts = (first_part, capacity // 2 - first_part)
    grad_other = swap_core(grad_out)
    slots = vmem_call(
        functools.partial(slots_kernel, slot_parts),
        [shape(experts * part, seq_len) for part in slot_parts]
        + [jax.ShapeDtypeStruct((experts, sum(slot_parts), width + EXTRA), bf16)],
        [pltpu.VMEM((seq_len, width + EXTRA), bf16)],
        [(at, 1), (order, 0), (order.T, 0), (grad_out, 0), (grad_other, 0), (code, 0)],
        "slots",
    )
    picks, grad_rows = slots[:2], slots[2]

    def exchange(rows):
        return lax.all_to_all(rows, "dp", 0, 0, tiled=True, axis_index_groups=groups)

    cosine, sine_table = rope_tables(seq_len, HD)
    cosine = jnp.concatenate([cosine, cosine], axis=1)
    sine_table = jnp.concatenate([-sine_table, sine_table], axis=1)
    seg_col, seg_row = segment_ids[:, None], segment_ids[None, :]

    (pair,) = gate([pair], cosine, sine_table, hidden_other, grad_other)
    if count == 2 * CUBE:
        edges = [expert_rows.shape[0] * k // 48 // 16 * 16 for k in (0, 13, 26, 32, 48)]
    else:
        edges = [0] * 4 + [expert_rows.shape[0]]
    pieces = [(expert_rows[None], 0, 0, 0), (swap_core(expert_rows)[None], 0, 0, 1)]

    def outer_chunk(k, *events):
        low, high = edges[k], edges[k + 1]
        if high == low:
            return [], []
        (chunk,) = gate([cut(expert_rows, (low, high), 0)], *events)
        arrays, first, swapped = outer_gather(chunk, count)[1:], 1, []
        for array in arrays:
            swapped.append(swap_core(array))
            pieces.append((array, first, low, 0))
            pieces.append((swapped[-1], first, low, 1))
            first += array.shape[0]
        return arrays, swapped

    with jax.named_scope("weights_near"):
        got = near(pair)
    arrays, swapped = outer_chunk(0, pair)
    got = gate_dict(got, NEAR, grad_rows, arrays, pieces[1][0])
    with jax.named_scope("weights_far"):
        got = far(got)
    arrays, swapped_next = outer_chunk(1, got[1])
    got = gate_dict(got, FAR, arrays, swapped)
    with jax.named_scope("weights_last"):
        got = last(got, 1)
    arrays, swapped = outer_chunk(2, got[3])
    got = gate_dict(got, LAST, arrays, swapped_next)
    sources, copies = piece_copies(got, block, me, count)
    grad_rows, seg_col = gate([grad_rows, seg_col], got[7])
    with jax.named_scope("grads_rows"):
        grad_rows = exchange(grad_rows)
    attended = vmem_call(
        functools.partial(attend_kernel, copies, (heads, kv_heads, len(sources))),
        [
            shape(seq_len, width),
            shape(seq_len, width),
            shape(seq_len, heads_cols),
            shape(seq_len, kv_cols),
            shape(seq_len, kv_cols),
            shape(seq_len, heads_cols),
            shape(seq_len, HD, f32),
            shape(width, qkv_cols),
            shape(width, EXTRA),
            shape(width, heads_cols),
            shape(16, width, f32),
            shape(tok_rows, width, f32),
            shape(tok_rows, width),
        ],
        [pltpu.SemaphoreType.DMA((3 * len(copies),))],
        [(at, 1), (hidden_in, 0), (hidden_other, 0), (seg_col, 0), (seg_row, 0)]
        + [(cosine, 0), (sine_table, 0)]
        + [(piece, 2) for piece in sources],
        "attend",
        flops=2 * seq_len * (width * (qkv_cols + heads_cols) + heads_cols * seq_len),
    )
    hid, normed, qs, ks, vs, mixed, lse, full_qkv, router, out_wt, gains = attended[:-2]
    attn_own, attn_other = attended[-2:]
    middle, normed2 = vmem_call(
        middle_kernel,
        [shape(tok_rows, width, f32), shape(tok_rows, width)],
        [],
        [(hidden_in, 0), (attn_own, 0), (swap_core(attn_other), 0), (gains, 0)],
        "middle",
    )

    rows = vmem_call(
        take_kernel,
        [shape(experts * part, width) for part in slot_parts],
        [pltpu.VMEM((seq_len, width), bf16)],
        [(at, 1), (normed2, 0), (swap_core(normed2), 0)] + [(pick, 0) for pick in picks],
        "take",
    )
    rows = list(rows)
    rows[0], grad_rows = gate([rows[0], grad_rows], swapped)
    with jax.named_scope("tokens_rows"):
        x_first = exchange(rows[0])
    arrays, _ = outer_chunk(3, rows[0])
    x_first, rows_second = gate([x_first, rows[1]], arrays)
    with jax.named_scope("tokens_rows"):
        x_second = exchange(rows_second)

    def experts_on(x, g, router, branch=None):
        held = (CUBE, sum(slot_parts))
        return moe(at, x, g, router, pieces, hidden, count // CUBE, *held, branch)

    branch, gradn_first, *first = experts_on(x_first, grad_rows, router)
    with jax.named_scope("gradn_rows"):
        gradn_first = exchange(gradn_first)
    (second_router,) = gate([router], first[0])
    branch, gradn_second, *second = experts_on(x_second, grad_rows, second_router, branch)

    xs = (x_first, x_second)
    pre_pairs = [(x, call[1]) for x, call in zip(xs, (first, second))]
    down_pairs = [(call[2], call[0]) for call in (first, second)]
    bits = outer_bits(count)
    top = (me // bits[-1]) % 2 if bits else jnp.zeros((), jnp.int32)

    def part_grads(half, pre, down, event):
        half = gate([half.reshape(1)], event)[0]
        outs = weight_grads(at, half, pre, down)
        return [(outs[i], outs[i + 1]) for i in range(0, len(outs), 2)]

    def both_cores(pair):
        return pair[0] + swap_core(pair[1]).astype(f32)

    (send_down,) = part_grads(1 - top, [], down_pairs, second[0])
    (gradn_second,) = gate([gradn_second], send_down)
    event = gradn_second
    with jax.named_scope("gradn_rows"):
        gradn_second = exchange(gradn_second)
    with jax.named_scope("expert_scatter"):
        down_part = both_cores(send_down).astype(bf16)
    (send_pre,) = part_grads(1 - top, pre_pairs, [], event)
    keep_pre, keep_down = part_grads(top, pre_pairs, down_pairs, send_pre)
    with jax.named_scope("expert_scatter"):
        send_pre = both_cores(send_pre).astype(bf16)

        sent = jnp.concatenate([send_pre, down_part], axis=1)
        sent_got = swap(sent, bits[-1], count) if bits else sent

    def give(picks, values, name):
        own, other = vmem_call(
            functools.partial(give_kernel, len(picks)),
            [shape(tok_rows, values[0].shape[-1], f32), shape(tok_rows, values[0].shape[-1])],
            [],
            [(at, 1)] + [(pick, 0) for pick in picks] + [(value, 0) for value in values],
            name,
        )
        return own, swap_core(other)

    gradn_second, gradn_first = gate([gradn_second, gradn_first], keep_pre[0])
    gradn = list(give(picks, (gradn_first, gradn_second), "give_gradn"))

    grad_middle, grad_mid_r, small_f = vmem_call(
        middle_back_kernel,
        [shape(tok_rows, width, f32), shape(tok_rows, width), shape(width, EXTRA, f32)],
        [],
        [(middle, 0), (normed2, 0), (grad_out, 0), (code_own, 0), (router, 0), (gains, 0)]
        + [(array, 0) for array in gradn],
        "middle_back",
    )

    grad_mid_other = swap_core(grad_mid_r)
    (branch,) = gate([branch], gradn[0])
    with jax.named_scope("branch_rows"):
        branch = exchange(branch)
    normed_own, normed_other, *parts = vmem_call(
        functools.partial(attend_back_kernel, block, (heads, kv_heads)),
        [shape(tok_rows, width, f32), shape(tok_rows, width)]
        + part_shapes(count, block, qkv_cols + EXTRA + heads_cols),
        [
            pltpu.VMEM((width, qkv_cols), f32),
            pltpu.VMEM((width, EXTRA), f32),
            pltpu.VMEM((seq_len, qkv_cols), bf16),
            pltpu.VMEM((seq_len, width), bf16),
            pltpu.VMEM((seq_len, heads_cols), bf16),
            pltpu.VMEM((width, heads_cols), f32),
        ],
        [(at, 1), (grad_mid_r, 0), (grad_mid_other, 0), (mixed, 0), (out_wt, 0)]
        + [(small_f, 0), (qs, 0), (ks, 0), (vs, 0), (lse, 0), (seg_col, 0)]
        + [(seg_row, 0), (cosine, 0), (sine_table, 0), (hid, 0), (normed, 0), (full_qkv, 0)],
        "attend_back",
        flops=4 * seq_len * (width * (qkv_cols + heads_cols) + 2 * heads_cols * seq_len),
    )
    parts = spread_parts(parts, me, count)

    parts = gate_dict(parts, (3,) + LAST)
    with jax.named_scope("attn_last"):
        got = sum_last(parts, count)
    grad_normed = normed_own + swap_core(normed_other).astype(f32)
    gated = gate([got[7], got[8], parts[3]])
    got, parts[3] = dict(zip(LAST, gated)), gated[2]
    with jax.named_scope("attn_far"):
        terms = far_terms(parts, got)
        attn_far = sum_far(parts, terms, count)
    with jax.named_scope("expert_scatter"):
        (sent_got,) = gate([sent_got], terms)
        keep = jnp.concatenate([both_cores(keep_pre), both_cores(keep_down)], axis=1)
        total = keep + sent_got.astype(f32) if bits else jnp.concatenate([keep, sent_got], axis=0)
        for bit in reversed(bits[:-1]):
            half = total.shape[0] // 2
            high = (me // bit) % 2
            mine = lax.dynamic_slice_in_dim(total, high * half, half, 0)
            other = lax.dynamic_slice_in_dim(total, (1 - high) * half, half, 0)
            total = mine + swap(other.astype(bf16), bit, count).astype(f32)
        total = total.astype(bf16)
    gated = gate([attn_far[k] for k in NEAR] + [total, branch])
    attn_far, total, branch = dict(zip(NEAR, gated)), gated[3], gated[4]
    with jax.named_scope("attn_near"):
        attn_near = sum_near(near_terms(parts, attn_far), count)
    with jax.named_scope("expert_scatter"):
        total = exchange(total)
    gated = gate([attn_near[k] for k in NEAR] + [branch])
    attn_near, branch = dict(zip(NEAR, gated)), gated[3]
    with jax.named_scope("attn_outer"):
        attn_grads = outer_sum(sum_own(parts, attn_near), count)
    branch_own, branch_other = give(picks, (branch,), "give_branch")
    layer_out = middle + branch_own + branch_other.astype(f32)

    expert_grads = total.reshape(experts, block, 3 * hidden).astype(f32)
    grad_gate_w = expert_grads[:, :, :hidden]
    grad_up_w = expert_grads[:, :, hidden : 2 * hidden]
    grad_down_w = jnp.swapaxes(expert_grads[:, :, 2 * hidden :], 1, 2)
    scaled_in, root_in = rms_parts(hidden_in.astype(f32))
    grad_in = grad_middle + norm_backward(grad_normed, scaled_in, root_in, gains[GAIN_A])
    smalls = attn_grads[:, qkv_cols : qkv_cols + EXTRA]
    smalls = smalls + swap_core(smalls)
    return (
        layer_out,
        grad_in,
        smalls[:, GAIN_A],
        attn_grads[:, :heads_cols],
        attn_grads[:, heads_cols : heads_cols + kv_cols],
        attn_grads[:, heads_cols + kv_cols : qkv_cols],
        attn_grads[:, qkv_cols + EXTRA :].T,
        smalls[:, GAIN_F],
        smalls[:, :experts],
        grad_gate_w,
        grad_up_w,
        grad_down_w,
    )


def solution(mesh):
    return jax.shard_map(
        functools.partial(per_device, mesh.shape["dp"]),
        mesh=mesh,
        in_specs=(
            P(("dp", "tensor"), None),
            P("dp"),
            P("dp", None),
            P("dp", None),
            P("dp"),
            P("dp", "tensor"),
            P("dp", "tensor"),
            P("dp", "tensor"),
            P("tensor", "dp"),
            P("dp"),
            P("dp", None),
            P(None, "dp", "tensor"),
            P(None, "dp", "tensor"),
            P(None, "tensor", "dp"),
            P(("dp", "tensor"), None),
        ),
        out_specs=(
            P(("dp", "tensor"), None),
            P(("dp", "tensor"), None),
            P("dp"),
            P("dp", "tensor"),
            P("dp", "tensor"),
            P("dp", "tensor"),
            P("tensor", "dp"),
            P("dp"),
            P("dp", None),
            P(None, "dp", "tensor"),
            P(None, "dp", "tensor"),
            P(None, "tensor", "dp"),
        ),
        check_vma=False,
    )
```

time: 2410 us -> 493 us (0.20)
  waiting for transfers between devices: 1770 us -> 163 us
  blocking collectives: 189 us -> 0 us
  matrix products: 168 us -> 0 us
  local copies, waits for them, and re-layouts: 195 us -> 38.5 us
  Pallas kernels: 0 us -> 138 us
  starting transfers between devices: 1.78 us -> 105 us
    reduce_scatter x11 -> x0, waiting for transfers between devices: 1430 us -> none  [the longest x1 290 us: per_device(): lax.psum_scatter(grad_down_w, 'dp', scatter_dimension=2, tiled=True)]
    all_gather x9 -> x0, waiting for transfers between devices: 321 us -> none  [the longest x1 112 us: per_device(): lax.all_gather(w_down, 'dp', axis=2, tiled=True)]
    dot_general x30 -> x0, matrix products: 168 us -> none  [the longest x1 15.5 us: per_device(): jnp.einsum('ech,edh->ecd', grad_up_r, upper_w, preferred_element_type=jnp...]
    pallas_call x0 -> x38, Pallas kernels: none -> 138 us  [the longest x8 68.5 us: vmem_call(): pl.pallas_call(kernel, out_shape=out_shapes, in_specs=[pl.BlockSpec(memor...]
    ppermute x0 -> x41, waiting for transfers between devices: none -> 125 us  [the longest x23 114 us: swap(): return lax.ppermute(values, 'dp', [(i, i ^ bit) for i in range(count)])]
    all_gather x3 -> x0, blocking collectives: 96.2 us -> none  [the longest x1 35.5 us: per_device(): lax.all_gather(w_key, 'dp', axis=0, tiled=True)]
    gather x11 -> x0, local copies, waits for them, and re-layouts: 93.1 us -> none  [the longest x1 19.5 us: per_device(): picked = out_padded[placing].reshape(seq_len, top_count, width)]
    unnamed x2 -> x0, blocking collectives: 89.1 us -> none
  transfers between devices with their start and end apart: 22 -> 49, of which waited for: 17 -> 20; matrix products, arithmetic and copies ran while one was open for 12% -> 12% of each run, Pallas kernels for 0% -> 27%
where the time goes in v2:
time: 493 us; the launch traced here: 486 us
  waiting for transfers between devices  163 us (33%)
  Pallas kernels  138 us (28%)
  starting transfers between devices  105 us (21%)
  other arithmetic  39.2 us (8%)
  local copies, waits for them, and re-layouts  38.5 us (8%)
    ppermute x23, waiting for transfers between devices, swap(): return lax.ppermute(values, 'dp', [(i, i ^ bit) for i in range(count)])  114 us
    pallas_call x8, Pallas kernels, vmem_call(): pl.pallas_call(kernel, out_shape=out_shapes, in_specs=[pl.BlockSpec(memor...  68.5 us
    ppermute x18, starting transfers between devices, swap_core(): return lax.ppermute(values, 'tensor', [(0, 1), (1, 0)])  41.3 us
    pallas_call x2, Pallas kernels, moe(): pl.pallas_call(functools.partial(moe_kernel, (copies, hidden, blocks, out...  38.5 us
    all_to_all x7, starting transfers between devices, exchange(): lax.all_to_all(rows, 'dp', 0, 0, tiled=True, axis_index_groups=groups)  31.3 us
    ppermute x23, starting transfers between devices, swap(): return lax.ppermute(values, 'dp', [(i, i ^ bit) for i in range(count)])  27.8 us
    pallas_call x3, Pallas kernels, weight_grads(): pl.pallas_call(functools.partial(weight_grads_kernel, len(pre or down), b...  23.2 us
    all_to_all x7, waiting for transfers between devices, exchange(): lax.all_to_all(rows, 'dp', 0, 0, tiled=True, axis_index_groups=groups)  21.4 us
  transfers between devices with their start and end apart: 49, of which 20 were waited for; matrix products, arithmetic and copies ran while one was open for 12% of the time, Pallas kernels for 27%

profile of v2, /device:TPU:3, one launch (start us, length us, event | category | flops | bytes accessed | tf_op | source)
XLA Modules:
  0.0 486.0 jit_solution(13013152012353137337)
XLA Ops:
  3.5 4.8 all-to-all-start
  20.1 16.8 %all-to-all-done = bf16[8,96,1152]{2,1,0:T(8,128)(2,1)S(1)} async-done(((bf16[8,96,1152]{2,1,0:T(8,128)(2,1)}), bf16[8,96,1152]{2,1,0:T(8,128)(2,1)S(1)}, u32[]{:S(2)}, u32[]{:S(2)}) %all-to-all-start) | async-done | bytes 1769504 | tf_op jit(solution)/shard_map/all_to_all | solution.py:828
  50.4 6.8 %slots.1 = (bf16[640,512]{1,0:T(8,128)(2,1)}, bf16[512,512]{1,0:T(8,128)(2,1)}, bf16[8,144,1664]{2,1,0:T(8,128)(2,1)}) custom-call(s32[2]{0:T(128)} %pad_add_fusion.at_ref, s32[512,8]{1,0:T(8,128)} %copy-done.25, s32[8,512]{1,0:T(8,128)} %bitcast.58, bf16[256,1536]{1,0:T(8,128)(2,1)} %grad_out.1, bf16[256,1536]{1,0:T(8,128)(2,1)} %collective-permute-done.1.other.refs_4_, ...), custom_call_target="tpu_custom_call" | custom-call | bytes 3000000 | tf_op jit(solution)/shard_map/slots/pallas_call | solution.py:264
  57.2 5.0 %collective-permute-done.3.refs_0_ = bf16[2,96,1920]{2,1,0:T(8,128)(2,1)S(1)} collective-permute-done((bf16[2,96,1920]{2,1,0:T(8,128)(2,1)}, bf16[2,96,1920]{2,1,0:T(8,128)(2,1)S(1)}, u32[]{:S(2)}, u32[]{:S(2)}) %collective-permute-start.3) | collective-permute-done | bytes 737312 | tf_op jit(solution)/shard_map/weights_near/ppermute | solution.py:43
  62.2 11.1 %collective-permute-done.5.refs_2_ = bf16[2,96,1920]{2,1,0:T(8,128)(2,1)} collective-permute-done((bf16[2,96,1920]{2,1,0:T(8,128)(2,1)}, bf16[2,96,1920]{2,1,0:T(8,128)(2,1)}, u32[]{:S(2)}, u32[]{:S(2)}) %collective-permute-start.5) | collective-permute-done | bytes 737312 | tf_op jit(solution)/shard_map/weights_near/ppermute | solution.py:43
  81.1 20.9 %collective-permute-done.11.refs_3_.refs_4_.refs_5_ = bf16[1,208,1152]{2,1,0:T(8,128)(2,1)} collective-permute-done((bf16[1,208,1152]{2,1,0:T(8,128)(2,1)}, bf16[1,208,1152]{2,1,0:T(8,128)(2,1)}, u32[]{:S(2)}, u32[]{:S(2)}) %collective-permute-start.11) | collective-permute-done | bytes 479264 | tf_op jit(solution)/shard_map/ppermute | solution.py:43
  115.3 9.4 %collective-permute-done.15.refs_2_.refs_6_.refs_7_ = bf16[1,96,1152]{2,1,0:T(8,128)(2,1)S(1)} collective-permute-done((bf16[1,96,1152]{2,1,0:T(8,128)(2,1)}, bf16[1,96,1152]{2,1,0:T(8,128)(2,1)S(1)}, u32[]{:S(2)}, u32[]{:S(2)}) %collective-permute-start.15) | collective-permute-done | bytes 221216 | tf_op jit(solution)/shard_map/ppermute | solution.py:43
  126.2 5.8 %all-to-all-start.1 = ((bf16[8,144,1664]{2,1,0:T(8,128)(2,1)}), bf16[8,144,1664]{2,1,0:T(8,128)(2,1)}, u32[]{:S(2)}, u32[]{:S(2)}) async-start(bf16[8,144,1664]{2,1,0:T(8,128)(2,1)} %get-tuple-element.123), calls=%async_computation.1 | async-start | bytes 7667712 | tf_op jit(solution)/shard_map/grads_rows/all_to_all | solution.py:862
  132.0 13.9 %attend.1 = (bf16[512,1536]{1,0:T(8,128)(2,1)}, bf16[512,1536]{1,0:T(8,128)(2,1)}, bf16[512,768]{1,0:T(8,128)(2,1)}, bf16[512,128]{1,0:T(8,128)(2,1)}, bf16[512,...) custom-call(s32[2]{0:T(128)} %pad_add_fusion.at_ref, ...), custom_call_target="tpu_custom_call" | custom-call | bytes 3000000 | tf_op jit(solution)/shard_map/attend/pallas_call | solution.py:264
  157.4 5.0 %take.1 = (bf16[640,1536]{1,0:T(8,128)(2,1)}, bf16[512,1536]{1,0:T(8,128)(2,1)}) custom-call(s32[2]{0:T(128)} %pad_add_fusion.at_ref, bf16[256,1536]{1,0:T(8,128)(2,1)} %get-tuple-element.120.own.normed, bf16[256,1536]{1,0:T(8,128)(2,1)} %copy-done.32, bf16[640,512]{1,0:T(8,128)(2,1)} %get-tuple-element.118.refs_0_, bf16[512,512]{1,0:T(8,128)(2,1)} %get-tuple-element.119.refs_1_), custom_call_target="tpu_custom_call" | custom-call | bytes 3000000 | tf_op jit(solution)/shard_map/take/pallas_call | solution.py:264
  162.4 17.9 %all-to-all-done.1.refs_1_ = bf16[8,144,1664]{2,1,0:T(8,128)(2,1)} async-done(((bf16[8,144,1664]{2,1,0:T(8,128)(2,1)}), bf16[8,144,1664]{2,1,0:T(8,128)(2,1)}, u32[]{:S(2)}, u32[]{:S(2)}) %all-to-all-start.1) | async-done | bytes 3833888 | tf_op jit(solution)/shard_map/grads_rows/all_to_all | solution.py:862
  185.8 29.9 %collective-permute-done.20.refs_2_.refs_8_.refs_9_ = bf16[1,256,1152]{2,1,0:T(8,128)(2,1)S(1)} collective-permute-done((bf16[1,256,1152]{2,1,0:T(8,128)(2,1)}, bf16[1,256,1152]{2,1,0:T(8,128)(2,1)S(1)}, u32[]{:S(2)}, u32[]{:S(2)}) %collective-permute-start.20) | collective-permute-done | bytes 589856 | tf_op jit(solution)/shard_map/ppermute | solution.py:43
  218.9 4.2 all-to-all-start.3
  229.1 20.8 %experts.2 = (bf16[8,144,1536]{2,1,0:T(8,128)(2,1)}, bf16[640,1664]{1,0:T(8,128)(2,1)}, bf16[640,768]{1,0:T(8,128)(2,1)}, bf16[640,1536]{1,0:T(8,128)(2,1)}, bf16[640,1536]{1,0:T(8,128)(2,1)}) custom-call(s32[2]{0:T(128)} %pad_add_fusion.at_ref, bf16[1536,128]{1,0:T(8,128)(2,1)} %get-tuple-element.121.router_ref.router, ...), custom_call_target="tpu_custom_call" | custom-call | bytes 3000000 | tf_op jit(solution)/shard_map/experts/pallas_call | solution.py:685
  251.1 5.0 %all-to-all-start.5 = ((bf16[8,80,1664]{2,1,0:T(8,128)(2,1)}), bf16[8,80,1664]{2,1,0:T(8,128)(2,1)}, u32[]{:S(2)}, u32[]{:S(2)}) async-start(bf16[8,80,1664]{2,1,0:T(8,128)(2,1)} %bitcast.52), calls=%async_computation.5 | async-start | bytes 4259840 | tf_op jit(solution)/shard_map/gradn_rows/all_to_all | solution.py:862
  256.9 17.8 %experts.3 = (bf16[8,144,1536]{2,1,0:T(8,128)(2,1)}, bf16[512,1664]{1,0:T(8,128)(2,1)}, bf16[512,768]{1,0:T(8,128)(2,1)}, bf16[512,1536]{1,0:T(8,128)(2,1)}, bf16[512,1536]{1,0:T(8,128)(2,1)}) custom-call(s32[2]{0:T(128)} %pad_add_fusion.at_ref, bf16[1536,128]{1,0:T(8,128)(2,1)} %gate.34.router_ref, ...), custom_call_target="tpu_custom_call", output_to_operand_aliasing={{0}: (4, {})} | custom-call | bytes 3000000 | tf_op jit(solution)/shard_map/experts/pallas_call | solution.py:685
  276.4 5.6 %weight_grads.3 = (f32[768,384]{1,0:T(8,128)}, bf16[768,384]{1,0:T(8,128)(2,1)}) custom-call(s32[3]{0:T(128)} %pad_add_fusion.1.at_ref, bf16[640,1536]{1,0:T(8,128)(2,1)} %get-tuple-element.133.refs_0_.refs_4_, bf16[512,1536]{1,0:T(8,128)(2,1)} %get-tuple-element.134.refs_1_.refs_5_, bf16[640,768]{1,0:T(8,128)(2,1)} %get-tuple-element.128.refs_1_.refs_2_.refs_6_, ...), custom_call_target="tpu_custom_call" | custom-call | bytes 3000000 | tf_op jit(solution)/shard_map/weight_grads/pallas_call | solution.py:755
  289.4 7.5 %weight_grads.4 = (f32[768,768]{1,0:T(8,128)}, bf16[768,768]{1,0:T(8,128)(2,1)}) custom-call(s32[3]{0:T(128)} %pad_add_fusion.3.at_ref, bf16[640,1536]{1,0:T(8,128)(2,1)} %get-tuple-element.126.x_in.refs_0_, bf16[512,1536]{1,0:T(8,128)(2,1)} %bitcast.44, bf16[640,1536]{1,0:T(8,128)(2,1)} %get-tuple-element.138.refs_2_, ...), custom_call_target="tpu_custom_call" | custom-call | bytes 3000000 | tf_op jit(solution)/shard_map/weight_grads/pallas_call | solution.py:755
  298.6 10.1 %weight_grads.5 = (f32[768,768]{1,0:T(8,128)}, bf16[768,768]{1,0:T(8,128)(2,1)}, f32[768,384]{1,0:T(8,128)}, bf16[768,384]{1,0:T(8,128)(2,1)}) custom-call(s32[3]{0:T(128)} %pad_add_fusion.4.at_ref, bf16[640,1536]{1,0:T(8,128)(2,1)} %get-tuple-element.126.x_in.refs_0_, bf16[512,1536]{1,0:T(8,128)(2,1)} %bitcast.45, ...), custom_call_target="tpu_custom_call" | custom-call | bytes 3000000 | tf_op jit(solution)/shard_map/weight_grads/pallas_call | solution.py:755
  310.0 6.2 %give_gradn.1 = (f32[256,1664]{1,0:T(8,128)}, bf16[256,1664]{1,0:T(8,128)(2,1)}) custom-call(s32[2]{0:T(128)} %pad_add_fusion.at_ref, bf16[640,512]{1,0:T(8,128)(2,1)} %get-tuple-element.118.refs_0_, bf16[512,512]{1,0:T(8,128)(2,1)} %get-tuple-element.119.refs_1_, bf16[640,1664]{1,0:T(8,128)(2,1)} %get-tuple-element.143.refs_2_, ...), custom_call_target="tpu_custom_call" | custom-call | bytes 3000000 | tf_op jit(solution)/shard_map/give_gradn/pallas_call | solution.py:264
  316.2 4.8 all-to-all-start.6
  334.0 6.4 %middle_back.1 = (f32[256,1536]{1,0:T(8,128)}, bf16[256,1536]{1,0:T(8,128)(2,1)}, f32[1536,128]{1,0:T(8,128)}) custom-call(f32[256,1536]{1,0:T(8,128)} %get-tuple-element.117.middle, bf16[256,1536]{1,0:T(8,128)(2,1)} %get-tuple-element.120.own.normed, bf16[256,1536]{1,0:T(8,128)(2,1)} %grad_out.1, bf16[256,128]{1,0:T(8,128)(2,1)} %constant_dynamic-slice_fusion.code, ...), custom_call_target="tpu_custom_call" | custom-call | bytes 3000000 | tf_op jit(solution)/shard_map/middle_back/pallas_call | solution.py:264
  343.3 20.9 %attend_back.1 = (f32[256,1536]{1,0:T(8,128)}, bf16[256,1536]{1,0:T(8,128)(2,1)}, bf16[2,96,1920]{2,1,0:T(8,128)(2,1)}, bf16[2,96,1920]{2,1,0:T(8,128)(2,1)}, bf...) custom-call(s32[2]{0:T(128)} %pad_add_fusion.at_ref, ...), custom_call_target="tpu_custom_call" | custom-call | bytes 3000000 | tf_op jit(solution)/shard_map/attend_back/pallas_call | solution.py:264
  369.6 14.2 %collective-permute-done.24.refs_0_ = bf16[2,48,1920]{2,1,0:T(8,128)(2,1)S(1)} collective-permute-done((bf16[2,48,1920]{2,1,0:T(8,128)(2,1)}, bf16[2,48,1920]{2,1,0:T(8,128)(2,1)S(1)}, u32[]{:S(2)}, u32[]{:S(2)}) %collective-permute-start.24) | collective-permute-done | bytes 368672 | tf_op jit(solution)/shard_map/attn_last/ppermute | solution.py:43
  387.0 4.0 collective-permute-start.27
  396.9 13.3 %collective-permute-done.33.refs_0_ = bf16[768,1152]{1,0:T(8,128)(2,1)} collective-permute-done((bf16[768,1152]{1,0:T(8,128)(2,1)}, bf16[768,1152]{1,0:T(8,128)(2,1)}, u32[]{:S(2)}, u32[]{:S(2)}) %collective-permute-start.33) | collective-permute-done | bytes 1769504 | tf_op jit(solution)/shard_map/expert_scatter/ppermute | solution.py:43
  410.2 4.1 fusion.refs_3_
  416.5 3.9 terms.1
  427.3 3.9 all-to-all-start.7
  431.2 7.7 %collective-permute-done.34.refs_0_ = bf16[2,96,1920]{2,1,0:T(8,128)(2,1)S(1)} collective-permute-done((bf16[2,96,1920]{2,1,0:T(8,128)(2,1)}, bf16[2,96,1920]{2,1,0:T(8,128)(2,1)S(1)}, u32[]{:S(2)}, u32[]{:S(2)}) %collective-permute-start.34) | collective-permute-done | bytes 737312 | tf_op jit(solution)/shard_map/attn_near/ppermute | solution.py:43
  447.8 5.8 %give_branch.1 = (f32[256,1536]{1,0:T(8,128)}, bf16[256,1536]{1,0:T(8,128)(2,1)}) custom-call(s32[2]{0:T(128)} %pad_add_fusion.at_ref, bf16[640,512]{1,0:T(8,128)(2,1)} %get-tuple-element.118.refs_0_, bf16[512,512]{1,0:T(8,128)(2,1)} %get-tuple-element.119.refs_1_, bf16[8,144,1536]{2,1,0:T(8,128)(2,1)} %get-tuple-element.185.refs_2_), custom_call_target="tpu_custom_call" | custom-call | bytes 3000000 | tf_op jit(solution)/shard_map/give_branch/pallas_call | solution.py:264
  453.6 19.8 %collective-permute-start.37 = (bf16[256,1536]{1,0:T(8,128)(2,1)}, bf16[256,1536]{1,0:T(8,128)(2,1)}, u32[]{:S(2)}, u32[]{:S(2)}) collective-permute-start(bf16[256,1536]{1,0:T(8,128)(2,1)} %get-tuple-element.187), channel_id=1, source_target_pairs={{0,1},{1,0},{2,3},{3,2},{4,5},{5,4},{6,7},{7,6},{8,9},{9,8},{10,11... | collective-permute-start | bytes 2359304 | tf_op jit(solution)/shard_map/ppermute | solution.py:47
  (246 shorter events, 151.1 us)
Async XLA Ops:
  3.5 33.5 %all-to-all-start = ((bf16[8,96,1152]{2,1,0:T(8,128)(2,1)}), bf16[8,96,1152]{2,1,0:T(8,128)(2,1)S(1)}, u32[]{:S(2)}, u32[]{:S(2)}) async-start(bf16[8,96,1152]{2,1,0:T(8,128)(2,1)} %pad_maximum_fusion), calls=%async_computation | async-start | bytes 3538944 | tf_op jit(solution)/shard_map/all_to_all | solution.py:828
  8.3 34.5 %collective-permute-start.1 = (bf16[256,1536]{1,0:T(8,128)(2,1)}, bf16[256,1536]{1,0:T(8,128)(2,1)}, u32[]{:S(2)}, u32[]{:S(2)}) collective-permute-start(bf16[256,1536]{1,0:T(8,128)(2,1)} %grad_out.1), channel_id=1, source_target_pairs={{0,1},{1,0},{2,3},{3,2},{4,5},{5,4},{6,7},{7,6},{8,9},{9,8},{10,11... | collective-permute-start | bytes 2359304 | tf_op jit(solution)/shard_map/ppermute | solution.py:47
  9.6 33.3 %collective-permute-start = (bf16[256,1536]{1,0:T(8,128)(2,1)S(1)}, bf16[256,1536]{1,0:T(8,128)(2,1)S(1)}, u32[]{:S(2)}, u32[]{:S(2)}) collective-permute-start(bf16[256,1536]{1,0:T(8,128)(2,1)S(1)} %copy-done.4), channel_id=1, source_target_pairs={{0,1},{1,0},{2,3},{3,2},{4,5},{5,4},{6,7},{7,6},{8,9},{9,8},{10,11... | collective-permute-start | bytes 2359304 | tf_op jit(solution)/shard_map/ppermute | solution.py:47
  14.6 26.2 %collective-permute-start.2 = (bf16[1,96,1920]{2,1,0:T(8,128)(2,1)}, bf16[1,96,1920]{2,1,0:T(8,128)(2,1)}, u32[]{:S(2)}, u32[]{:S(2)}) collective-permute-start(bf16[1,96,1920]{2,1,0:T(8,128)(2,1)} %bitcast.7), channel_id=1, source_target_pairs={{0,16},{2,18},{4,20},{6,22},{8,24},{10,26},{12,28},{14,30},{16,0},... | collective-permute-start | bytes 1105928 | tf_op jit(solution)/shard_map/ppermute | solution.py:43
  37.0 36.4 %collective-permute-start.7 = (bf16[768,1152]{1,0:T(8,128)(2,1)S(1)}, bf16[768,1152]{1,0:T(8,128)(2,1)}, u32[]{:S(2)}, u32[]{:S(2)}) collective-permute-start(bf16[768,1152]{1,0:T(8,128)(2,1)S(1)} %bitcast.37), channel_id=1, source_target_pairs={{0,1},{1,0},{2,3},{3,2},{4,5},{5,4},{6,7},{7,6},{8,9},{9,8},{10,11... | collective-permute-start | bytes 5308424 | tf_op jit(solution)/shard_map/ppermute | solution.py:47
  45.0 28.3 %collective-permute-start.5 = (bf16[2,96,1920]{2,1,0:T(8,128)(2,1)}, bf16[2,96,1920]{2,1,0:T(8,128)(2,1)}, u32[]{:S(2)}, u32[]{:S(2)}) collective-permute-start(bf16[2,96,1920]{2,1,0:T(8,128)(2,1)} %gate.23.refs_1_.refs_0_), channel_id=1, source_target_pairs={{0,8},{2,10},{4,12},{6,14},{8,0},{10,2},{12,4},{14,6},{16,24},{18,... | collective-permute-start | bytes 2211848 | tf_op jit(solution)/shard_map/weights_near/ppermute | solution.py:43
  46.0 27.3 %collective-permute-start.6 = (bf16[1,208,1152]{2,1,0:T(8,128)(2,1)}, bf16[1,208,1152]{2,1,0:T(8,128)(2,1)S(1)}, u32[]{:S(2)}, u32[]{:S(2)}) collective-permute-start(bf16[1,208,1152]{2,1,0:T(8,128)(2,1)} %bitcast.54), channel_id=1, source_target_pairs={{0,16},{2,18},{4,20},{6,22},{8,24},{10,26},{12,28},{14,30},{16,0},... | collective-permute-start | bytes 1437704 | tf_op jit(solution)/shard_map/ppermute | solution.py:43
  74.1 30.5 %collective-permute-start.8 = (bf16[2,96,1920]{2,1,0:T(8,128)(2,1)}, bf16[2,96,1920]{2,1,0:T(8,128)(2,1)S(1)}, u32[]{:S(2)}, u32[]{:S(2)}) collective-permute-start(bf16[2,96,1920]{2,1,0:T(8,128)(2,1)} %get-tuple-element.105.refs_2_), channel_id=1, source_target_pairs={{0,2},{2,0},{4,6},{6,4},{8,10},{10,8},{12,14},{14,12},{16,18},{18,... | collective-permute-start | bytes 2211848 | tf_op jit(solution)/shard_map/weights_far/ppermute | solution.py:43
  75.3 29.3 %collective-permute-start.9 = (bf16[2,96,1920]{2,1,0:T(8,128)(2,1)}, bf16[2,96,1920]{2,1,0:T(8,128)(2,1)S(1)}, u32[]{:S(2)}, u32[]{:S(2)}) collective-permute-start(bf16[2,96,1920]{2,1,0:T(8,128)(2,1)} %get-tuple-element.106.refs_4_), channel_id=1, source_target_pairs={{0,4},{2,6},{4,0},{6,2},{8,12},{10,14},{12,8},{14,10},{16,20},{18,... | collective-permute-start | bytes 2211848 | tf_op jit(solution)/shard_map/weights_far/ppermute | solution.py:43
  75.5 29.8 %collective-permute-start.10 = (bf16[2,96,1920]{2,1,0:T(8,128)(2,1)}, bf16[2,96,1920]{2,1,0:T(8,128)(2,1)}, u32[]{:S(2)}, u32[]{:S(2)}) collective-permute-start(bf16[2,96,1920]{2,1,0:T(8,128)(2,1)} %get-tuple-element.107.refs_1_), channel_id=1, source_target_pairs={{0,8},{2,10},{4,12},{6,14},{8,0},{10,2},{12,4},{14,6},{16,24},{18,... | collective-permute-start | bytes 2211848 | tf_op jit(solution)/shard_map/weights_far/ppermute | solution.py:43
  77.3 24.7 %collective-permute-start.11 = (bf16[1,208,1152]{2,1,0:T(8,128)(2,1)}, bf16[1,208,1152]{2,1,0:T(8,128)(2,1)}, u32[]{:S(2)}, u32[]{:S(2)}) collective-permute-start(bf16[1,208,1152]{2,1,0:T(8,128)(2,1)} %bitcast.53), channel_id=1, source_target_pairs={{0,16},{2,18},{4,20},{6,22},{8,24},{10,26},{12,28},{14,30},{16,0},... | collective-permute-start | bytes 1437704 | tf_op jit(solution)/shard_map/ppermute | solution.py:43
  78.5 26.1 %collective-permute-start.12 = (bf16[1,208,1152]{2,1,0:T(8,128)(2,1)S(1)}, bf16[1,208,1152]{2,1,0:T(8,128)(2,1)S(1)}, u32[]{:S(2)}, u32[]{:S(2)}) collective-permute-start(bf16[1,208,1152]{2,1,0:T(8,128)(2,1)S(1)} %copy-done.18), channel_id=1, source_target_pairs={{0,1},{1,0},{2,3},{3,2},{4,5},{5,4},{6,7},{7,6},{8,9},{9,8},{10,11... | collective-permute-start | bytes 1437704 | tf_op jit(solution)/shard_map/ppermute | solution.py:47
  126.2 54.0 %all-to-all-start.1 = ((bf16[8,144,1664]{2,1,0:T(8,128)(2,1)}), bf16[8,144,1664]{2,1,0:T(8,128)(2,1)}, u32[]{:S(2)}, u32[]{:S(2)}) async-start(bf16[8,144,1664]{2,1,0:T(8,128)(2,1)} %get-tuple-element.123), calls=%async_computation.1 | async-start | bytes 7667712 | tf_op jit(solution)/shard_map/grads_rows/all_to_all | solution.py:862
  180.3 37.3 %all-to-all-start.2 = ((bf16[8,80,1536]{2,1,0:T(8,128)(2,1)}), bf16[8,80,1536]{2,1,0:T(8,128)(2,1)S(1)}, u32[]{:S(2)}, u32[]{:S(2)}) async-start(bf16[8,80,1536]{2,1,0:T(8,128)(2,1)} %bitcast.46), calls=%async_computation.2 | async-start | bytes 3932160 | tf_op jit(solution)/shard_map/tokens_rows/all_to_all | solution.py:862
  185.8 29.9 %collective-permute-start.20 = (bf16[1,256,1152]{2,1,0:T(8,128)(2,1)}, bf16[1,256,1152]{2,1,0:T(8,128)(2,1)S(1)}, u32[]{:S(2)}, u32[]{:S(2)}) collective-permute-start(bf16[1,256,1152]{2,1,0:T(8,128)(2,1)} %bitcast.51), channel_id=1, source_target_pairs={{0,16},{2,18},{4,20},{6,22},{8,24},{10,26},{12,28},{14,30},{16,0},... | collective-permute-start | bytes 1769480 | tf_op jit(solution)/shard_map/ppermute | solution.py:43
  218.9 31.0 %all-to-all-start.3 = ((bf16[8,64,1536]{2,1,0:T(8,128)(2,1)}), bf16[8,64,1536]{2,1,0:T(8,128)(2,1)S(1)}, u32[]{:S(2)}, u32[]{:S(2)}) async-start(bf16[8,64,1536]{2,1,0:T(8,128)(2,1)} %bitcast.50), calls=%async_computation.3 | async-start | bytes 3145728 | tf_op jit(solution)/shard_map/tokens_rows/all_to_all | solution.py:862
  251.1 32.7 %all-to-all-start.5 = ((bf16[8,80,1664]{2,1,0:T(8,128)(2,1)}), bf16[8,80,1664]{2,1,0:T(8,128)(2,1)}, u32[]{:S(2)}, u32[]{:S(2)}) async-start(bf16[8,80,1664]{2,1,0:T(8,128)(2,1)} %bitcast.52), calls=%async_computation.5 | async-start | bytes 4259840 | tf_op jit(solution)/shard_map/gradn_rows/all_to_all | solution.py:862
  283.7 25.0 %all-to-all-start.4 = ((bf16[8,64,1664]{2,1,0:T(8,128)(2,1)}), bf16[8,64,1664]{2,1,0:T(8,128)(2,1)S(1)}, u32[]{:S(2)}, u32[]{:S(2)}) async-start(bf16[8,64,1664]{2,1,0:T(8,128)(2,1)} %bitcast.48), calls=%async_computation.4 | async-start | bytes 3407872 | tf_op jit(solution)/shard_map/gradn_rows/all_to_all | solution.py:862
  316.2 98.5 %all-to-all-start.6 = ((bf16[8,144,1536]{2,1,0:T(8,128)(2,1)}), bf16[8,144,1536]{2,1,0:T(8,128)(2,1)S(1)}, u32[]{:S(2)}, u32[]{:S(2)}) async-start(bf16[8,144,1536]{2,1,0:T(8,128)(2,1)} %gate.43), calls=%async_computation.6 | async-start | bytes 7077888 | tf_op jit(solution)/shard_map/branch_rows/all_to_all | solution.py:862
  331.1 79.0 %collective-permute-start.33 = (bf16[768,1152]{1,0:T(8,128)(2,1)}, bf16[768,1152]{1,0:T(8,128)(2,1)}, u32[]{:S(2)}, u32[]{:S(2)}) collective-permute-start(bf16[768,1152]{1,0:T(8,128)(2,1)} %pad_maximum_fusion.1), channel_id=1, source_target_pairs={{0,16},{2,18},{4,20},{6,22},{8,24},{10,26},{12,28},{14,30},{16,0},... | collective-permute-start | bytes 5308424 | tf_op jit(solution)/shard_map/expert_scatter/ppermute | solution.py:43
  341.1 50.7 %collective-permute-start.29 = (bf16[768,768]{1,0:T(8,128)(2,1)}, bf16[768,768]{1,0:T(8,128)(2,1)}, u32[]{:S(2)}, u32[]{:S(2)}) collective-permute-start(bf16[768,768]{1,0:T(8,128)(2,1)} %get-tuple-element.174), channel_id=1, source_target_pairs={{0,1},{1,0},{2,3},{3,2},{4,5},{5,4},{6,7},{7,6},{8,9},{9,8},{10,11... | collective-permute-start | bytes 3538952 | tf_op jit(solution)/shard_map/expert_scatter/ppermute | solution.py:47
  341.1 26.0 %collective-permute-start.30 = (bf16[768,384]{1,0:T(8,128)(2,1)}, bf16[768,384]{1,0:T(8,128)(2,1)}, u32[]{:S(2)}, u32[]{:S(2)}) collective-permute-start(bf16[768,384]{1,0:T(8,128)(2,1)} %get-tuple-element.176), channel_id=1, source_target_pairs={{0,1},{1,0},{2,3},{3,2},{4,5},{5,4},{6,7},{7,6},{8,9},{9,8},{10,11... | collective-permute-start | bytes 1769480 | tf_op jit(solution)/shard_map/expert_scatter/ppermute | solution.py:47
  364.2 19.7 %collective-permute-start.24 = (bf16[2,48,1920]{2,1,0:T(8,128)(2,1)}, bf16[2,48,1920]{2,1,0:T(8,128)(2,1)S(1)}, u32[]{:S(2)}, u32[]{:S(2)}) collective-permute-start(bf16[2,48,1920]{2,1,0:T(8,128)(2,1)} %get-tuple-element.166), channel_id=1, source_target_pairs={{0,2},{2,0},{4,6},{6,4},{8,10},{10,8},{12,14},{14,12},{16,18},{18,... | collective-permute-start | bytes 1105928 | tf_op jit(solution)/shard_map/attn_last/ppermute | solution.py:43
  364.3 19.6 %collective-permute-start.25 = (bf16[2,48,1920]{2,1,0:T(8,128)(2,1)}, bf16[2,48,1920]{2,1,0:T(8,128)(2,1)}, u32[]{:S(2)}, u32[]{:S(2)}) collective-permute-start(bf16[2,48,1920]{2,1,0:T(8,128)(2,1)} %get-tuple-element.167), channel_id=1, source_target_pairs={{0,4},{2,6},{4,0},{6,2},{8,12},{10,14},{12,8},{14,10},{16,20},{18,... | collective-permute-start | bytes 1105928 | tf_op jit(solution)/shard_map/attn_last/ppermute | solution.py:43
  387.0 27.8 %collective-permute-start.26 = (bf16[2,96,1920]{2,1,0:T(8,128)(2,1)}, bf16[2,96,1920]{2,1,0:T(8,128)(2,1)}, u32[]{:S(2)}, u32[]{:S(2)}) collective-permute-start(bf16[2,96,1920]{2,1,0:T(8,128)(2,1)} %get-tuple-element.171.refs_2_), channel_id=1, source_target_pairs={{0,8},{2,10},{4,12},{6,14},{8,0},{10,2},{12,4},{14,6},{16,24},{18,... | collective-permute-start | bytes 2211848 | tf_op jit(solution)/shard_map/attn_far/ppermute | solution.py:43
  387.0 27.8 %collective-permute-start.27 = (bf16[2,96,1920]{2,1,0:T(8,128)(2,1)}, bf16[2,96,1920]{2,1,0:T(8,128)(2,1)}, u32[]{:S(2)}, u32[]{:S(2)}) collective-permute-start(bf16[2,96,1920]{2,1,0:T(8,128)(2,1)} %get-tuple-element.172), channel_id=1, source_target_pairs={{0,2},{2,0},{4,6},{6,4},{8,10},{10,8},{12,14},{14,12},{16,18},{18,... | collective-permute-start | bytes 2211848 | tf_op jit(solution)/shard_map/attn_far/ppermute | solution.py:43
  390.9 23.8 %collective-permute-start.28 = (bf16[2,96,1920]{2,1,0:T(8,128)(2,1)}, bf16[2,96,1920]{2,1,0:T(8,128)(2,1)}, u32[]{:S(2)}, u32[]{:S(2)}) collective-permute-start(bf16[2,96,1920]{2,1,0:T(8,128)(2,1)} %get-tuple-element.173.refs_1_), channel_id=1, source_target_pairs={{0,4},{2,6},{4,0},{6,2},{8,12},{10,14},{12,8},{14,10},{16,20},{18,... | collective-permute-start | bytes 2211848 | tf_op jit(solution)/shard_map/attn_far/ppermute | solution.py:43
  395.4 30.3 %collective-permute-start.38 = (bf16[256,1536]{1,0:T(8,128)(2,1)}, bf16[256,1536]{1,0:T(8,128)(2,1)}, u32[]{:S(2)}, u32[]{:S(2)}) collective-permute-start(bf16[256,1536]{1,0:T(8,128)(2,1)} %get-tuple-element.190), channel_id=1, source_target_pairs={{0,1},{1,0},{2,3},{3,2},{4,5},{5,4},{6,7},{7,6},{8,9},{9,8},{10,11... | collective-permute-start | bytes 2359304 | tf_op jit(solution)/shard_map/ppermute | solution.py:47
  420.4 18.6 %collective-permute-start.34 = (bf16[2,96,1920]{2,1,0:T(8,128)(2,1)}, bf16[2,96,1920]{2,1,0:T(8,128)(2,1)S(1)}, u32[]{:S(2)}, u32[]{:S(2)}) collective-permute-start(bf16[2,96,1920]{2,1,0:T(8,128)(2,1)} %get-tuple-element.181), channel_id=1, source_target_pairs={{0,2},{2,0},{4,6},{6,4},{8,10},{10,8},{12,14},{14,12},{16,18},{18,... | collective-permute-start | bytes 2211848 | tf_op jit(solution)/shard_map/attn_near/ppermute | solution.py:43
  427.3 55.3 %all-to-all-start.7 = ((bf16[8,96,1152]{2,1,0:T(8,128)(2,1)}), bf16[8,96,1152]{2,1,0:T(8,128)(2,1)S(1)}, u32[]{:S(2)}, u32[]{:S(2)}) async-start(bf16[8,96,1152]{2,1,0:T(8,128)(2,1)} %bitcast.47), calls=%async_computation.7 | async-start | bytes 3538944 | tf_op jit(solution)/shard_map/expert_scatter/all_to_all | solution.py:862
  444.9 28.5 %collective-permute-start.39 = (bf16[1,96,1920]{2,1,0:T(8,128)(2,1)}, bf16[1,96,1920]{2,1,0:T(8,128)(2,1)S(1)}, u32[]{:S(2)}, u32[]{:S(2)}) collective-permute-start(bf16[1,96,1920]{2,1,0:T(8,128)(2,1)} %slice.108), channel_id=1, source_target_pairs={{0,16},{2,18},{4,20},{6,22},{8,24},{10,26},{12,28},{14,30},{16,0},... | collective-permute-start | bytes 1105928 | tf_op jit(solution)/shard_map/attn_outer/ppermute | solution.py:43
  453.6 25.9 %collective-permute-start.37 = (bf16[256,1536]{1,0:T(8,128)(2,1)}, bf16[256,1536]{1,0:T(8,128)(2,1)}, u32[]{:S(2)}, u32[]{:S(2)}) collective-permute-start(bf16[256,1536]{1,0:T(8,128)(2,1)} %get-tuple-element.187), channel_id=1, source_target_pairs={{0,1},{1,0},{2,3},{3,2},{4,5},{5,4},{6,7},{7,6},{8,9},{9,8},{10,11... | collective-permute-start | bytes 2359304 | tf_op jit(solution)/shard_map/ppermute | solution.py:47
  (60 other events, 447.5 us)

commit v3 on v2

--- a/solution.py
+++ b/solution.py
@@ -13,6 +13,8 @@
 GAIN_A, GAIN_F = 8, 9
 CUBE = 8
 BRIEF = pl.CostEstimate(flops=0, bytes_accessed=3_000_000, transcendentals=0)
+LIGHT = ("attend", "middle", "take", "give_gradn", "middle_back", "attend_back")
+FREE = pl.CostEstimate(flops=0, bytes_accessed=0, transcendentals=0)
 epsilon = 1e-06
 highest = lax.Precision.HIGHEST
 f32 = jnp.float32
@@ -75,7 +77,7 @@
     return lax.slice_in_dim(values, span[0], span[1], axis=axis)
 
 
-NEAR, FAR, LAST = (1, 2, 4), (3, 6, 5), (7, 8)
+NEAR, FAR, LAST = (1, 2, 4), (3, 9, 6, 5), (7, 8)
 
 
 def add_round(left, right):
@@ -94,14 +96,13 @@
 def patch(first, second, low, high):
     shape = first.shape
     half = low.shape
-    if half[-2] % 16:
+    if half[1] % 16:
         return (
-            jnp.concatenate([add_round(first[..., : half[-2], :], low), first[..., half[-2] :, :]], -2),
-            jnp.concatenate([second[..., : half[-2], :], add_round(second[..., half[-2] :, :], high)], -2),
+            jnp.concatenate([add_round(first[: half[0]], low), first[half[0] :]], axis=0),
+            jnp.concatenate([second[: half[0]], add_round(second[half[0] :], high)], axis=0),
         )
-    lead = (0,) * (len(shape) - 2)
-    top = pl.BlockSpec(half, lambda i: lead + (0, 0))
-    bottom = pl.BlockSpec(half, lambda i: lead + (1, 0))
+    top = pl.BlockSpec(half, lambda i: (0, 0, 0))
+    bottom = pl.BlockSpec(half, lambda i: (1, 0, 0))
     return pl.pallas_call(
         patch_kernel,
         grid=(1,),
@@ -110,7 +111,7 @@
         out_specs=[top, bottom],
         input_output_aliases={0: 0, 1: 1},
         compiler_params=pltpu.CompilerParams(vmem_limit_bytes=60 * 1024 * 1024),
-        cost_estimate=BRIEF,
+        cost_estimate=FREE,
         name="patch",
     )(first, second, low, high)
 
@@ -143,7 +144,7 @@
         in_specs=[spec] * 6,
         out_specs=[spec] * 3,
         compiler_params=pltpu.CompilerParams(vmem_limit_bytes=60 * 1024 * 1024),
-        cost_estimate=BRIEF,
+        cost_estimate=FREE,
         name="terms",
     )(*args)
     return dict(zip(NEAR, outs))
@@ -179,26 +180,26 @@
 
 
 def piece_copies(got, block, me, count):
-    if block % 32:
-        stacked = jnp.stack(
-            [got[b] for b in range(7)] + [jnp.concatenate([got[b] for b in LAST], axis=1)],
-            axis=1,
-        )
+    outer = got[0].shape[0]
+    if block % 16:
+        wholes = got | {3: jnp.concatenate([got[3], got[9]]), 7: jnp.concatenate([got[7], got[8]])}
+        stacked = jnp.stack([wholes[b] for b in range(CUBE)], axis=1)
         whole = stacked.reshape(count, block, -1)[jnp.arange(count) ^ me]
-        return [whole.reshape(1, count * block, -1)], [(0, 0, 0, count * block, None, block)]
+        return [whole.reshape(1, count * block, -1)], [(0, 0, count * block, None, block)]
     sources, copies = [], []
-    spans = [(0, block)] * 7 + list(halves(block))
-    for b, span in enumerate(spans):
+    for b in range(CUBE + 2):
+        first = outer // 2 if b >= 8 else 0
+        offset = {8: 7, 9: 3}.get(b, b)
         for j in range(got[b].shape[0]):
-            copies.append((b, j, span[0], span[1] - span[0], 8 * j + min(b, 7), block))
+            copies.append((b, j, block, 8 * (first + j) + offset, block))
         sources.append(got[b])
     return sources, copies
 
 
 def lay_rows(copies, sources, targets, sems, me):
     started = []
-    for number, (source, entry, start, rows, offset, block) in enumerate(copies):
-        row = 0 if offset is None else pl.multiple_of((me ^ offset) * block + start, 16)
+    for number, (source, entry, rows, offset, block) in enumerate(copies):
+        row = 0 if offset is None else pl.multiple_of((me ^ offset) * block, 16)
         column = 0
         for k, target in enumerate(targets):
             cols = target.shape[1]
@@ -214,16 +215,17 @@
         copy.wait()
 
 
-def part_order(block):
-    return [(b, (0, block)) for b in range(7)] + [(7, span) for span in halves(block)]
+def part_order(count):
+    outer = count // CUBE
+    return [(b, (0, outer)) for b in range(7)] + [(7, span) for span in halves(outer)]
 
 
 def part_shapes(count, block, width):
-    if block % 32:
+    if block % 16:
         return [jax.ShapeDtypeStruct((count * block, width), bf16)]
     return [
-        jax.ShapeDtypeStruct((count // CUBE, span[1] - span[0], width), bf16)
-        for _, span in part_order(block)
+        jax.ShapeDtypeStruct((span[1] - span[0], block, width), bf16)
+        for _, span in part_order(count)
     ]
 
 
@@ -232,21 +234,19 @@
     if len(parts) == 1:
         parts[0][:, cols] = whole[...].astype(bf16)
         return
-    for part, (offset, span) in zip(parts, part_order(block)):
+    for part, (offset, span) in zip(parts, part_order(whole.shape[0] // block)):
         for j in range(part.shape[0]):
-            row = pl.multiple_of((me ^ (8 * j + offset)) * block + span[0], 16)
-            part[j, :, cols] = whole[pl.ds(row, span[1] - span[0])].astype(bf16)
+            row = pl.multiple_of((me ^ (8 * (span[0] + j) + offset)) * block, 16)
+            part[j, :, cols] = whole[pl.ds(row, block)].astype(bf16)
 
 
 def spread_parts(parts, me, count):
     if len(parts) > 1:
         return dict(enumerate(parts))
-    block = parts[0].shape[0] // count
-    outer = jnp.arange(count // CUBE) * CUBE
-    blocks = parts[0].reshape(count, block, -1)
+    blocks = parts[0].reshape(count, parts[0].shape[0] // count, -1)
     return {
-        k: cut(blocks[(offset + outer) ^ me], span, 1)
-        for k, (offset, span) in enumerate(part_order(block))
+        k: blocks[(offset + CUBE * jnp.arange(*span)) ^ me]
+        for k, (offset, span) in enumerate(part_order(count))
     }
 
 
@@ -268,7 +268,7 @@
         out_specs=[pl.BlockSpec(memory_space=pltpu.VMEM)] * len(out_shapes),
         scratch_shapes=scratch,
         compiler_params=pltpu.CompilerParams(vmem_limit_bytes=60 * 1024 * 1024),
-        cost_estimate=BRIEF,
+        cost_estimate=FREE if name in LIGHT else BRIEF,
         name=name,
     )(*[a for a, _ in args])
 
@@ -707,13 +707,12 @@
     )(at, router, *args)
 
 
-def weight_grads_kernel(calls, pre, down, at_ref, *refs):
-    kinds = int(pre) + int(down)
+def weight_grads_kernel(calls, at_ref, *refs):
     pairs = []
-    for _ in range(kinds):
+    for _ in range(2):
         pairs.append((refs[:calls], refs[calls : 2 * calls]))
         refs = refs[2 * calls :]
-    outs, buffers, sems = refs[: 2 * kinds], refs[2 * kinds : -1], refs[-1]
+    own, other, *buffers, sems = refs
     cols = buffers[0].shape[1]
     columns = pl.ds(pl.multiple_of(at_ref[2] * cols, cols), cols)
     copies = []
@@ -728,7 +727,8 @@
                 copies.append(pltpu.make_async_copy(source, target, sems.at[len(copies)]))
                 copies[-1].start()
             row += left.shape[0]
-    for number in range(kinds):
+    at = 0
+    for number in range(2):
         for copy in copies[2 * calls * number : 2 * calls * (number + 1)]:
             copy.wait()
         total = lax.dot_general(
@@ -736,32 +736,31 @@
             buffers[2 * number + 1][...],
             TN,
             preferred_element_type=f32,
-        )
-        width = total.shape[1]
-        outs[2 * number][...] = total[:, : width // 2]
-        outs[2 * number + 1][...] = total[:, width // 2 :].astype(bf16)
+        ).astype(bf16)
+        width = total.shape[1] // 2
+        own[:, at : at + width] = total[:, :width]
+        other[:, at : at + width] = total[:, width:]
+        at += width
 
 
 def weight_grads(at, half, pre, down):
-    args, outs, scratch = [], [], []
+    args, scratch, width = [], [], 0
     for pairs in (pre, down):
-        if not pairs:
-            continue
         args += [p[0] for p in pairs] + [p[1] for p in pairs]
         rows = sum(p[0].shape[0] for p in pairs)
         left, right = pairs[0][0].shape[1] // 2, pairs[0][1].shape[1]
-        outs += [((left, right // 2), f32), ((left, right // 2), bf16)]
         scratch += [(rows, left), (rows, right)]
+        width += right // 2
     return pl.pallas_call(
-        functools.partial(weight_grads_kernel, len(pre or down), bool(pre), bool(down)),
-        out_shape=[jax.ShapeDtypeStruct(dims, kind) for dims, kind in outs],
+        functools.partial(weight_grads_kernel, len(pre)),
+        out_shape=[jax.ShapeDtypeStruct((left, width), bf16)] * 2,
         in_specs=[pl.BlockSpec(memory_space=pltpu.SMEM)]
         + [pl.BlockSpec(memory_space=pl.ANY)] * len(args),
-        out_specs=[pl.BlockSpec(memory_space=pltpu.VMEM)] * len(outs),
+        out_specs=[pl.BlockSpec(memory_space=pltpu.VMEM)] * 2,
         scratch_shapes=[pltpu.VMEM(dims, bf16) for dims in scratch]
         + [pltpu.SemaphoreType.DMA((len(args),))],
         compiler_params=pltpu.CompilerParams(vmem_limit_bytes=60 * 1024 * 1024),
-        cost_estimate=BRIEF,
+        cost_estimate=FREE,
         name="weight_grads",
     )(jnp.concatenate([at, half.reshape(1)]), *args)
 
@@ -804,17 +803,19 @@
         return {0: own} | {bit: swap(own, bit, count) for bit in NEAR}
 
     def far(got):
+        spans = halves(got[0].shape[0])
         return got | {
-            3: swap(got[2], 1, count),
+            3: swap(cut(got[2], spans[0], 0), 1, count),
+            9: swap(cut(got[1], spans[1], 0), 2, count),
             6: swap(got[4], 2, count),
-            5: swap(got[1], 4, count),
+            5: swap(got[4], 1, count),
         }
 
-    def last(got, axis):
-        spans = halves(got[0].shape[axis])
+    def last(got):
+        spans = halves(got[0].shape[0])
         return got | {
-            7: swap(cut(got[6], spans[0], axis), 1, count),
-            8: swap(cut(got[5], spans[1], axis), 2, count),
+            7: swap(cut(got[6], spans[0], 0), 1, count),
+            8: swap(cut(got[5], spans[1], 0), 2, count),
         }
 
     small = jnp.concatenate([w_router, gain_attn[:, None], gain_ffn[:, None]], axis=1)
@@ -845,7 +846,7 @@
     code = (order < seq_len * top_count).astype(bf16)
     code = jnp.pad(code, ((0, 0), (0, EXTRA - experts)))
     code_own = lax.dynamic_slice_in_dim(code, core * tok_rows, tok_rows, 0)
-    first_part = (capacity // 4 + 15) // 16 * 16
+    first_part = capacity // 4 // 16 * 16
     slot_parts = (first_part, capacity // 2 - first_part)
     grad_other = swap_core(grad_out)
     slots = vmem_call(
@@ -866,11 +867,11 @@
     sine_table = jnp.concatenate([-sine_table, sine_table], axis=1)
     seg_col, seg_row = segment_ids[:, None], segment_ids[None, :]
 
-    (pair,) = gate([pair], cosine, sine_table, hidden_other, grad_other)
+    pair, expert_rows = gate([pair, expert_rows], cosine, sine_table, hidden_other, grad_other)
     if count == 2 * CUBE:
-        edges = [expert_rows.shape[0] * k // 48 // 16 * 16 for k in (0, 13, 26, 32, 48)]
+        edges = [expert_rows.shape[0] * k // 48 // 16 * 16 for k in (0, 10, 25, 31, 44, 48)]
     else:
-        edges = [0] * 4 + [expert_rows.shape[0]]
+        edges = [0] * 5 + [expert_rows.shape[0]]
     pieces = [(expert_rows[None], 0, 0, 0), (swap_core(expert_rows)[None], 0, 0, 1)]
 
     def outer_chunk(k, *events):
@@ -895,7 +896,7 @@
     arrays, swapped_next = outer_chunk(1, got[1])
     got = gate_dict(got, FAR, arrays, swapped)
     with jax.named_scope("weights_last"):
-        got = last(got, 1)
+        got = last(got)
     arrays, swapped = outer_chunk(2, got[3])
     got = gate_dict(got, LAST, arrays, swapped_next)
     sources, copies = piece_copies(got, block, me, count)
@@ -928,6 +929,7 @@
     )
     hid, normed, qs, ks, vs, mixed, lse, full_qkv, router, out_wt, gains = attended[:-2]
     attn_own, attn_other = attended[-2:]
+    arrays, swapped_next = outer_chunk(3, got[7])
     middle, normed2 = vmem_call(
         middle_kernel,
         [shape(tok_rows, width, f32), shape(tok_rows, width)],
@@ -944,11 +946,11 @@
         "take",
     )
     rows = list(rows)
-    rows[0], grad_rows = gate([rows[0], grad_rows], swapped)
+    rows[0], grad_rows = gate([rows[0], grad_rows], arrays, swapped)
     with jax.named_scope("tokens_rows"):
         x_first = exchange(rows[0])
-    arrays, _ = outer_chunk(3, rows[0])
-    x_first, rows_second = gate([x_first, rows[1]], arrays)
+    arrays, _ = outer_chunk(4, rows[0])
+    x_first, rows_second = gate([x_first, rows[1]], arrays, swapped_next)
     with jax.named_scope("tokens_rows"):
         x_second = exchange(rows_second)
 
@@ -968,27 +970,16 @@
     bits = outer_bits(count)
     top = (me // bits[-1]) % 2 if bits else jnp.zeros((), jnp.int32)
 
-    def part_grads(half, pre, down, event):
-        half = gate([half.reshape(1)], event)[0]
-        outs = weight_grads(at, half, pre, down)
-        return [(outs[i], outs[i + 1]) for i in range(0, len(outs), 2)]
-
-    def both_cores(pair):
-        return pair[0] + swap_core(pair[1]).astype(f32)
-
-    (send_down,) = part_grads(1 - top, [], down_pairs, second[0])
-    (gradn_second,) = gate([gradn_second], send_down)
-    event = gradn_second
+    def half_grads(half, *events):
+        half = gate([half.reshape(1)], *events)[0]
+        return weight_grads(at, half, pre_pairs, down_pairs)
+
     with jax.named_scope("gradn_rows"):
         gradn_second = exchange(gradn_second)
+    sent, sent_other = half_grads(1 - top, second[0])
+    keep, keep_other = half_grads(top, sent_other)
     with jax.named_scope("expert_scatter"):
-        down_part = both_cores(send_down).astype(bf16)
-    (send_pre,) = part_grads(1 - top, pre_pairs, [], event)
-    keep_pre, keep_down = part_grads(top, pre_pairs, down_pairs, send_pre)
-    with jax.named_scope("expert_scatter"):
-        send_pre = both_cores(send_pre).astype(bf16)
-
-        sent = jnp.concatenate([send_pre, down_part], axis=1)
+        sent = add_round(sent, swap_core(sent_other))
         sent_got = swap(sent, bits[-1], count) if bits else sent
 
     def give(picks, values, name):
@@ -1001,7 +992,7 @@
         )
         return own, swap_core(other)
 
-    gradn_second, gradn_first = gate([gradn_second, gradn_first], keep_pre[0])
+    gradn_second, gradn_first = gate([gradn_second, gradn_first], sent, keep)
     gradn = list(give(picks, (gradn_first, gradn_second), "give_gradn"))
 
     grad_middle, grad_mid_r, small_f = vmem_call(
@@ -1014,7 +1005,7 @@
     )
 
     grad_mid_other = swap_core(grad_mid_r)
-    (branch,) = gate([branch], gradn[0])
+    (branch,) = gate([branch], gradn_second)
     with jax.named_scope("branch_rows"):
         branch = exchange(branch)
     normed_own, normed_other, *parts = vmem_call(
@@ -1040,16 +1031,19 @@
     parts = gate_dict(parts, (3,) + LAST)
     with jax.named_scope("attn_last"):
         got = sum_last(parts, count)
-    grad_normed = normed_own + swap_core(normed_other).astype(f32)
-    gated = gate([got[7], got[8], parts[3]])
+    normed_swapped = swap_core(normed_other)
+    gated = gate([got[7], got[8], parts[3]], normed_swapped)
     got, parts[3] = dict(zip(LAST, gated)), gated[2]
     with jax.named_scope("attn_far"):
         terms = far_terms(parts, got)
         attn_far = sum_far(parts, terms, count)
     with jax.named_scope("expert_scatter"):
-        (sent_got,) = gate([sent_got], terms)
-        keep = jnp.concatenate([both_cores(keep_pre), both_cores(keep_down)], axis=1)
-        total = keep + sent_got.astype(f32) if bits else jnp.concatenate([keep, sent_got], axis=0)
+        sent_got, keep = gate([sent_got, keep], terms)
+        keep_swapped = swap_core(keep_other)
+        if bits:
+            total = keep.astype(f32) + keep_swapped.astype(f32) + sent_got.astype(f32)
+        else:
+            total = jnp.concatenate([add_round(keep, keep_swapped), sent_got]).astype(f32)
         for bit in reversed(bits[:-1]):
             half = total.shape[0] // 2
             high = (me // bit) % 2
@@ -1057,17 +1051,17 @@
             other = lax.dynamic_slice_in_dim(total, (1 - high) * half, half, 0)
             total = mine + swap(other.astype(bf16), bit, count).astype(f32)
         total = total.astype(bf16)
-    gated = gate([attn_far[k] for k in NEAR] + [total, branch])
-    attn_far, total, branch = dict(zip(NEAR, gated)), gated[3], gated[4]
+    grad_normed = normed_own + normed_swapped.astype(f32)
+    gated = gate([attn_far[k] for k in NEAR] + [branch, total])
+    attn_far, branch, total = dict(zip(NEAR, gated)), gated[3], gated[4]
     with jax.named_scope("attn_near"):
         attn_near = sum_near(near_terms(parts, attn_far), count)
+    branch_own, branch_other = give(picks, (branch,), "give_branch")
     with jax.named_scope("expert_scatter"):
         total = exchange(total)
-    gated = gate([attn_near[k] for k in NEAR] + [branch])
-    attn_near, branch = dict(zip(NEAR, gated)), gated[3]
+    attn_near = gate_dict(attn_near, NEAR, branch_own)
     with jax.named_scope("attn_outer"):
         attn_grads = outer_sum(sum_own(parts, attn_near), count)
-    branch_own, branch_other = give(picks, (branch,), "give_branch")
     layer_out = middle + branch_own + branch_other.astype(f32)
 
     expert_grads = total.reshape(experts, block, 3 * hidden).astype(f32)

time: 493 us -> 482 us (0.978)
  other arithmetic: 39.2 us -> 31.1 us
  waiting for transfers between devices: 163 us -> 168 us
    ppermute x23 -> x25, waiting for transfers between devices: 114 us -> 158 us  [swap(): return lax.ppermute(values, 'dp', [(i, i ^ bit) for i in range(count)])]
    all_to_all x7, waiting for transfers between devices: 21.4 us -> 4.43 us  [exchange(): lax.all_to_all(rows, 'dp', 0, 0, tiled=True, axis_index_groups=groups)]
    all_to_all x1, waiting for transfers between devices: 16.8 us -> 0.01 us  [per_device(): lax.all_to_all(expert_shard.reshape(experts * block, 3 * hidden), 'dp', 0...]
    ppermute x18 -> x17, starting transfers between devices: 41.3 us -> 25.8 us  [swap_core(): return lax.ppermute(values, 'tensor', [(0, 1), (1, 0)])]
    ppermute x23 -> x25, starting transfers between devices: 27.8 us -> 35.8 us  [swap(): return lax.ppermute(values, 'dp', [(i, i ^ bit) for i in range(count)])]
    add x2 -> x0, other arithmetic: 6.17 us -> none  [both_cores(): return pair[0] + swap_core(pair[1]).astype(f32)]
    ppermute x18 -> x17, waiting for transfers between devices: 11.4 us -> 5.44 us  [swap_core(): return lax.ppermute(values, 'tensor', [(0, 1), (1, 0)])]
    pallas_call x3 -> x2, Pallas kernels: 23.2 us -> 21.2 us  [weight_grads(): pl.pallas_call(functools.partial(weight_grads_kernel, len(pre)), out_shap...]
  transfers between devices with their start and end apart: 49 -> 50, of which waited for: 20 -> 18; matrix products, arithmetic and copies ran while one was open for 12% -> 10% of each run, Pallas kernels for 27% -> 28%
where the time goes in v3:
time: 482 us; the launch traced here: 475 us
  waiting for transfers between devices  168 us (35%)
  Pallas kernels  136 us (28%)
  starting transfers between devices  101 us (21%)
  local copies, waits for them, and re-layouts  37.5 us (8%)
  other arithmetic  31.1 us (6%)
    ppermute x25, waiting for transfers between devices, swap(): return lax.ppermute(values, 'dp', [(i, i ^ bit) for i in range(count)])  158 us
    pallas_call x8, Pallas kernels, vmem_call(): pl.pallas_call(kernel, out_shape=out_shapes, in_specs=[pl.BlockSpec(memor...  68.6 us
    pallas_call x2, Pallas kernels, moe(): pl.pallas_call(functools.partial(moe_kernel, (copies, hidden, blocks, out...  38.9 us
    ppermute x25, starting transfers between devices, swap(): return lax.ppermute(values, 'dp', [(i, i ^ bit) for i in range(count)])  35.8 us
    all_to_all x7, starting transfers between devices, exchange(): lax.all_to_all(rows, 'dp', 0, 0, tiled=True, axis_index_groups=groups)  34.6 us
    ppermute x17, starting transfers between devices, swap_core(): return lax.ppermute(values, 'tensor', [(0, 1), (1, 0)])  25.8 us
    pallas_call x2, Pallas kernels, weight_grads(): pl.pallas_call(functools.partial(weight_grads_kernel, len(pre)), out_shap...  21.2 us
    unnamed x97, local copies, waits for them, and re-layouts  19.1 us
  transfers between devices with their start and end apart: 50, of which 18 were waited for; matrix products, arithmetic and copies ran while one was open for 10% of the time, Pallas kernels for 28%

profile of v3, /device:TPU:3, one launch (start us, length us, event | category | flops | bytes accessed | tf_op | source)
XLA Modules:
  0.0 474.7 jit_solution(8202611092688773080)
XLA Ops:
  3.5 4.8 %all-to-all-start = ((bf16[8,96,1152]{2,1,0:T(8,128)(2,1)}), bf16[8,96,1152]{2,1,0:T(8,128)(2,1)S(1)}, u32[]{:S(2)}, u32[]{:S(2)}) async-start(bf16[8,96,1152]{2,1,0:T(8,128)(2,1)} %pad_maximum_fusion), calls=%async_computation | async-start | bytes 3538944 | tf_op jit(solution)/shard_map/all_to_all | solution.py:829
  15.9 20.2 %collective-permute-done.2 = bf16[1,96,1920]{2,1,0:T(8,128)(2,1)S(1)} collective-permute-done((bf16[1,96,1920]{2,1,0:T(8,128)(2,1)S(1)}, bf16[1,96,1920]{2,1,0:T(8,128)(2,1)S(1)}, u32[]{:S(2)}, u32[]{:S(2)}) %collective-permute-start.2) | collective-permute-done | bytes 368672 | tf_op jit(solution)/shard_map/ppermute | solution.py:45
  41.7 4.3 collective-permute-start.5
  50.8 6.7 %slots.1 = (bf16[512,512]{1,0:T(8,128)(2,1)}, bf16[640,512]{1,0:T(8,128)(2,1)}, bf16[8,144,1664]{2,1,0:T(8,128)(2,1)}) custom-call(s32[2]{0:T(128)} %pad_add_fusion.at_ref, s32[512,8]{1,0:T(8,128)} %copy-done.25, s32[8,512]{1,0:T(8,128)} %bitcast.61, bf16[256,1536]{1,0:T(8,128)(2,1)} %grad_out.1, bf16[256,1536]{1,0:T(8,128)(2,1)} %collective-permute-done.1.other.refs_5_, ...), custom_call_target="tpu_custom_call" | custom-call | bytes 3000000 | tf_op jit(solution)/shard_map/slots/pallas_call | solution.py:264
  57.6 12.1 %collective-permute-done.6.refs_4_.refs_2_.refs_3_ = bf16[1,160,1152]{2,1,0:T(8,128)(2,1)} collective-permute-done((bf16[1,160,1152]{2,1,0:T(8,128)(2,1)}, bf16[1,160,1152]{2,1,0:T(8,128)(2,1)}, u32[]{:S(2)}, u32[]{:S(2)}) %collective-permute-start.6) | collective-permute-done | bytes 368672 | tf_op jit(solution)/shard_map/ppermute | solution.py:45
  80.9 22.4 %collective-permute-done.12.refs_4_.refs_5_ = bf16[1,240,1152]{2,1,0:T(8,128)(2,1)S(1)} collective-permute-done((bf16[1,240,1152]{2,1,0:T(8,128)(2,1)}, bf16[1,240,1152]{2,1,0:T(8,128)(2,1)S(1)}, u32[]{:S(2)}, u32[]{:S(2)}) %collective-permute-start.12) | collective-permute-done | bytes 552992 | tf_op jit(solution)/shard_map/ppermute | solution.py:45
  111.2 10.0 %collective-permute-done.16.refs_2_.refs_6_.refs_7_ = bf16[1,96,1152]{2,1,0:T(8,128)(2,1)S(1)} collective-permute-done((bf16[1,96,1152]{2,1,0:T(8,128)(2,1)}, bf16[1,96,1152]{2,1,0:T(8,128)(2,1)S(1)}, u32[]{:S(2)}, u32[]{:S(2)}) %collective-permute-start.16) | collective-permute-done | bytes 221216 | tf_op jit(solution)/shard_map/ppermute | solution.py:45
  122.8 5.8 %all-to-all-start.1 = ((bf16[8,144,1664]{2,1,0:T(8,128)(2,1)}), bf16[8,144,1664]{2,1,0:T(8,128)(2,1)}, u32[]{:S(2)}, u32[]{:S(2)}) async-start(bf16[8,144,1664]{2,1,0:T(8,128)(2,1)} %get-tuple-element.126), calls=%async_computation.1 | async-start | bytes 7667712 | tf_op jit(solution)/shard_map/grads_rows/all_to_all | solution.py:863
  128.5 13.7 %attend.1 = (bf16[512,1536]{1,0:T(8,128)(2,1)}, bf16[512,1536]{1,0:T(8,128)(2,1)}, bf16[512,768]{1,0:T(8,128)(2,1)}, bf16[512,128]{1,0:T(8,128)(2,1)}, bf16[512,...) custom-call(s32[2]{0:T(128)} %pad_add_fusion.at_ref, ...), custom_call_target="tpu_custom_call" | custom-call | tf_op jit(solution)/shard_map/attend/pallas_call | solution.py:264
  153.1 5.1 %take.1 = (bf16[512,1536]{1,0:T(8,128)(2,1)}, bf16[640,1536]{1,0:T(8,128)(2,1)}) custom-call(s32[2]{0:T(128)} %pad_add_fusion.at_ref, bf16[256,1536]{1,0:T(8,128)(2,1)} %get-tuple-element.123.own.normed, bf16[256,1536]{1,0:T(8,128)(2,1)} %copy-done.32, bf16[512,512]{1,0:T(8,128)(2,1)} %get-tuple-element.121.refs_0_, bf16[640,512]{1,0:T(8,128)(2,1)} %get-tuple-element.122.refs_1_), custom_call_target="tpu_custom_call" | custom-call | tf_op jit(solution)/shard_map/take/pallas_call | solution.py:264
  158.2 27.3 %collective-permute-done.20.refs_2_.refs_8_.refs_9_ = bf16[1,208,1152]{2,1,0:T(8,128)(2,1)S(1)} collective-permute-done((bf16[1,208,1152]{2,1,0:T(8,128)(2,1)}, bf16[1,208,1152]{2,1,0:T(8,128)(2,1)S(1)}, u32[]{:S(2)}, u32[]{:S(2)}) %collective-permute-start.20) | collective-permute-done | bytes 479264 | tf_op jit(solution)/shard_map/ppermute | solution.py:45
  196.5 13.6 %collective-permute-done.22.refs_2_.refs_10_.refs_11_ = bf16[1,64,1152]{2,1,0:T(8,128)(2,1)S(1)} collective-permute-done((bf16[1,64,1152]{2,1,0:T(8,128)(2,1)}, bf16[1,64,1152]{2,1,0:T(8,128)(2,1)S(1)}, u32[]{:S(2)}, u32[]{:S(2)}) %collective-permute-start.22) | collective-permute-done | bytes 147488 | tf_op jit(solution)/shard_map/ppermute | solution.py:45
  213.0 5.3 %all-to-all-start.3 = ((bf16[8,80,1536]{2,1,0:T(8,128)(2,1)}), bf16[8,80,1536]{2,1,0:T(8,128)(2,1)S(1)}, u32[]{:S(2)}, u32[]{:S(2)}) async-start(bf16[8,80,1536]{2,1,0:T(8,128)(2,1)} %bitcast.49), calls=%async_computation.3 | async-start | bytes 3932160 | tf_op jit(solution)/shard_map/tokens_rows/all_to_all | solution.py:863
  223.5 17.9 %experts.2 = (bf16[8,144,1536]{2,1,0:T(8,128)(2,1)}, bf16[512,1664]{1,0:T(8,128)(2,1)}, bf16[512,768]{1,0:T(8,128)(2,1)}, bf16[512,1536]{1,0:T(8,128)(2,1)}, bf16[512,1536]{1,0:T(8,128)(2,1)}) custom-call(s32[2]{0:T(128)} %pad_add_fusion.at_ref, bf16[1536,128]{1,0:T(8,128)(2,1)} %get-tuple-element.124.router_ref.router, ...), custom_call_target="tpu_custom_call" | custom-call | bytes 3000000 | tf_op jit(solution)/shard_map/experts/pallas_call | solution.py:685
  243.2 5.4 %all-to-all-start.5 = ((bf16[8,64,1664]{2,1,0:T(8,128)(2,1)}), bf16[8,64,1664]{2,1,0:T(8,128)(2,1)}, u32[]{:S(2)}, u32[]{:S(2)}) async-start(bf16[8,64,1664]{2,1,0:T(8,128)(2,1)} %bitcast.53), calls=%async_computation.5 | async-start | bytes 3407872 | tf_op jit(solution)/shard_map/gradn_rows/all_to_all | solution.py:863
  249.4 21.0 %experts.3 = (bf16[8,144,1536]{2,1,0:T(8,128)(2,1)}, bf16[640,1664]{1,0:T(8,128)(2,1)}, bf16[640,768]{1,0:T(8,128)(2,1)}, bf16[640,1536]{1,0:T(8,128)(2,1)}, bf16[640,1536]{1,0:T(8,128)(2,1)}) custom-call(s32[2]{0:T(128)} %pad_add_fusion.at_ref, bf16[1536,128]{1,0:T(8,128)(2,1)} %gate.34.router_ref, ...), custom_call_target="tpu_custom_call", output_to_operand_aliasing={{0}: (4, {})} | custom-call | bytes 3000000 | tf_op jit(solution)/shard_map/experts/pallas_call | solution.py:685
  270.4 4.8 %all-to-all-start.4 = ((bf16[8,80,1664]{2,1,0:T(8,128)(2,1)}), bf16[8,80,1664]{2,1,0:T(8,128)(2,1)S(1)}, u32[]{:S(2)}, u32[]{:S(2)}) async-start(bf16[8,80,1664]{2,1,0:T(8,128)(2,1)} %bitcast.51), calls=%async_computation.4 | async-start | bytes 4259840 | tf_op jit(solution)/shard_map/gradn_rows/all_to_all | solution.py:863
  277.1 10.6 %weight_grads.2 = (bf16[768,1152]{1,0:T(8,128)(2,1)}, bf16[768,1152]{1,0:T(8,128)(2,1)}) custom-call(s32[3]{0:T(128)} %pad_add_fusion.1.at_ref, bf16[512,1536]{1,0:T(8,128)(2,1)} %get-tuple-element.129.x_in.refs_0_, bf16[640,1536]{1,0:T(8,128)(2,1)} %bitcast.43, bf16[512,1536]{1,0:T(8,128)(2,1)} %get-tuple-element.137.refs_2_, ...), custom_call_target="tpu_custom_call" | custom-call | tf_op jit(solution)/shard_map/weight_grads/pallas_call | solution.py:754
  291.9 10.5 %weight_grads.3 = (bf16[768,1152]{1,0:T(8,128)(2,1)}, bf16[768,1152]{1,0:T(8,128)(2,1)}) custom-call(s32[3]{0:T(128)} %pad_add_fusion.3.at_ref, bf16[512,1536]{1,0:T(8,128)(2,1)} %get-tuple-element.129.x_in.refs_0_, bf16[640,1536]{1,0:T(8,128)(2,1)} %bitcast.44, bf16[512,1536]{1,0:T(8,128)(2,1)} %get-tuple-element.137.refs_2_, ...), custom_call_target="tpu_custom_call" | custom-call | tf_op jit(solution)/shard_map/weight_grads/pallas_call | solution.py:754
  307.5 4.7 all-to-all-start.6
  312.2 6.3 %give_gradn.1 = (f32[256,1664]{1,0:T(8,128)}, bf16[256,1664]{1,0:T(8,128)(2,1)}) custom-call(s32[2]{0:T(128)} %pad_add_fusion.at_ref, bf16[512,512]{1,0:T(8,128)(2,1)} %get-tuple-element.121.refs_0_, bf16[640,512]{1,0:T(8,128)(2,1)} %get-tuple-element.122.refs_1_, bf16[512,1664]{1,0:T(8,128)(2,1)} %get-tuple-element.144.refs_2_, ...), custom_call_target="tpu_custom_call" | custom-call | tf_op jit(solution)/shard_map/give_gradn/pallas_call | solution.py:264
  321.5 6.4 %middle_back.1 = (f32[256,1536]{1,0:T(8,128)}, bf16[256,1536]{1,0:T(8,128)(2,1)}, f32[1536,128]{1,0:T(8,128)}) custom-call(f32[256,1536]{1,0:T(8,128)} %get-tuple-element.120.middle, bf16[256,1536]{1,0:T(8,128)(2,1)} %get-tuple-element.123.own.normed, bf16[256,1536]{1,0:T(8,128)(2,1)} %grad_out.1, bf16[256,128]{1,0:T(8,128)(2,1)} %constant_dynamic-slice_fusion.code, ...), custom_call_target="tpu_custom_call" | custom-call | tf_op jit(solution)/shard_map/middle_back/pallas_call | solution.py:264
  330.6 20.9 %attend_back.1 = (f32[256,1536]{1,0:T(8,128)}, bf16[256,1536]{1,0:T(8,128)(2,1)}, bf16[2,96,1920]{2,1,0:T(8,128)(2,1)}, bf16[2,96,1920]{2,1,0:T(8,128)(2,1)}, bf...) custom-call(s32[2]{0:T(128)} %pad_add_fusion.at_ref, ...), custom_call_target="tpu_custom_call" | custom-call | tf_op jit(solution)/shard_map/attend_back/pallas_call | solution.py:264
  355.5 7.6 %collective-permute-done.28.refs_0_ = bf16[1,96,1920]{2,1,0:T(8,128)(2,1)S(1)} collective-permute-done((bf16[1,96,1920]{2,1,0:T(8,128)(2,1)}, bf16[1,96,1920]{2,1,0:T(8,128)(2,1)S(1)}, u32[]{:S(2)}, u32[]{:S(2)}) %collective-permute-start.28) | collective-permute-done | bytes 368672 | tf_op jit(solution)/shard_map/attn_last/ppermute | solution.py:45
  363.1 9.4 %collective-permute-done.29.refs_1_ = bf16[1,96,1920]{2,1,0:T(8,128)(2,1)} collective-permute-done((bf16[1,96,1920]{2,1,0:T(8,128)(2,1)}, bf16[1,96,1920]{2,1,0:T(8,128)(2,1)}, u32[]{:S(2)}, u32[]{:S(2)}) %collective-permute-start.29) | collective-permute-done | bytes 368672 | tf_op jit(solution)/shard_map/attn_last/ppermute | solution.py:45
  374.8 9.9 %collective-permute-start.32 = (bf16[2,96,1920]{2,1,0:T(8,128)(2,1)}, bf16[2,96,1920]{2,1,0:T(8,128)(2,1)}, u32[]{:S(2)}, u32[]{:S(2)}) collective-permute-start(bf16[2,96,1920]{2,1,0:T(8,128)(2,1)} %get-tuple-element.171), channel_id=1, source_target_pairs={{0,2},{2,0},{4,6},{6,4},{8,10},{10,8},{12,14},{14,12},{16,18},{18,... | collective-permute-start | bytes 2211848 | tf_op jit(solution)/shard_map/attn_far/ppermute | solution.py:45
  385.9 12.7 %collective-permute-done.34.refs_0_ = bf16[768,1152]{1,0:T(8,128)(2,1)} collective-permute-done((bf16[768,1152]{1,0:T(8,128)(2,1)}, bf16[768,1152]{1,0:T(8,128)(2,1)}, u32[]{:S(2)}, u32[]{:S(2)}) %collective-permute-start.34) | collective-permute-done | bytes 1769504 | tf_op jit(solution)/shard_map/expert_scatter/ppermute | solution.py:45
  404.9 4.2 collective-permute-done.31.refs_0_
  418.3 5.0 %all-to-all-start.7 = ((bf16[8,96,1152]{2,1,0:T(8,128)(2,1)}), bf16[8,96,1152]{2,1,0:T(8,128)(2,1)S(1)}, u32[]{:S(2)}, u32[]{:S(2)}) async-start(bf16[8,96,1152]{2,1,0:T(8,128)(2,1)} %bitcast.30), calls=%async_computation.7 | async-start | bytes 3538944 | tf_op jit(solution)/shard_map/expert_scatter/all_to_all | solution.py:863
  423.3 5.8 %give_branch.1 = (f32[256,1536]{1,0:T(8,128)}, bf16[256,1536]{1,0:T(8,128)(2,1)}) custom-call(s32[2]{0:T(128)} %pad_add_fusion.at_ref, bf16[512,512]{1,0:T(8,128)(2,1)} %get-tuple-element.121.refs_0_, bf16[640,512]{1,0:T(8,128)(2,1)} %get-tuple-element.122.refs_1_, bf16[8,144,1536]{2,1,0:T(8,128)(2,1)} %get-tuple-element.177.refs_2_), custom_call_target="tpu_custom_call" | custom-call | bytes 3000000 | tf_op jit(solution)/shard_map/give_branch/pallas_call | solution.py:264
  442.3 18.3 %collective-permute-done.40 = bf16[1,96,1920]{2,1,0:T(8,128)(2,1)S(1)} collective-permute-done((bf16[1,96,1920]{2,1,0:T(8,128)(2,1)S(1)}, bf16[1,96,1920]{2,1,0:T(8,128)(2,1)S(1)}, u32[]{:S(2)}, u32[]{:S(2)}) %collective-permute-start.40) | collective-permute-done | bytes 368672 | tf_op jit(solution)/shard_map/attn_outer/ppermute | solution.py:45
  460.6 7.8 %collective-permute-start.41 = (f32[96,128]{1,0:T(8,128)S(1)}, f32[96,128]{1,0:T(8,128)S(1)}, u32[]{:S(2)}, u32[]{:S(2)}) collective-permute-start(f32[96,128]{1,0:T(8,128)S(1)} %slice.95), channel_id=1, source_target_pairs={{0,1},{1,0},{2,3},{3,2},{4,5},{5,4},{6,7},{7,6},{8,9},{9,8},{10,11... | collective-permute-start | bytes 147464 | tf_op jit(solution)/shard_map/ppermute | solution.py:49
  (249 shorter events, 132.5 us)
Async XLA Ops:
  3.5 33.6 %all-to-all-start = ((bf16[8,96,1152]{2,1,0:T(8,128)(2,1)}), bf16[8,96,1152]{2,1,0:T(8,128)(2,1)S(1)}, u32[]{:S(2)}, u32[]{:S(2)}) async-start(bf16[8,96,1152]{2,1,0:T(8,128)(2,1)} %pad_maximum_fusion), calls=%async_computation | async-start | bytes 3538944 | tf_op jit(solution)/shard_map/all_to_all | solution.py:829
  8.3 28.7 %collective-permute-start.1 = (bf16[256,1536]{1,0:T(8,128)(2,1)}, bf16[256,1536]{1,0:T(8,128)(2,1)}, u32[]{:S(2)}, u32[]{:S(2)}) collective-permute-start(bf16[256,1536]{1,0:T(8,128)(2,1)} %grad_out.1), channel_id=1, source_target_pairs={{0,1},{1,0},{2,3},{3,2},{4,5},{5,4},{6,7},{7,6},{8,9},{9,8},{10,11... | collective-permute-start | bytes 2359304 | tf_op jit(solution)/shard_map/ppermute | solution.py:49
  9.6 27.5 %collective-permute-start = (bf16[256,1536]{1,0:T(8,128)(2,1)S(1)}, bf16[256,1536]{1,0:T(8,128)(2,1)S(1)}, u32[]{:S(2)}, u32[]{:S(2)}) collective-permute-start(bf16[256,1536]{1,0:T(8,128)(2,1)S(1)} %copy-done.6), channel_id=1, source_target_pairs={{0,1},{1,0},{2,3},{3,2},{4,5},{5,4},{6,7},{7,6},{8,9},{9,8},{10,11... | collective-permute-start | bytes 2359304 | tf_op jit(solution)/shard_map/ppermute | solution.py:49
  11.5 24.6 %collective-permute-start.2 = (bf16[1,96,1920]{2,1,0:T(8,128)(2,1)S(1)}, bf16[1,96,1920]{2,1,0:T(8,128)(2,1)S(1)}, u32[]{:S(2)}, u32[]{:S(2)}) collective-permute-start(bf16[1,96,1920]{2,1,0:T(8,128)(2,1)S(1)} %bitcast.57), channel_id=1, source_target_pairs={{0,16},{2,18},{4,20},{6,22},{8,24},{10,26},{12,28},{14,30},{16,0},... | collective-permute-start | bytes 1105928 | tf_op jit(solution)/shard_map/ppermute | solution.py:45
  38.7 32.3 %collective-permute-start.7 = (bf16[768,1152]{1,0:T(8,128)(2,1)}, bf16[768,1152]{1,0:T(8,128)(2,1)S(1)}, u32[]{:S(2)}, u32[]{:S(2)}) collective-permute-start(bf16[768,1152]{1,0:T(8,128)(2,1)} %get-tuple-element.106), channel_id=1, source_target_pairs={{0,1},{1,0},{2,3},{3,2},{4,5},{5,4},{6,7},{7,6},{8,9},{9,8},{10,11... | collective-permute-start | bytes 5308424 | tf_op jit(solution)/shard_map/ppermute | solution.py:49
  40.5 30.4 %collective-permute-start.3 = (bf16[2,96,1920]{2,1,0:T(8,128)(2,1)}, bf16[2,96,1920]{2,1,0:T(8,128)(2,1)S(1)}, u32[]{:S(2)}, u32[]{:S(2)}) collective-permute-start(bf16[2,96,1920]{2,1,0:T(8,128)(2,1)} %get-tuple-element.105.refs_1_.refs_0_), channel_id=1, source_target_pairs={{0,2},{2,0},{4,6},{6,4},{8,10},{10,8},{12,14},{14,12},{16,18},{18,... | collective-permute-start | bytes 2211848 | tf_op jit(solution)/shard_map/weights_near/ppermute | solution.py:45
  40.5 30.4 %collective-permute-start.4 = (bf16[2,96,1920]{2,1,0:T(8,128)(2,1)}, bf16[2,96,1920]{2,1,0:T(8,128)(2,1)S(1)}, u32[]{:S(2)}, u32[]{:S(2)}) collective-permute-start(bf16[2,96,1920]{2,1,0:T(8,128)(2,1)} %get-tuple-element.105.refs_1_.refs_0_), channel_id=1, source_target_pairs={{0,4},{2,6},{4,0},{6,2},{8,12},{10,14},{12,8},{14,10},{16,20},{18,... | collective-permute-start | bytes 2211848 | tf_op jit(solution)/shard_map/weights_near/ppermute | solution.py:45
  41.7 29.3 %collective-permute-start.5 = (bf16[2,96,1920]{2,1,0:T(8,128)(2,1)}, bf16[2,96,1920]{2,1,0:T(8,128)(2,1)}, u32[]{:S(2)}, u32[]{:S(2)}) collective-permute-start(bf16[2,96,1920]{2,1,0:T(8,128)(2,1)} %get-tuple-element.105.refs_1_.refs_0_), channel_id=1, source_target_pairs={{0,8},{2,10},{4,12},{6,14},{8,0},{10,2},{12,4},{14,6},{16,24},{18,... | collective-permute-start | bytes 2211848 | tf_op jit(solution)/shard_map/weights_near/ppermute | solution.py:45
  49.3 20.3 %collective-permute-start.6 = (bf16[1,160,1152]{2,1,0:T(8,128)(2,1)}, bf16[1,160,1152]{2,1,0:T(8,128)(2,1)}, u32[]{:S(2)}, u32[]{:S(2)}) collective-permute-start(bf16[1,160,1152]{2,1,0:T(8,128)(2,1)} %bitcast.54), channel_id=1, source_target_pairs={{0,16},{2,18},{4,20},{6,22},{8,24},{10,26},{12,28},{14,30},{16,0},... | collective-permute-start | bytes 1105928 | tf_op jit(solution)/shard_map/ppermute | solution.py:45
  72.6 31.3 %collective-permute-start.10 = (bf16[2,96,1920]{2,1,0:T(8,128)(2,1)}, bf16[2,96,1920]{2,1,0:T(8,128)(2,1)}, u32[]{:S(2)}, u32[]{:S(2)}) collective-permute-start(bf16[2,96,1920]{2,1,0:T(8,128)(2,1)} %get-tuple-element.109.refs_4_), channel_id=1, source_target_pairs={{0,4},{2,6},{4,0},{6,2},{8,12},{10,14},{12,8},{14,10},{16,20},{18,... | collective-permute-start | bytes 2211848 | tf_op jit(solution)/shard_map/weights_far/ppermute | solution.py:45
  72.9 31.0 %collective-permute-start.11 = (bf16[2,96,1920]{2,1,0:T(8,128)(2,1)}, bf16[2,96,1920]{2,1,0:T(8,128)(2,1)}, u32[]{:S(2)}, u32[]{:S(2)}) collective-permute-start(bf16[2,96,1920]{2,1,0:T(8,128)(2,1)} %get-tuple-element.109.refs_4_), channel_id=1, source_target_pairs={{0,2},{2,0},{4,6},{6,4},{8,10},{10,8},{12,14},{14,12},{16,18},{18,... | collective-permute-start | bytes 2211848 | tf_op jit(solution)/shard_map/weights_far/ppermute | solution.py:45
  75.2 28.1 %collective-permute-start.12 = (bf16[1,240,1152]{2,1,0:T(8,128)(2,1)}, bf16[1,240,1152]{2,1,0:T(8,128)(2,1)S(1)}, u32[]{:S(2)}, u32[]{:S(2)}) collective-permute-start(bf16[1,240,1152]{2,1,0:T(8,128)(2,1)} %bitcast.50), channel_id=1, source_target_pairs={{0,16},{2,18},{4,20},{6,22},{8,24},{10,26},{12,28},{14,30},{16,0},... | collective-permute-start | bytes 1658888 | tf_op jit(solution)/shard_map/ppermute | solution.py:45
  79.4 24.5 %collective-permute-start.8 = (bf16[1,96,1920]{2,1,0:T(8,128)(2,1)S(1)}, bf16[1,96,1920]{2,1,0:T(8,128)(2,1)S(1)}, u32[]{:S(2)}, u32[]{:S(2)}) collective-permute-start(bf16[1,96,1920]{2,1,0:T(8,128)(2,1)S(1)} %slice.71), channel_id=1, source_target_pairs={{0,2},{2,0},{4,6},{6,4},{8,10},{10,8},{12,14},{14,12},{16,18},{18,... | collective-permute-start | bytes 1105928 | tf_op jit(solution)/shard_map/weights_far/ppermute | solution.py:45
  80.6 23.2 %collective-permute-start.9 = (bf16[1,96,1920]{2,1,0:T(8,128)(2,1)S(1)}, bf16[1,96,1920]{2,1,0:T(8,128)(2,1)}, u32[]{:S(2)}, u32[]{:S(2)}) collective-permute-start(bf16[1,96,1920]{2,1,0:T(8,128)(2,1)S(1)} %slice.72), channel_id=1, source_target_pairs={{0,4},{2,6},{4,0},{6,2},{8,12},{10,14},{12,8},{14,10},{16,20},{18,... | collective-permute-start | bytes 1105928 | tf_op jit(solution)/shard_map/weights_far/ppermute | solution.py:45
  122.8 64.8 %all-to-all-start.1 = ((bf16[8,144,1664]{2,1,0:T(8,128)(2,1)}), bf16[8,144,1664]{2,1,0:T(8,128)(2,1)}, u32[]{:S(2)}, u32[]{:S(2)}) async-start(bf16[8,144,1664]{2,1,0:T(8,128)(2,1)} %get-tuple-element.126), calls=%async_computation.1 | async-start | bytes 7667712 | tf_op jit(solution)/shard_map/grads_rows/all_to_all | solution.py:863
  150.9 34.6 %collective-permute-start.20 = (bf16[1,208,1152]{2,1,0:T(8,128)(2,1)}, bf16[1,208,1152]{2,1,0:T(8,128)(2,1)S(1)}, u32[]{:S(2)}, u32[]{:S(2)}) collective-permute-start(bf16[1,208,1152]{2,1,0:T(8,128)(2,1)} %bitcast.52), channel_id=1, source_target_pairs={{0,16},{2,18},{4,20},{6,22},{8,24},{10,26},{12,28},{14,30},{16,0},... | collective-permute-start | bytes 1437704 | tf_op jit(solution)/shard_map/ppermute | solution.py:45
  187.6 24.2 %all-to-all-start.2 = ((bf16[8,64,1536]{2,1,0:T(8,128)(2,1)}), bf16[8,64,1536]{2,1,0:T(8,128)(2,1)S(1)}, u32[]{:S(2)}, u32[]{:S(2)}) async-start(bf16[8,64,1536]{2,1,0:T(8,128)(2,1)} %bitcast.48), calls=%async_computation.2 | async-start | bytes 3145728 | tf_op jit(solution)/shard_map/tokens_rows/all_to_all | solution.py:863
  213.0 28.9 %all-to-all-start.3 = ((bf16[8,80,1536]{2,1,0:T(8,128)(2,1)}), bf16[8,80,1536]{2,1,0:T(8,128)(2,1)S(1)}, u32[]{:S(2)}, u32[]{:S(2)}) async-start(bf16[8,80,1536]{2,1,0:T(8,128)(2,1)} %bitcast.49), calls=%async_computation.3 | async-start | bytes 3932160 | tf_op jit(solution)/shard_map/tokens_rows/all_to_all | solution.py:863
  243.2 27.2 %all-to-all-start.5 = ((bf16[8,64,1664]{2,1,0:T(8,128)(2,1)}), bf16[8,64,1664]{2,1,0:T(8,128)(2,1)}, u32[]{:S(2)}, u32[]{:S(2)}) async-start(bf16[8,64,1664]{2,1,0:T(8,128)(2,1)} %bitcast.53), calls=%async_computation.5 | async-start | bytes 3407872 | tf_op jit(solution)/shard_map/gradn_rows/all_to_all | solution.py:863
  270.4 35.7 %all-to-all-start.4 = ((bf16[8,80,1664]{2,1,0:T(8,128)(2,1)}), bf16[8,80,1664]{2,1,0:T(8,128)(2,1)S(1)}, u32[]{:S(2)}, u32[]{:S(2)}) async-start(bf16[8,80,1664]{2,1,0:T(8,128)(2,1)} %bitcast.51), calls=%async_computation.4 | async-start | bytes 4259840 | tf_op jit(solution)/shard_map/gradn_rows/all_to_all | solution.py:863
  307.5 101.6 %all-to-all-start.6 = ((bf16[8,144,1536]{2,1,0:T(8,128)(2,1)}), bf16[8,144,1536]{2,1,0:T(8,128)(2,1)S(1)}, u32[]{:S(2)}, u32[]{:S(2)}) async-start(bf16[8,144,1536]{2,1,0:T(8,128)(2,1)} %gate.40), calls=%async_computation.6 | async-start | bytes 7077888 | tf_op jit(solution)/shard_map/branch_rows/all_to_all | solution.py:863
  319.1 79.4 %collective-permute-start.34 = (bf16[768,1152]{1,0:T(8,128)(2,1)}, bf16[768,1152]{1,0:T(8,128)(2,1)}, u32[]{:S(2)}, u32[]{:S(2)}) collective-permute-start(bf16[768,1152]{1,0:T(8,128)(2,1)} %add_convert_fusion.1.refs_2_), channel_id=1, source_target_pairs={{0,16},{2,18},{4,20},{6,22},{8,24},{10,26},{12,28},{14,30},{16,0},... | collective-permute-start | bytes 5308424 | tf_op jit(solution)/shard_map/expert_scatter/ppermute | solution.py:45
  328.3 72.7 %collective-permute-start.35 = (bf16[768,1152]{1,0:T(8,128)(2,1)}, bf16[768,1152]{1,0:T(8,128)(2,1)}, u32[]{:S(2)}, u32[]{:S(2)}) collective-permute-start(bf16[768,1152]{1,0:T(8,128)(2,1)} %get-tuple-element.175), channel_id=1, source_target_pairs={{0,1},{1,0},{2,3},{3,2},{4,5},{5,4},{6,7},{7,6},{8,9},{9,8},{10,11... | collective-permute-start | bytes 5308424 | tf_op jit(solution)/shard_map/expert_scatter/ppermute | solution.py:49
  351.5 21.0 %collective-permute-start.30 = (bf16[256,1536]{1,0:T(8,128)(2,1)}, bf16[256,1536]{1,0:T(8,128)(2,1)}, u32[]{:S(2)}, u32[]{:S(2)}) collective-permute-start(bf16[256,1536]{1,0:T(8,128)(2,1)} %get-tuple-element.167), channel_id=1, source_target_pairs={{0,1},{1,0},{2,3},{3,2},{4,5},{5,4},{6,7},{7,6},{8,9},{9,8},{10,11... | collective-permute-start | bytes 2359304 | tf_op jit(solution)/shard_map/ppermute | solution.py:49
  351.9 20.6 %collective-permute-start.29 = (bf16[1,96,1920]{2,1,0:T(8,128)(2,1)}, bf16[1,96,1920]{2,1,0:T(8,128)(2,1)}, u32[]{:S(2)}, u32[]{:S(2)}) collective-permute-start(bf16[1,96,1920]{2,1,0:T(8,128)(2,1)} %get-tuple-element.165), channel_id=1, source_target_pairs={{0,4},{2,6},{4,0},{6,2},{8,12},{10,14},{12,8},{14,10},{16,20},{18,... | collective-permute-start | bytes 1105928 | tf_op jit(solution)/shard_map/attn_last/ppermute | solution.py:45
  374.8 34.3 %collective-permute-start.31 = (bf16[2,96,1920]{2,1,0:T(8,128)(2,1)}, bf16[2,96,1920]{2,1,0:T(8,128)(2,1)}, u32[]{:S(2)}, u32[]{:S(2)}) collective-permute-start(bf16[2,96,1920]{2,1,0:T(8,128)(2,1)} %get-tuple-element.170.refs_3_), channel_id=1, source_target_pairs={{0,8},{2,10},{4,12},{6,14},{8,0},{10,2},{12,4},{14,6},{16,24},{18,... | collective-permute-start | bytes 2211848 | tf_op jit(solution)/shard_map/attn_far/ppermute | solution.py:45
  374.8 34.3 %collective-permute-start.32 = (bf16[2,96,1920]{2,1,0:T(8,128)(2,1)}, bf16[2,96,1920]{2,1,0:T(8,128)(2,1)}, u32[]{:S(2)}, u32[]{:S(2)}) collective-permute-start(bf16[2,96,1920]{2,1,0:T(8,128)(2,1)} %get-tuple-element.171), channel_id=1, source_target_pairs={{0,2},{2,0},{4,6},{6,4},{8,10},{10,8},{12,14},{14,12},{16,18},{18,... | collective-permute-start | bytes 2211848 | tf_op jit(solution)/shard_map/attn_far/ppermute | solution.py:45
  384.7 24.4 %collective-permute-start.33 = (bf16[2,96,1920]{2,1,0:T(8,128)(2,1)}, bf16[2,96,1920]{2,1,0:T(8,128)(2,1)}, u32[]{:S(2)}, u32[]{:S(2)}) collective-permute-start(bf16[2,96,1920]{2,1,0:T(8,128)(2,1)} %get-tuple-element.172.refs_2_), channel_id=1, source_target_pairs={{0,4},{2,6},{4,0},{6,2},{8,12},{10,14},{12,8},{14,10},{16,20},{18,... | collective-permute-start | bytes 2211848 | tf_op jit(solution)/shard_map/attn_far/ppermute | solution.py:45
  414.6 20.4 %collective-permute-start.37 = (bf16[2,96,1920]{2,1,0:T(8,128)(2,1)}, bf16[2,96,1920]{2,1,0:T(8,128)(2,1)S(1)}, u32[]{:S(2)}, u32[]{:S(2)}) collective-permute-start(bf16[2,96,1920]{2,1,0:T(8,128)(2,1)} %get-tuple-element.189), channel_id=1, source_target_pairs={{0,2},{2,0},{4,6},{6,4},{8,10},{10,8},{12,14},{14,12},{16,18},{18,... | collective-permute-start | bytes 2211848 | tf_op jit(solution)/shard_map/attn_near/ppermute | solution.py:45
  414.8 20.3 %collective-permute-start.38 = (bf16[2,96,1920]{2,1,0:T(8,128)(2,1)}, bf16[2,96,1920]{2,1,0:T(8,128)(2,1)}, u32[]{:S(2)}, u32[]{:S(2)}) collective-permute-start(bf16[2,96,1920]{2,1,0:T(8,128)(2,1)} %get-tuple-element.190), channel_id=1, source_target_pairs={{0,4},{2,6},{4,0},{6,2},{8,12},{10,14},{12,8},{14,10},{16,20},{18,... | collective-permute-start | bytes 2211848 | tf_op jit(solution)/shard_map/attn_near/ppermute | solution.py:45
  418.3 53.0 %all-to-all-start.7 = ((bf16[8,96,1152]{2,1,0:T(8,128)(2,1)}), bf16[8,96,1152]{2,1,0:T(8,128)(2,1)S(1)}, u32[]{:S(2)}, u32[]{:S(2)}) async-start(bf16[8,96,1152]{2,1,0:T(8,128)(2,1)} %bitcast.30), calls=%async_computation.7 | async-start | bytes 3538944 | tf_op jit(solution)/shard_map/expert_scatter/all_to_all | solution.py:863
  439.1 21.5 %collective-permute-start.40 = (bf16[1,96,1920]{2,1,0:T(8,128)(2,1)S(1)}, bf16[1,96,1920]{2,1,0:T(8,128)(2,1)S(1)}, u32[]{:S(2)}, u32[]{:S(2)}) collective-permute-start(bf16[1,96,1920]{2,1,0:T(8,128)(2,1)S(1)} %slice.116), channel_id=1, source_target_pairs={{0,16},{2,18},{4,20},{6,22},{8,24},{10,26},{12,28},{14,30},{16,0},... | collective-permute-start | bytes 1105928 | tf_op jit(solution)/shard_map/attn_outer/ppermute | solution.py:45
  (63 other events, 360.3 us)

commit v4 on v3

--- a/solution.py
+++ b/solution.py
@@ -122,27 +122,39 @@
 
 def sum_far(parts, terms, count):
     first, second = terms
-    return {4: swap(first, 2, count), 1: swap(second, 4, count), 2: swap(parts[3], 1, count)}
-
-
-def terms_kernel(*refs):
-    for k in range(3):
-        refs[6 + k][...] = (refs[k][...].astype(f32) + refs[3 + k][...].astype(f32)).astype(bf16)
+    return {
+        6: swap(first, 2, count),
+        5: swap(second, 1, count),
+        3: swap(parts[3], 1, count),
+        9: swap(parts[9], 2, count),
+    }
+
+
+def terms_kernel(one, two, four, six, five, three, nine, one_out, two_out, four_out):
+    four_out[...] = (
+        four[...].astype(f32) + six[...].astype(f32) + five[...].astype(f32)
+    ).astype(bf16)
+    first = three.shape[0]
+    two_out[:first] = (two[:first].astype(f32) + three[...].astype(f32)).astype(bf16)
+    two_out[first:] = two[first:]
+    one_out[:first] = one[:first]
+    one_out[first:] = (one[first:].astype(f32) + nine[...].astype(f32)).astype(bf16)
 
 
 def near_terms(parts, got):
-    args = [parts[bit] for bit in NEAR] + [got[bit] for bit in NEAR]
+    args = [parts[bit] for bit in NEAR] + [got[k] for k in (6, 5, 3, 9)]
     shape = parts[1].shape
-    grid = 4 if shape[-2] % 64 == 0 else 1
-    block = shape[:-2] + (shape[-2] // grid, shape[-1])
-    lead = (0,) * (len(shape) - 2)
-    spec = pl.BlockSpec(block, lambda i: lead + (i, 0))
+    grid = 6 if shape[1] % 96 == 0 else 1
+
+    def spec(dims):
+        return pl.BlockSpec((dims[0], dims[1] // grid, dims[2]), lambda i: (0, i, 0))
+
     outs = pl.pallas_call(
         terms_kernel,
         grid=(grid,),
         out_shape=[jax.ShapeDtypeStruct(shape, bf16)] * 3,
-        in_specs=[spec] * 6,
-        out_specs=[spec] * 3,
+        in_specs=[spec(arg.shape) for arg in args],
+        out_specs=[spec(shape)] * 3,
         compiler_params=pltpu.CompilerParams(vmem_limit_bytes=60 * 1024 * 1024),
         cost_estimate=FREE,
         name="terms",
@@ -217,7 +229,10 @@
 
 def part_order(count):
     outer = count // CUBE
-    return [(b, (0, outer)) for b in range(7)] + [(7, span) for span in halves(outer)]
+    first, second = halves(outer)
+    offsets = {3: first, 7: first}
+    order = [(b, offsets.get(b, (0, outer))) for b in range(CUBE)]
+    return order + [(7, second), (3, second)]
 
 
 def part_shapes(count, block, width):
@@ -869,7 +884,7 @@
 
     pair, expert_rows = gate([pair, expert_rows], cosine, sine_table, hidden_other, grad_other)
     if count == 2 * CUBE:
-        edges = [expert_rows.shape[0] * k // 48 // 16 * 16 for k in (0, 10, 25, 31, 44, 48)]
+        edges = [expert_rows.shape[0] * k // 48 // 16 * 16 for k in (0, 10, 26, 26, 34, 48)]
     else:
         edges = [0] * 5 + [expert_rows.shape[0]]
     pieces = [(expert_rows[None], 0, 0, 0), (swap_core(expert_rows)[None], 0, 0, 1)]
@@ -1028,18 +1043,18 @@
     )
     parts = spread_parts(parts, me, count)
 
-    parts = gate_dict(parts, (3,) + LAST)
+    keep_swapped = swap_core(keep_other)
+    parts = gate_dict(parts, (3, 9) + LAST, keep_swapped)
     with jax.named_scope("attn_last"):
         got = sum_last(parts, count)
     normed_swapped = swap_core(normed_other)
-    gated = gate([got[7], got[8], parts[3]], normed_swapped)
-    got, parts[3] = dict(zip(LAST, gated)), gated[2]
+    gated = gate([got[7], got[8], parts[3], parts[9]], normed_swapped)
+    got, parts[3], parts[9] = dict(zip(LAST, gated)), gated[2], gated[3]
     with jax.named_scope("attn_far"):
         terms = far_terms(parts, got)
         attn_far = sum_far(parts, terms, count)
     with jax.named_scope("expert_scatter"):
         sent_got, keep = gate([sent_got, keep], terms)
-        keep_swapped = swap_core(keep_other)
         if bits:
             total = keep.astype(f32) + keep_swapped.astype(f32) + sent_got.astype(f32)
         else:
@@ -1052,8 +1067,8 @@
             total = mine + swap(other.astype(bf16), bit, count).astype(f32)
         total = total.astype(bf16)
     grad_normed = normed_own + normed_swapped.astype(f32)
-    gated = gate([attn_far[k] for k in NEAR] + [branch, total])
-    attn_far, branch, total = dict(zip(NEAR, gated)), gated[3], gated[4]
+    gated = gate([attn_far[k] for k in FAR] + [branch, total])
+    attn_far, branch, total = dict(zip(FAR, gated)), gated[4], gated[5]
     with jax.named_scope("attn_near"):
         attn_near = sum_near(near_terms(parts, attn_far), count)
     branch_own, branch_other = give(picks, (branch,), "give_branch")

time: 482 us -> 473 us (0.981)
  waiting for transfers between devices: 168 us -> 158 us
    ppermute x25, waiting for transfers between devices: 158 us -> 144 us  [swap(): return lax.ppermute(values, 'dp', [(i, i ^ bit) for i in range(count)])]
    ppermute x17 -> x16, starting transfers between devices: 25.8 us -> 31.8 us  [swap_core(): return lax.ppermute(values, 'tensor', [(0, 1), (1, 0)])]
    unnamed x97 -> x87, local copies, waits for them, and re-layouts: 19.1 us -> 17.2 us
    slice x9 -> x8, local copies, waits for them, and re-layouts: 9.39 us -> 9.71 us  [cut(): return lax.slice_in_dim(values, span[0], span[1], axis=axis)]
  transfers between devices with their start and end apart: 50 -> 49, of which waited for: 18 -> 22; matrix products, arithmetic and copies ran while one was open for 10% -> 10% of each run, Pallas kernels for 28% -> 28%
where the time goes in v4:
time: 473 us; the launch traced here: 466 us
  waiting for transfers between devices  158 us (33%)
  Pallas kernels  137 us (29%)
  starting transfers between devices  101 us (21%)
  local copies, waits for them, and re-layouts  36.6 us (8%)
  other arithmetic  32.5 us (7%)
    ppermute x25, waiting for transfers between devices, swap(): return lax.ppermute(values, 'dp', [(i, i ^ bit) for i in range(count)])  144 us
    pallas_call x8, Pallas kernels, vmem_call(): pl.pallas_call(kernel, out_shape=out_shapes, in_specs=[pl.BlockSpec(memor...  68.5 us
    pallas_call x2, Pallas kernels, moe(): pl.pallas_call(functools.partial(moe_kernel, (copies, hidden, blocks, out...  38.6 us
    all_to_all x7, starting transfers between devices, exchange(): lax.all_to_all(rows, 'dp', 0, 0, tiled=True, axis_index_groups=groups)  32.9 us
    ppermute x16, starting transfers between devices, swap_core(): return lax.ppermute(values, 'tensor', [(0, 1), (1, 0)])  31.8 us
    ppermute x25, starting transfers between devices, swap(): return lax.ppermute(values, 'dp', [(i, i ^ bit) for i in range(count)])  31.5 us
    pallas_call x2, Pallas kernels, weight_grads(): pl.pallas_call(functools.partial(weight_grads_kernel, len(pre)), out_shap...  21 us
    unnamed x87, local copies, waits for them, and re-layouts  17.2 us
  transfers between devices with their start and end apart: 49, of which 22 were waited for; matrix products, arithmetic and copies ran while one was open for 10% of the time, Pallas kernels for 28%

profile of v4, /device:TPU:3, one launch (start us, length us, event | category | flops | bytes accessed | tf_op | source)
XLA Modules:
  0.0 466.0 jit_solution(3846066202892604544)
XLA Ops:
  3.5 4.8 %all-to-all-start = ((bf16[8,96,1152]{2,1,0:T(8,128)(2,1)}), bf16[8,96,1152]{2,1,0:T(8,128)(2,1)S(1)}, u32[]{:S(2)}, u32[]{:S(2)}) async-start(bf16[8,96,1152]{2,1,0:T(8,128)(2,1)} %pad_maximum_fusion), calls=%async_computation | async-start | bytes 3538944 | tf_op jit(solution)/shard_map/all_to_all | solution.py:844
  15.9 20.2 %collective-permute-done.2 = bf16[1,96,1920]{2,1,0:T(8,128)(2,1)S(1)} collective-permute-done((bf16[1,96,1920]{2,1,0:T(8,128)(2,1)S(1)}, bf16[1,96,1920]{2,1,0:T(8,128)(2,1)S(1)}, u32[]{:S(2)}, u32[]{:S(2)}) %collective-permute-start.2) | collective-permute-done | bytes 368672 | tf_op jit(solution)/shard_map/ppermute | solution.py:45
  53.1 6.7 %slots.1 = (bf16[512,512]{1,0:T(8,128)(2,1)}, bf16[640,512]{1,0:T(8,128)(2,1)}, bf16[8,144,1664]{2,1,0:T(8,128)(2,1)}) custom-call(s32[2]{0:T(128)} %pad_add_fusion.at_ref, s32[512,8]{1,0:T(8,128)} %copy.103.order_col, s32[8,512]{1,0:T(8,128)} %bitcast.59, bf16[256,1536]{1,0:T(8,128)(2,1)} %grad_out.1, ...), custom_call_target="tpu_custom_call" | custom-call | bytes 3000000 | tf_op jit(solution)/shard_map/slots/pallas_call | solution.py:279
  60.7 9.0 %collective-permute-done.6.refs_4_.refs_2_.refs_3_ = bf16[1,160,1152]{2,1,0:T(8,128)(2,1)} collective-permute-done((bf16[1,160,1152]{2,1,0:T(8,128)(2,1)}, bf16[1,160,1152]{2,1,0:T(8,128)(2,1)}, u32[]{:S(2)}, u32[]{:S(2)}) %collective-permute-start.6) | collective-permute-done | bytes 368672 | tf_op jit(solution)/shard_map/ppermute | solution.py:45
  80.6 20.0 %collective-permute-done.12.refs_4_.refs_5_ = bf16[1,256,1152]{2,1,0:T(8,128)(2,1)S(1)} collective-permute-done((bf16[1,256,1152]{2,1,0:T(8,128)(2,1)}, bf16[1,256,1152]{2,1,0:T(8,128)(2,1)S(1)}, u32[]{:S(2)}, u32[]{:S(2)}) %collective-permute-start.12) | collective-permute-done | bytes 589856 | tf_op jit(solution)/shard_map/ppermute | solution.py:45
  117.4 4.9 %all-to-all-start.1 = ((bf16[8,144,1664]{2,1,0:T(8,128)(2,1)}), bf16[8,144,1664]{2,1,0:T(8,128)(2,1)}, u32[]{:S(2)}, u32[]{:S(2)}) async-start(bf16[8,144,1664]{2,1,0:T(8,128)(2,1)} %get-tuple-element.130), calls=%async_computation.1 | async-start | bytes 7667712 | tf_op jit(solution)/shard_map/grads_rows/all_to_all | solution.py:878
  122.3 13.7 %attend.1 = (bf16[512,1536]{1,0:T(8,128)(2,1)}, bf16[512,1536]{1,0:T(8,128)(2,1)}, bf16[512,768]{1,0:T(8,128)(2,1)}, bf16[512,128]{1,0:T(8,128)(2,1)}, bf16[512,...) custom-call(s32[2]{0:T(128)} %pad_add_fusion.at_ref, ...), custom_call_target="tpu_custom_call" | custom-call | tf_op jit(solution)/shard_map/attend/pallas_call | solution.py:279
  148.5 5.1 %take.1 = (bf16[512,1536]{1,0:T(8,128)(2,1)}, bf16[640,1536]{1,0:T(8,128)(2,1)}) custom-call(s32[2]{0:T(128)} %pad_add_fusion.at_ref, bf16[256,1536]{1,0:T(8,128)(2,1)} %get-tuple-element.127.own.normed, bf16[256,1536]{1,0:T(8,128)(2,1)} %copy-done.29, bf16[512,512]{1,0:T(8,128)(2,1)} %get-tuple-element.125.refs_0_, bf16[640,512]{1,0:T(8,128)(2,1)} %get-tuple-element.126.refs_1_), custom_call_target="tpu_custom_call" | custom-call | tf_op jit(solution)/shard_map/take/pallas_call | solution.py:279
  153.6 19.1 %collective-permute-done.19.refs_2_.refs_6_.refs_7_ = bf16[1,128,1152]{2,1,0:T(8,128)(2,1)S(1)} collective-permute-done((bf16[1,128,1152]{2,1,0:T(8,128)(2,1)}, bf16[1,128,1152]{2,1,0:T(8,128)(2,1)S(1)}, u32[]{:S(2)}, u32[]{:S(2)}) %collective-permute-start.19) | collective-permute-done | bytes 294944 | tf_op jit(solution)/shard_map/ppermute | solution.py:45
  186.0 18.4 %collective-permute-done.20.refs_2_.refs_8_.refs_9_ = bf16[1,224,1152]{2,1,0:T(8,128)(2,1)S(1)} collective-permute-done((bf16[1,224,1152]{2,1,0:T(8,128)(2,1)}, bf16[1,224,1152]{2,1,0:T(8,128)(2,1)S(1)}, u32[]{:S(2)}, u32[]{:S(2)}) %collective-permute-start.20) | collective-permute-done | bytes 516128 | tf_op jit(solution)/shard_map/ppermute | solution.py:45
  208.1 5.0 %all-to-all-start.3 = ((bf16[8,80,1536]{2,1,0:T(8,128)(2,1)}), bf16[8,80,1536]{2,1,0:T(8,128)(2,1)S(1)}, u32[]{:S(2)}, u32[]{:S(2)}) async-start(bf16[8,80,1536]{2,1,0:T(8,128)(2,1)} %bitcast.48), calls=%async_computation.3 | async-start | bytes 3932160 | tf_op jit(solution)/shard_map/tokens_rows/all_to_all | solution.py:878
  213.1 4.4 collective-permute-start.22
  219.9 17.8 %experts.2 = (bf16[8,144,1536]{2,1,0:T(8,128)(2,1)}, bf16[512,1664]{1,0:T(8,128)(2,1)}, bf16[512,768]{1,0:T(8,128)(2,1)}, bf16[512,1536]{1,0:T(8,128)(2,1)}, bf16[512,1536]{1,0:T(8,128)(2,1)}) custom-call(s32[2]{0:T(128)} %pad_add_fusion.at_ref, bf16[1536,128]{1,0:T(8,128)(2,1)} %get-tuple-element.128.router_ref.router, ...), custom_call_target="tpu_custom_call" | custom-call | bytes 3000000 | tf_op jit(solution)/shard_map/experts/pallas_call | solution.py:700
  238.9 4.8 %all-to-all-start.5 = ((bf16[8,64,1664]{2,1,0:T(8,128)(2,1)}), bf16[8,64,1664]{2,1,0:T(8,128)(2,1)}, u32[]{:S(2)}, u32[]{:S(2)}) async-start(bf16[8,64,1664]{2,1,0:T(8,128)(2,1)} %bitcast.52), calls=%async_computation.5 | async-start | bytes 3407872 | tf_op jit(solution)/shard_map/gradn_rows/all_to_all | solution.py:878
  244.5 20.8 %experts.3 = (bf16[8,144,1536]{2,1,0:T(8,128)(2,1)}, bf16[640,1664]{1,0:T(8,128)(2,1)}, bf16[640,768]{1,0:T(8,128)(2,1)}, bf16[640,1536]{1,0:T(8,128)(2,1)}, bf16[640,1536]{1,0:T(8,128)(2,1)}) custom-call(s32[2]{0:T(128)} %pad_add_fusion.at_ref, bf16[1536,128]{1,0:T(8,128)(2,1)} %gate.32.router_ref, ...), custom_call_target="tpu_custom_call", output_to_operand_aliasing={{0}: (4, {})} | custom-call | bytes 3000000 | tf_op jit(solution)/shard_map/experts/pallas_call | solution.py:700
  265.3 4.8 %all-to-all-start.4 = ((bf16[8,80,1664]{2,1,0:T(8,128)(2,1)}), bf16[8,80,1664]{2,1,0:T(8,128)(2,1)S(1)}, u32[]{:S(2)}, u32[]{:S(2)}) async-start(bf16[8,80,1664]{2,1,0:T(8,128)(2,1)} %bitcast.50), calls=%async_computation.4 | async-start | bytes 4259840 | tf_op jit(solution)/shard_map/gradn_rows/all_to_all | solution.py:878
  271.9 10.5 %weight_grads.2 = (bf16[768,1152]{1,0:T(8,128)(2,1)}, bf16[768,1152]{1,0:T(8,128)(2,1)}) custom-call(s32[3]{0:T(128)} %pad_add_fusion.1.at_ref, bf16[512,1536]{1,0:T(8,128)(2,1)} %get-tuple-element.133.x_in.refs_0_, bf16[640,1536]{1,0:T(8,128)(2,1)} %bitcast.42, bf16[512,1536]{1,0:T(8,128)(2,1)} %get-tuple-element.141.refs_2_, ...), custom_call_target="tpu_custom_call" | custom-call | tf_op jit(solution)/shard_map/weight_grads/pallas_call | solution.py:769
  286.1 10.5 %weight_grads.3 = (bf16[768,1152]{1,0:T(8,128)(2,1)}, bf16[768,1152]{1,0:T(8,128)(2,1)}) custom-call(s32[3]{0:T(128)} %pad_add_fusion.3.at_ref, bf16[512,1536]{1,0:T(8,128)(2,1)} %get-tuple-element.133.x_in.refs_0_, bf16[640,1536]{1,0:T(8,128)(2,1)} %bitcast.43, bf16[512,1536]{1,0:T(8,128)(2,1)} %get-tuple-element.141.refs_2_, ...), custom_call_target="tpu_custom_call" | custom-call | tf_op jit(solution)/shard_map/weight_grads/pallas_call | solution.py:769
  301.6 4.9 %all-to-all-start.6 = ((bf16[8,144,1536]{2,1,0:T(8,128)(2,1)}), bf16[8,144,1536]{2,1,0:T(8,128)(2,1)S(1)}, u32[]{:S(2)}, u32[]{:S(2)}) async-start(bf16[8,144,1536]{2,1,0:T(8,128)(2,1)} %gate.38), calls=%async_computation.6 | async-start | bytes 7077888 | tf_op jit(solution)/shard_map/branch_rows/all_to_all | solution.py:878
  306.6 6.3 %give_gradn.1 = (f32[256,1664]{1,0:T(8,128)}, bf16[256,1664]{1,0:T(8,128)(2,1)}) custom-call(s32[2]{0:T(128)} %pad_add_fusion.at_ref, bf16[512,512]{1,0:T(8,128)(2,1)} %get-tuple-element.125.refs_0_, bf16[640,512]{1,0:T(8,128)(2,1)} %get-tuple-element.126.refs_1_, bf16[512,1664]{1,0:T(8,128)(2,1)} %get-tuple-element.148.refs_2_, ...), custom_call_target="tpu_custom_call" | custom-call | tf_op jit(solution)/shard_map/give_gradn/pallas_call | solution.py:279
  315.8 6.4 %middle_back.1 = (f32[256,1536]{1,0:T(8,128)}, bf16[256,1536]{1,0:T(8,128)(2,1)}, f32[1536,128]{1,0:T(8,128)}) custom-call(f32[256,1536]{1,0:T(8,128)} %get-tuple-element.124.middle, bf16[256,1536]{1,0:T(8,128)(2,1)} %get-tuple-element.127.own.normed, bf16[256,1536]{1,0:T(8,128)(2,1)} %grad_out.1, bf16[256,128]{1,0:T(8,128)(2,1)} %constant_dynamic-slice_fusion.code, ...), custom_call_target="tpu_custom_call" | custom-call | tf_op jit(solution)/shard_map/middle_back/pallas_call | solution.py:279
  324.9 20.9 %attend_back.1 = (f32[256,1536]{1,0:T(8,128)}, bf16[256,1536]{1,0:T(8,128)(2,1)}, bf16[2,96,1920]{2,1,0:T(8,128)(2,1)}, bf16[2,96,1920]{2,1,0:T(8,128)(2,1)}, bf...) custom-call(s32[2]{0:T(128)} %pad_add_fusion.at_ref, ...), custom_call_target="tpu_custom_call" | custom-call | tf_op jit(solution)/shard_map/attend_back/pallas_call | solution.py:279
  349.9 6.7 %collective-permute-done.27.refs_0_ = bf16[1,96,1920]{2,1,0:T(8,128)(2,1)S(1)} collective-permute-done((bf16[1,96,1920]{2,1,0:T(8,128)(2,1)}, bf16[1,96,1920]{2,1,0:T(8,128)(2,1)S(1)}, u32[]{:S(2)}, u32[]{:S(2)}) %collective-permute-start.27) | collective-permute-done | bytes 368672 | tf_op jit(solution)/shard_map/attn_last/ppermute | solution.py:45
  356.6 9.6 %collective-permute-done.28.refs_1_ = bf16[1,96,1920]{2,1,0:T(8,128)(2,1)} collective-permute-done((bf16[1,96,1920]{2,1,0:T(8,128)(2,1)}, bf16[1,96,1920]{2,1,0:T(8,128)(2,1)}, u32[]{:S(2)}, u32[]{:S(2)}) %collective-permute-start.28) | collective-permute-done | bytes 368672 | tf_op jit(solution)/shard_map/attn_last/ppermute | solution.py:45
  366.2 9.6 %collective-permute-start.30 = (bf16[1,96,1920]{2,1,0:T(8,128)(2,1)}, bf16[1,96,1920]{2,1,0:T(8,128)(2,1)S(1)}, u32[]{:S(2)}, u32[]{:S(2)}) collective-permute-start(bf16[1,96,1920]{2,1,0:T(8,128)(2,1)} %get-tuple-element.173), channel_id=1, source_target_pairs={{0,2},{2,0},{4,6},{6,4},{8,10},{10,8},{12,14},{14,12},{16,18},{18,... | collective-permute-start | bytes 1105928 | tf_op jit(solution)/shard_map/attn_far/ppermute | solution.py:45
  379.6 12.8 %collective-permute-done.34.refs_0_ = bf16[768,1152]{1,0:T(8,128)(2,1)} collective-permute-done((bf16[768,1152]{1,0:T(8,128)(2,1)}, bf16[768,1152]{1,0:T(8,128)(2,1)}, u32[]{:S(2)}, u32[]{:S(2)}) %collective-permute-start.34) | collective-permute-done | bytes 1769504 | tf_op jit(solution)/shard_map/expert_scatter/ppermute | solution.py:45
  392.3 4.6 add_convert_fusion.refs_5_
  403.0 5.3 %terms.1 = (bf16[2,96,1920]{2,1,0:T(8,128)(2,1)}, bf16[2,96,1920]{2,1,0:T(8,128)(2,1)}, bf16[2,96,1920]{2,1,0:T(8,128)(2,1)}) custom-call(bf16[2,96,1920]{2,1,0:T(8,128)(2,1)} %get-tuple-element.190.one, bf16[2,96,1920]{2,1,0:T(8,128)(2,1)} %get-tuple-element.191.two, bf16[2,96,1920]{2,1,0:T(8,128)(2,1)} %get-tuple-element.192.four, ...), custom_call_target="tpu_custom_call" | custom-call | tf_op jit(solution)/shard_map/attn_near/terms/pallas_call | solution.py:152
  409.4 4.6 all-to-all-start.7
  414.0 5.8 %give_branch.1 = (f32[256,1536]{1,0:T(8,128)}, bf16[256,1536]{1,0:T(8,128)(2,1)}) custom-call(s32[2]{0:T(128)} %pad_add_fusion.at_ref, bf16[512,512]{1,0:T(8,128)(2,1)} %get-tuple-element.125.refs_0_, bf16[640,512]{1,0:T(8,128)(2,1)} %get-tuple-element.126.refs_1_, bf16[8,144,1536]{2,1,0:T(8,128)(2,1)} %get-tuple-element.184.refs_2_), custom_call_target="tpu_custom_call" | custom-call | bytes 3000000 | tf_op jit(solution)/shard_map/give_branch/pallas_call | solution.py:279
  434.2 16.4 %collective-permute-done.39 = bf16[1,96,1920]{2,1,0:T(8,128)(2,1)S(1)} collective-permute-done((bf16[1,96,1920]{2,1,0:T(8,128)(2,1)S(1)}, bf16[1,96,1920]{2,1,0:T(8,128)(2,1)S(1)}, u32[]{:S(2)}, u32[]{:S(2)}) %collective-permute-start.39) | collective-permute-done | bytes 368672 | tf_op jit(solution)/shard_map/attn_outer/ppermute | solution.py:45
  450.7 9.2 %collective-permute-start.40 = (f32[96,128]{1,0:T(8,128)S(1)}, f32[96,128]{1,0:T(8,128)S(1)}, u32[]{:S(2)}, u32[]{:S(2)}) collective-permute-start(f32[96,128]{1,0:T(8,128)S(1)} %slice.91), channel_id=1, source_target_pairs={{0,1},{1,0},{2,3},{3,2},{4,5},{5,4},{6,7},{7,6},{8,9},{9,8},{10,11... | collective-permute-start | bytes 147464 | tf_op jit(solution)/shard_map/ppermute | solution.py:49
  (235 shorter events, 141.0 us)
Async XLA Ops:
  3.5 33.6 %all-to-all-start = ((bf16[8,96,1152]{2,1,0:T(8,128)(2,1)}), bf16[8,96,1152]{2,1,0:T(8,128)(2,1)S(1)}, u32[]{:S(2)}, u32[]{:S(2)}) async-start(bf16[8,96,1152]{2,1,0:T(8,128)(2,1)} %pad_maximum_fusion), calls=%async_computation | async-start | bytes 3538944 | tf_op jit(solution)/shard_map/all_to_all | solution.py:844
  8.3 28.8 %collective-permute-start.1 = (bf16[256,1536]{1,0:T(8,128)(2,1)}, bf16[256,1536]{1,0:T(8,128)(2,1)}, u32[]{:S(2)}, u32[]{:S(2)}) collective-permute-start(bf16[256,1536]{1,0:T(8,128)(2,1)} %grad_out.1), channel_id=1, source_target_pairs={{0,1},{1,0},{2,3},{3,2},{4,5},{5,4},{6,7},{7,6},{8,9},{9,8},{10,11... | collective-permute-start | bytes 2359304 | tf_op jit(solution)/shard_map/ppermute | solution.py:49
  9.6 27.5 %collective-permute-start = (bf16[256,1536]{1,0:T(8,128)(2,1)S(1)}, bf16[256,1536]{1,0:T(8,128)(2,1)S(1)}, u32[]{:S(2)}, u32[]{:S(2)}) collective-permute-start(bf16[256,1536]{1,0:T(8,128)(2,1)S(1)} %copy-done.6), channel_id=1, source_target_pairs={{0,1},{1,0},{2,3},{3,2},{4,5},{5,4},{6,7},{7,6},{8,9},{9,8},{10,11... | collective-permute-start | bytes 2359304 | tf_op jit(solution)/shard_map/ppermute | solution.py:49
  11.5 24.6 %collective-permute-start.2 = (bf16[1,96,1920]{2,1,0:T(8,128)(2,1)S(1)}, bf16[1,96,1920]{2,1,0:T(8,128)(2,1)S(1)}, u32[]{:S(2)}, u32[]{:S(2)}) collective-permute-start(bf16[1,96,1920]{2,1,0:T(8,128)(2,1)S(1)} %bitcast.56), channel_id=1, source_target_pairs={{0,16},{2,18},{4,20},{6,22},{8,24},{10,26},{12,28},{14,30},{16,0},... | collective-permute-start | bytes 1105928 | tf_op jit(solution)/shard_map/ppermute | solution.py:45
  38.6 32.1 %collective-permute-start.7 = (bf16[768,1152]{1,0:T(8,128)(2,1)}, bf16[768,1152]{1,0:T(8,128)(2,1)S(1)}, u32[]{:S(2)}, u32[]{:S(2)}) collective-permute-start(bf16[768,1152]{1,0:T(8,128)(2,1)} %get-tuple-element.110), channel_id=1, source_target_pairs={{0,1},{1,0},{2,3},{3,2},{4,5},{5,4},{6,7},{7,6},{8,9},{9,8},{10,11... | collective-permute-start | bytes 5308424 | tf_op jit(solution)/shard_map/ppermute | solution.py:49
  40.5 29.2 %collective-permute-start.3 = (bf16[2,96,1920]{2,1,0:T(8,128)(2,1)}, bf16[2,96,1920]{2,1,0:T(8,128)(2,1)}, u32[]{:S(2)}, u32[]{:S(2)}) collective-permute-start(bf16[2,96,1920]{2,1,0:T(8,128)(2,1)} %get-tuple-element.109.refs_1_.refs_0_), channel_id=1, source_target_pairs={{0,2},{2,0},{4,6},{6,4},{8,10},{10,8},{12,14},{14,12},{16,18},{18,... | collective-permute-start | bytes 2211848 | tf_op jit(solution)/shard_map/weights_near/ppermute | solution.py:45
  40.5 29.2 %collective-permute-start.4 = (bf16[2,96,1920]{2,1,0:T(8,128)(2,1)}, bf16[2,96,1920]{2,1,0:T(8,128)(2,1)}, u32[]{:S(2)}, u32[]{:S(2)}) collective-permute-start(bf16[2,96,1920]{2,1,0:T(8,128)(2,1)} %get-tuple-element.109.refs_1_.refs_0_), channel_id=1, source_target_pairs={{0,4},{2,6},{4,0},{6,2},{8,12},{10,14},{12,8},{14,10},{16,20},{18,... | collective-permute-start | bytes 2211848 | tf_op jit(solution)/shard_map/weights_near/ppermute | solution.py:45
  41.6 29.1 %collective-permute-start.5 = (bf16[2,96,1920]{2,1,0:T(8,128)(2,1)}, bf16[2,96,1920]{2,1,0:T(8,128)(2,1)}, u32[]{:S(2)}, u32[]{:S(2)}) collective-permute-start(bf16[2,96,1920]{2,1,0:T(8,128)(2,1)} %get-tuple-element.109.refs_1_.refs_0_), channel_id=1, source_target_pairs={{0,8},{2,10},{4,12},{6,14},{8,0},{10,2},{12,4},{14,6},{16,24},{18,... | collective-permute-start | bytes 2211848 | tf_op jit(solution)/shard_map/weights_near/ppermute | solution.py:45
  50.0 19.7 %collective-permute-start.6 = (bf16[1,160,1152]{2,1,0:T(8,128)(2,1)}, bf16[1,160,1152]{2,1,0:T(8,128)(2,1)}, u32[]{:S(2)}, u32[]{:S(2)}) collective-permute-start(bf16[1,160,1152]{2,1,0:T(8,128)(2,1)} %bitcast.53), channel_id=1, source_target_pairs={{0,16},{2,18},{4,20},{6,22},{8,24},{10,26},{12,28},{14,30},{16,0},... | collective-permute-start | bytes 1105928 | tf_op jit(solution)/shard_map/ppermute | solution.py:45
  72.0 28.6 %collective-permute-start.12 = (bf16[1,256,1152]{2,1,0:T(8,128)(2,1)}, bf16[1,256,1152]{2,1,0:T(8,128)(2,1)S(1)}, u32[]{:S(2)}, u32[]{:S(2)}) collective-permute-start(bf16[1,256,1152]{2,1,0:T(8,128)(2,1)} %bitcast.49), channel_id=1, source_target_pairs={{0,16},{2,18},{4,20},{6,22},{8,24},{10,26},{12,28},{14,30},{16,0},... | collective-permute-start | bytes 1769480 | tf_op jit(solution)/shard_map/ppermute | solution.py:45
  75.5 26.4 %collective-permute-start.10 = (bf16[2,96,1920]{2,1,0:T(8,128)(2,1)}, bf16[2,96,1920]{2,1,0:T(8,128)(2,1)}, u32[]{:S(2)}, u32[]{:S(2)}) collective-permute-start(bf16[2,96,1920]{2,1,0:T(8,128)(2,1)} %get-tuple-element.113.refs_4_), channel_id=1, source_target_pairs={{0,4},{2,6},{4,0},{6,2},{8,12},{10,14},{12,8},{14,10},{16,20},{18,... | collective-permute-start | bytes 2211848 | tf_op jit(solution)/shard_map/weights_far/ppermute | solution.py:45
  75.8 26.1 %collective-permute-start.11 = (bf16[2,96,1920]{2,1,0:T(8,128)(2,1)}, bf16[2,96,1920]{2,1,0:T(8,128)(2,1)}, u32[]{:S(2)}, u32[]{:S(2)}) collective-permute-start(bf16[2,96,1920]{2,1,0:T(8,128)(2,1)} %get-tuple-element.113.refs_4_), channel_id=1, source_target_pairs={{0,2},{2,0},{4,6},{6,4},{8,10},{10,8},{12,14},{14,12},{16,18},{18,... | collective-permute-start | bytes 2211848 | tf_op jit(solution)/shard_map/weights_far/ppermute | solution.py:45
  79.3 22.6 %collective-permute-start.8 = (bf16[1,96,1920]{2,1,0:T(8,128)(2,1)S(1)}, bf16[1,96,1920]{2,1,0:T(8,128)(2,1)S(1)}, u32[]{:S(2)}, u32[]{:S(2)}) collective-permute-start(bf16[1,96,1920]{2,1,0:T(8,128)(2,1)S(1)} %slice.68), channel_id=1, source_target_pairs={{0,2},{2,0},{4,6},{6,4},{8,10},{10,8},{12,14},{14,12},{16,18},{18,... | collective-permute-start | bytes 1105928 | tf_op jit(solution)/shard_map/weights_far/ppermute | solution.py:45
  79.4 22.5 %collective-permute-start.9 = (bf16[1,96,1920]{2,1,0:T(8,128)(2,1)S(1)}, bf16[1,96,1920]{2,1,0:T(8,128)(2,1)}, u32[]{:S(2)}, u32[]{:S(2)}) collective-permute-start(bf16[1,96,1920]{2,1,0:T(8,128)(2,1)S(1)} %slice.69), channel_id=1, source_target_pairs={{0,4},{2,6},{4,0},{6,2},{8,12},{10,14},{12,8},{14,10},{16,20},{18,... | collective-permute-start | bytes 1105928 | tf_op jit(solution)/shard_map/weights_far/ppermute | solution.py:45
  117.4 57.2 %all-to-all-start.1 = ((bf16[8,144,1664]{2,1,0:T(8,128)(2,1)}), bf16[8,144,1664]{2,1,0:T(8,128)(2,1)}, u32[]{:S(2)}, u32[]{:S(2)}) async-start(bf16[8,144,1664]{2,1,0:T(8,128)(2,1)} %get-tuple-element.130), calls=%async_computation.1 | async-start | bytes 7667712 | tf_op jit(solution)/shard_map/grads_rows/all_to_all | solution.py:878
  146.2 26.5 %collective-permute-start.19 = (bf16[1,128,1152]{2,1,0:T(8,128)(2,1)}, bf16[1,128,1152]{2,1,0:T(8,128)(2,1)S(1)}, u32[]{:S(2)}, u32[]{:S(2)}) collective-permute-start(bf16[1,128,1152]{2,1,0:T(8,128)(2,1)} %bitcast.54), channel_id=1, source_target_pairs={{0,16},{2,18},{4,20},{6,22},{8,24},{10,26},{12,28},{14,30},{16,0},... | collective-permute-start | bytes 884744 | tf_op jit(solution)/shard_map/ppermute | solution.py:45
  174.7 32.2 %all-to-all-start.2 = ((bf16[8,64,1536]{2,1,0:T(8,128)(2,1)}), bf16[8,64,1536]{2,1,0:T(8,128)(2,1)S(1)}, u32[]{:S(2)}, u32[]{:S(2)}) async-start(bf16[8,64,1536]{2,1,0:T(8,128)(2,1)} %bitcast.47), calls=%async_computation.2 | async-start | bytes 3145728 | tf_op jit(solution)/shard_map/tokens_rows/all_to_all | solution.py:878
  179.5 24.9 %collective-permute-start.20 = (bf16[1,224,1152]{2,1,0:T(8,128)(2,1)}, bf16[1,224,1152]{2,1,0:T(8,128)(2,1)S(1)}, u32[]{:S(2)}, u32[]{:S(2)}) collective-permute-start(bf16[1,224,1152]{2,1,0:T(8,128)(2,1)} %bitcast.51), channel_id=1, source_target_pairs={{0,16},{2,18},{4,20},{6,22},{8,24},{10,26},{12,28},{14,30},{16,0},... | collective-permute-start | bytes 1548296 | tf_op jit(solution)/shard_map/ppermute | solution.py:45
  208.1 29.6 %all-to-all-start.3 = ((bf16[8,80,1536]{2,1,0:T(8,128)(2,1)}), bf16[8,80,1536]{2,1,0:T(8,128)(2,1)S(1)}, u32[]{:S(2)}, u32[]{:S(2)}) async-start(bf16[8,80,1536]{2,1,0:T(8,128)(2,1)} %bitcast.48), calls=%async_computation.3 | async-start | bytes 3932160 | tf_op jit(solution)/shard_map/tokens_rows/all_to_all | solution.py:878
  238.9 26.4 %all-to-all-start.5 = ((bf16[8,64,1664]{2,1,0:T(8,128)(2,1)}), bf16[8,64,1664]{2,1,0:T(8,128)(2,1)}, u32[]{:S(2)}, u32[]{:S(2)}) async-start(bf16[8,64,1664]{2,1,0:T(8,128)(2,1)} %bitcast.52), calls=%async_computation.5 | async-start | bytes 3407872 | tf_op jit(solution)/shard_map/gradn_rows/all_to_all | solution.py:878
  265.3 34.9 %all-to-all-start.4 = ((bf16[8,80,1664]{2,1,0:T(8,128)(2,1)}), bf16[8,80,1664]{2,1,0:T(8,128)(2,1)S(1)}, u32[]{:S(2)}, u32[]{:S(2)}) async-start(bf16[8,80,1664]{2,1,0:T(8,128)(2,1)} %bitcast.50), calls=%async_computation.4 | async-start | bytes 4259840 | tf_op jit(solution)/shard_map/gradn_rows/all_to_all | solution.py:878
  301.6 99.6 %all-to-all-start.6 = ((bf16[8,144,1536]{2,1,0:T(8,128)(2,1)}), bf16[8,144,1536]{2,1,0:T(8,128)(2,1)S(1)}, u32[]{:S(2)}, u32[]{:S(2)}) async-start(bf16[8,144,1536]{2,1,0:T(8,128)(2,1)} %gate.38), calls=%async_computation.6 | async-start | bytes 7077888 | tf_op jit(solution)/shard_map/branch_rows/all_to_all | solution.py:878
  313.5 32.7 %collective-permute-start.26 = (bf16[768,1152]{1,0:T(8,128)(2,1)}, bf16[768,1152]{1,0:T(8,128)(2,1)}, u32[]{:S(2)}, u32[]{:S(2)}) collective-permute-start(bf16[768,1152]{1,0:T(8,128)(2,1)} %get-tuple-element.167), channel_id=1, source_target_pairs={{0,1},{1,0},{2,3},{3,2},{4,5},{5,4},{6,7},{7,6},{8,9},{9,8},{10,11... | collective-permute-start | bytes 5308424 | tf_op jit(solution)/shard_map/ppermute | solution.py:49
  313.5 78.8 %collective-permute-start.34 = (bf16[768,1152]{1,0:T(8,128)(2,1)}, bf16[768,1152]{1,0:T(8,128)(2,1)}, u32[]{:S(2)}, u32[]{:S(2)}) collective-permute-start(bf16[768,1152]{1,0:T(8,128)(2,1)} %add_convert_fusion.1.refs_2_), channel_id=1, source_target_pairs={{0,16},{2,18},{4,20},{6,22},{8,24},{10,26},{12,28},{14,30},{16,0},... | collective-permute-start | bytes 5308424 | tf_op jit(solution)/shard_map/expert_scatter/ppermute | solution.py:45
  345.8 20.4 %collective-permute-start.29 = (bf16[256,1536]{1,0:T(8,128)(2,1)}, bf16[256,1536]{1,0:T(8,128)(2,1)}, u32[]{:S(2)}, u32[]{:S(2)}) collective-permute-start(bf16[256,1536]{1,0:T(8,128)(2,1)} %get-tuple-element.172), channel_id=1, source_target_pairs={{0,1},{1,0},{2,3},{3,2},{4,5},{5,4},{6,7},{7,6},{8,9},{9,8},{10,11... | collective-permute-start | bytes 2359304 | tf_op jit(solution)/shard_map/ppermute | solution.py:49
  346.2 19.9 %collective-permute-start.28 = (bf16[1,96,1920]{2,1,0:T(8,128)(2,1)}, bf16[1,96,1920]{2,1,0:T(8,128)(2,1)}, u32[]{:S(2)}, u32[]{:S(2)}) collective-permute-start(bf16[1,96,1920]{2,1,0:T(8,128)(2,1)} %get-tuple-element.169), channel_id=1, source_target_pairs={{0,4},{2,6},{4,0},{6,2},{8,12},{10,14},{12,8},{14,10},{16,20},{18,... | collective-permute-start | bytes 1105928 | tf_op jit(solution)/shard_map/attn_last/ppermute | solution.py:45
  366.2 32.3 %collective-permute-start.30 = (bf16[1,96,1920]{2,1,0:T(8,128)(2,1)}, bf16[1,96,1920]{2,1,0:T(8,128)(2,1)S(1)}, u32[]{:S(2)}, u32[]{:S(2)}) collective-permute-start(bf16[1,96,1920]{2,1,0:T(8,128)(2,1)} %get-tuple-element.173), channel_id=1, source_target_pairs={{0,2},{2,0},{4,6},{6,4},{8,10},{10,8},{12,14},{14,12},{16,18},{18,... | collective-permute-start | bytes 1105928 | tf_op jit(solution)/shard_map/attn_far/ppermute | solution.py:45
  375.8 22.8 %collective-permute-start.31 = (bf16[1,96,1920]{2,1,0:T(8,128)(2,1)}, bf16[1,96,1920]{2,1,0:T(8,128)(2,1)}, u32[]{:S(2)}, u32[]{:S(2)}) collective-permute-start(bf16[1,96,1920]{2,1,0:T(8,128)(2,1)} %get-tuple-element.174), channel_id=1, source_target_pairs={{0,4},{2,6},{4,0},{6,2},{8,12},{10,14},{12,8},{14,10},{16,20},{18,... | collective-permute-start | bytes 1105928 | tf_op jit(solution)/shard_map/attn_far/ppermute | solution.py:45
  378.7 22.6 %collective-permute-start.32 = (bf16[2,96,1920]{2,1,0:T(8,128)(2,1)}, bf16[2,96,1920]{2,1,0:T(8,128)(2,1)}, u32[]{:S(2)}, u32[]{:S(2)}) collective-permute-start(bf16[2,96,1920]{2,1,0:T(8,128)(2,1)} %get-tuple-element.179.refs_2_), channel_id=1, source_target_pairs={{0,4},{2,6},{4,0},{6,2},{8,12},{10,14},{12,8},{14,10},{16,20},{18,... | collective-permute-start | bytes 2211848 | tf_op jit(solution)/shard_map/attn_far/ppermute | solution.py:45
  379.5 21.7 %collective-permute-start.33 = (bf16[2,96,1920]{2,1,0:T(8,128)(2,1)}, bf16[2,96,1920]{2,1,0:T(8,128)(2,1)}, u32[]{:S(2)}, u32[]{:S(2)}) collective-permute-start(bf16[2,96,1920]{2,1,0:T(8,128)(2,1)} %get-tuple-element.180.refs_3_), channel_id=1, source_target_pairs={{0,2},{2,0},{4,6},{6,4},{8,10},{10,8},{12,14},{14,12},{16,18},{18,... | collective-permute-start | bytes 2211848 | tf_op jit(solution)/shard_map/attn_far/ppermute | solution.py:45
  409.4 53.4 %all-to-all-start.7 = ((bf16[8,96,1152]{2,1,0:T(8,128)(2,1)}), bf16[8,96,1152]{2,1,0:T(8,128)(2,1)S(1)}, u32[]{:S(2)}, u32[]{:S(2)}) async-start(bf16[8,96,1152]{2,1,0:T(8,128)(2,1)} %bitcast.29), calls=%async_computation.7 | async-start | bytes 3538944 | tf_op jit(solution)/shard_map/expert_scatter/all_to_all | solution.py:878
  430.4 20.2 %collective-permute-start.39 = (bf16[1,96,1920]{2,1,0:T(8,128)(2,1)S(1)}, bf16[1,96,1920]{2,1,0:T(8,128)(2,1)S(1)}, u32[]{:S(2)}, u32[]{:S(2)}) collective-permute-start(bf16[1,96,1920]{2,1,0:T(8,128)(2,1)S(1)} %slice.112), channel_id=1, source_target_pairs={{0,16},{2,18},{4,20},{6,22},{8,24},{10,26},{12,28},{14,30},{16,0},... | collective-permute-start | bytes 1105928 | tf_op jit(solution)/shard_map/attn_outer/ppermute | solution.py:45
  (57 other events, 368.9 us)

commit v5 on v4

--- a/solution.py
+++ b/solution.py
@@ -144,7 +144,7 @@
 def near_terms(parts, got):
     args = [parts[bit] for bit in NEAR] + [got[k] for k in (6, 5, 3, 9)]
     shape = parts[1].shape
-    grid = 6 if shape[1] % 96 == 0 else 1
+    grid = 2 if shape[1] % 32 == 0 else 1
 
     def spec(dims):
         return pl.BlockSpec((dims[0], dims[1] // grid, dims[2]), lambda i: (0, i, 0))
@@ -882,9 +882,11 @@
     sine_table = jnp.concatenate([-sine_table, sine_table], axis=1)
     seg_col, seg_row = segment_ids[:, None], segment_ids[None, :]
 
-    pair, expert_rows = gate([pair, expert_rows], cosine, sine_table, hidden_other, grad_other)
+    pair, expert_rows, code_own = gate(
+        [pair, expert_rows, code_own], cosine, sine_table, hidden_other, grad_other
+    )
     if count == 2 * CUBE:
-        edges = [expert_rows.shape[0] * k // 48 // 16 * 16 for k in (0, 10, 26, 26, 34, 48)]
+        edges = [expert_rows.shape[0] * k // 48 // 16 * 16 for k in (0, 10, 26, 26, 37, 48)]
     else:
         edges = [0] * 5 + [expert_rows.shape[0]]
     pieces = [(expert_rows[None], 0, 0, 0), (swap_core(expert_rows)[None], 0, 0, 1)]

time: 473 us -> 472 us (level)
    unnamed x87 -> x89, local copies, waits for them, and re-layouts: 17.2 us -> 18.9 us
    slice x8 -> x7, local copies, waits for them, and re-layouts: 9.71 us -> 9.11 us  [cut(): return lax.slice_in_dim(values, span[0], span[1], axis=axis)]
  transfers between devices with their start and end apart: 49 -> 49, of which waited for: 22 -> 21; matrix products, arithmetic and copies ran while one was open for 10% -> 11% of each run, Pallas kernels for 28% -> 28%
where the time goes in v5:
time: 472 us; the launch traced here: 464 us
  waiting for transfers between devices  154 us (33%)
  Pallas kernels  135 us (29%)
  starting transfers between devices  101 us (21%)
  local copies, waits for them, and re-layouts  39.2 us (8%)
  other arithmetic  32.9 us (7%)
    ppermute x25, waiting for transfers between devices, swap(): return lax.ppermute(values, 'dp', [(i, i ^ bit) for i in range(count)])  142 us
    pallas_call x8, Pallas kernels, vmem_call(): pl.pallas_call(kernel, out_shape=out_shapes, in_specs=[pl.BlockSpec(memor...  68.5 us
    pallas_call x2, Pallas kernels, moe(): pl.pallas_call(functools.partial(moe_kernel, (copies, hidden, blocks, out...  38.7 us
    all_to_all x7, starting transfers between devices, exchange(): lax.all_to_all(rows, 'dp', 0, 0, tiled=True, axis_index_groups=groups)  33.4 us
    ppermute x25, starting transfers between devices, swap(): return lax.ppermute(values, 'dp', [(i, i ^ bit) for i in range(count)])  31.6 us
    ppermute x16, starting transfers between devices, swap_core(): return lax.ppermute(values, 'tensor', [(0, 1), (1, 0)])  31.4 us
    pallas_call x2, Pallas kernels, weight_grads(): pl.pallas_call(functools.partial(weight_grads_kernel, len(pre)), out_shap...  21.1 us
    unnamed x89, local copies, waits for them, and re-layouts  18.9 us
  transfers between devices with their start and end apart: 49, of which 21 were waited for; matrix products, arithmetic and copies ran while one was open for 11% of the time, Pallas kernels for 28%

profile of v5, /device:TPU:3, one launch (start us, length us, event | category | flops | bytes accessed | tf_op | source)
XLA Modules:
  0.0 464.5 jit_solution(16171257787994431892)
XLA Ops:
  3.5 4.8 %all-to-all-start = ((bf16[8,96,1152]{2,1,0:T(8,128)(2,1)}), bf16[8,96,1152]{2,1,0:T(8,128)(2,1)S(1)}, u32[]{:S(2)}, u32[]{:S(2)}) async-start(bf16[8,96,1152]{2,1,0:T(8,128)(2,1)} %pad_maximum_fusion), calls=%async_computation | async-start | bytes 3538944 | tf_op jit(solution)/shard_map/all_to_all | solution.py:844
  26.0 10.2 %collective-permute-done.2 = bf16[1,96,1920]{2,1,0:T(8,128)(2,1)} collective-permute-done((bf16[1,96,1920]{2,1,0:T(8,128)(2,1)}, bf16[1,96,1920]{2,1,0:T(8,128)(2,1)}, u32[]{:S(2)}, u32[]{:S(2)}) %collective-permute-start.2) | collective-permute-done | bytes 368672 | tf_op jit(solution)/shard_map/ppermute | solution.py:45
  49.5 6.7 %slots.1 = (bf16[512,512]{1,0:T(8,128)(2,1)}, bf16[640,512]{1,0:T(8,128)(2,1)}, bf16[8,144,1664]{2,1,0:T(8,128)(2,1)}) custom-call(s32[2]{0:T(128)} %pad_add_fusion.at_ref, s32[512,8]{1,0:T(8,128)} %copy.104.order_col, s32[8,512]{1,0:T(8,128)} %bitcast.57, bf16[256,1536]{1,0:T(8,128)(2,1)} %grad_out.1, ...), custom_call_target="tpu_custom_call" | custom-call | bytes 3000000 | tf_op jit(solution)/shard_map/slots/pallas_call | solution.py:279
  57.1 13.9 %collective-permute-done.6.refs_4_.refs_2_.refs_3_ = bf16[1,160,1152]{2,1,0:T(8,128)(2,1)} collective-permute-done((bf16[1,160,1152]{2,1,0:T(8,128)(2,1)}, bf16[1,160,1152]{2,1,0:T(8,128)(2,1)}, u32[]{:S(2)}, u32[]{:S(2)}) %collective-permute-start.6) | collective-permute-done | bytes 368672 | tf_op jit(solution)/shard_map/ppermute | solution.py:45
  81.9 20.1 %collective-permute-done.12.refs_4_.refs_5_ = bf16[1,256,1152]{2,1,0:T(8,128)(2,1)S(1)} collective-permute-done((bf16[1,256,1152]{2,1,0:T(8,128)(2,1)}, bf16[1,256,1152]{2,1,0:T(8,128)(2,1)S(1)}, u32[]{:S(2)}, u32[]{:S(2)}) %collective-permute-start.12) | collective-permute-done | bytes 589856 | tf_op jit(solution)/shard_map/ppermute | solution.py:45
  110.7 4.4 collective-permute-done.14.refs_0_
  118.7 4.7 %all-to-all-start.1 = ((bf16[8,144,1664]{2,1,0:T(8,128)(2,1)}), bf16[8,144,1664]{2,1,0:T(8,128)(2,1)}, u32[]{:S(2)}, u32[]{:S(2)}) async-start(bf16[8,144,1664]{2,1,0:T(8,128)(2,1)} %get-tuple-element.132), calls=%async_computation.1 | async-start | bytes 7667712 | tf_op jit(solution)/shard_map/grads_rows/all_to_all | solution.py:878
  123.4 13.7 %attend.1 = (bf16[512,1536]{1,0:T(8,128)(2,1)}, bf16[512,1536]{1,0:T(8,128)(2,1)}, bf16[512,768]{1,0:T(8,128)(2,1)}, bf16[512,128]{1,0:T(8,128)(2,1)}, bf16[512,...) custom-call(s32[2]{0:T(128)} %pad_add_fusion.at_ref, ...), custom_call_target="tpu_custom_call" | custom-call | tf_op jit(solution)/shard_map/attend/pallas_call | solution.py:279
  149.6 5.1 %take.1 = (bf16[512,1536]{1,0:T(8,128)(2,1)}, bf16[640,1536]{1,0:T(8,128)(2,1)}) custom-call(s32[2]{0:T(128)} %pad_add_fusion.at_ref, bf16[256,1536]{1,0:T(8,128)(2,1)} %get-tuple-element.128.own.normed, bf16[256,1536]{1,0:T(8,128)(2,1)} %copy-done.30, bf16[512,512]{1,0:T(8,128)(2,1)} %get-tuple-element.126.refs_0_, bf16[640,512]{1,0:T(8,128)(2,1)} %get-tuple-element.127.refs_1_), custom_call_target="tpu_custom_call" | custom-call | tf_op jit(solution)/shard_map/take/pallas_call | solution.py:279
  154.7 21.5 %collective-permute-done.19.refs_2_.refs_6_.refs_7_ = bf16[1,176,1152]{2,1,0:T(8,128)(2,1)S(1)} collective-permute-done((bf16[1,176,1152]{2,1,0:T(8,128)(2,1)}, bf16[1,176,1152]{2,1,0:T(8,128)(2,1)S(1)}, u32[]{:S(2)}, u32[]{:S(2)}) %collective-permute-start.19) | collective-permute-done | bytes 405536 | tf_op jit(solution)/shard_map/ppermute | solution.py:45
  187.4 18.3 %collective-permute-done.20.refs_2_.refs_8_.refs_9_ = bf16[1,176,1152]{2,1,0:T(8,128)(2,1)S(1)} collective-permute-done((bf16[1,176,1152]{2,1,0:T(8,128)(2,1)}, bf16[1,176,1152]{2,1,0:T(8,128)(2,1)S(1)}, u32[]{:S(2)}, u32[]{:S(2)}) %collective-permute-start.20) | collective-permute-done | bytes 405536 | tf_op jit(solution)/shard_map/ppermute | solution.py:45
  208.7 5.3 %all-to-all-start.3 = ((bf16[8,80,1536]{2,1,0:T(8,128)(2,1)}), bf16[8,80,1536]{2,1,0:T(8,128)(2,1)S(1)}, u32[]{:S(2)}, u32[]{:S(2)}) async-start(bf16[8,80,1536]{2,1,0:T(8,128)(2,1)} %bitcast.48), calls=%async_computation.3 | async-start | bytes 3932160 | tf_op jit(solution)/shard_map/tokens_rows/all_to_all | solution.py:878
  214.0 4.5 collective-permute-start.22
  220.6 17.8 %experts.2 = (bf16[8,144,1536]{2,1,0:T(8,128)(2,1)}, bf16[512,1664]{1,0:T(8,128)(2,1)}, bf16[512,768]{1,0:T(8,128)(2,1)}, bf16[512,1536]{1,0:T(8,128)(2,1)}, bf16[512,1536]{1,0:T(8,128)(2,1)}) custom-call(s32[2]{0:T(128)} %pad_add_fusion.at_ref, bf16[1536,128]{1,0:T(8,128)(2,1)} %get-tuple-element.130.router_ref.router, ...), custom_call_target="tpu_custom_call" | custom-call | bytes 3000000 | tf_op jit(solution)/shard_map/experts/pallas_call | solution.py:700
  238.4 5.1 %all-to-all-start.5 = ((bf16[8,64,1664]{2,1,0:T(8,128)(2,1)}), bf16[8,64,1664]{2,1,0:T(8,128)(2,1)}, u32[]{:S(2)}, u32[]{:S(2)}) async-start(bf16[8,64,1664]{2,1,0:T(8,128)(2,1)} %bitcast.51), calls=%async_computation.5 | async-start | bytes 3407872 | tf_op jit(solution)/shard_map/gradn_rows/all_to_all | solution.py:878
  244.4 20.9 %experts.3 = (bf16[8,144,1536]{2,1,0:T(8,128)(2,1)}, bf16[640,1664]{1,0:T(8,128)(2,1)}, bf16[640,768]{1,0:T(8,128)(2,1)}, bf16[640,1536]{1,0:T(8,128)(2,1)}, bf16[640,1536]{1,0:T(8,128)(2,1)}) custom-call(s32[2]{0:T(128)} %pad_add_fusion.at_ref, bf16[1536,128]{1,0:T(8,128)(2,1)} %gate.32.router_ref, ...), custom_call_target="tpu_custom_call", output_to_operand_aliasing={{0}: (4, {})} | custom-call | bytes 3000000 | tf_op jit(solution)/shard_map/experts/pallas_call | solution.py:700
  265.2 4.7 %all-to-all-start.4 = ((bf16[8,80,1664]{2,1,0:T(8,128)(2,1)}), bf16[8,80,1664]{2,1,0:T(8,128)(2,1)S(1)}, u32[]{:S(2)}, u32[]{:S(2)}) async-start(bf16[8,80,1664]{2,1,0:T(8,128)(2,1)} %bitcast.50), calls=%async_computation.4 | async-start | bytes 4259840 | tf_op jit(solution)/shard_map/gradn_rows/all_to_all | solution.py:878
  271.8 10.5 %weight_grads.2 = (bf16[768,1152]{1,0:T(8,128)(2,1)}, bf16[768,1152]{1,0:T(8,128)(2,1)}) custom-call(s32[3]{0:T(128)} %pad_add_fusion.1.at_ref, bf16[512,1536]{1,0:T(8,128)(2,1)} %get-tuple-element.135.x_in.refs_0_, bf16[640,1536]{1,0:T(8,128)(2,1)} %bitcast.42, bf16[512,1536]{1,0:T(8,128)(2,1)} %get-tuple-element.143.refs_2_, ...), custom_call_target="tpu_custom_call" | custom-call | tf_op jit(solution)/shard_map/weight_grads/pallas_call | solution.py:769
  286.0 10.6 %weight_grads.3 = (bf16[768,1152]{1,0:T(8,128)(2,1)}, bf16[768,1152]{1,0:T(8,128)(2,1)}) custom-call(s32[3]{0:T(128)} %pad_add_fusion.3.at_ref, bf16[512,1536]{1,0:T(8,128)(2,1)} %get-tuple-element.135.x_in.refs_0_, bf16[640,1536]{1,0:T(8,128)(2,1)} %bitcast.43, bf16[512,1536]{1,0:T(8,128)(2,1)} %get-tuple-element.143.refs_2_, ...), custom_call_target="tpu_custom_call" | custom-call | tf_op jit(solution)/shard_map/weight_grads/pallas_call | solution.py:769
  301.6 4.7 %all-to-all-start.6 = ((bf16[8,144,1536]{2,1,0:T(8,128)(2,1)}), bf16[8,144,1536]{2,1,0:T(8,128)(2,1)S(1)}, u32[]{:S(2)}, u32[]{:S(2)}) async-start(bf16[8,144,1536]{2,1,0:T(8,128)(2,1)} %gate.38), calls=%async_computation.6 | async-start | bytes 7077888 | tf_op jit(solution)/shard_map/branch_rows/all_to_all | solution.py:878
  306.3 6.3 %give_gradn.1 = (f32[256,1664]{1,0:T(8,128)}, bf16[256,1664]{1,0:T(8,128)(2,1)}) custom-call(s32[2]{0:T(128)} %pad_add_fusion.at_ref, bf16[512,512]{1,0:T(8,128)(2,1)} %get-tuple-element.126.refs_0_, bf16[640,512]{1,0:T(8,128)(2,1)} %get-tuple-element.127.refs_1_, bf16[512,1664]{1,0:T(8,128)(2,1)} %get-tuple-element.150.refs_2_, ...), custom_call_target="tpu_custom_call" | custom-call | tf_op jit(solution)/shard_map/give_gradn/pallas_call | solution.py:279
  315.5 6.4 %middle_back.1 = (f32[256,1536]{1,0:T(8,128)}, bf16[256,1536]{1,0:T(8,128)(2,1)}, f32[1536,128]{1,0:T(8,128)}) custom-call(f32[256,1536]{1,0:T(8,128)} %get-tuple-element.125.middle, bf16[256,1536]{1,0:T(8,128)(2,1)} %get-tuple-element.128.own.normed, bf16[256,1536]{1,0:T(8,128)(2,1)} %grad_out.1, bf16[256,128]{1,0:T(8,128)(2,1)} %get-tuple-element.129.code, ...), custom_call_target="tpu_custom_call" | custom-call | tf_op jit(solution)/shard_map/middle_back/pallas_call | solution.py:279
  324.6 20.9 %attend_back.1 = (f32[256,1536]{1,0:T(8,128)}, bf16[256,1536]{1,0:T(8,128)(2,1)}, bf16[2,96,1920]{2,1,0:T(8,128)(2,1)}, bf16[2,96,1920]{2,1,0:T(8,128)(2,1)}, bf...) custom-call(s32[2]{0:T(128)} %pad_add_fusion.at_ref, ...), custom_call_target="tpu_custom_call" | custom-call | tf_op jit(solution)/shard_map/attend_back/pallas_call | solution.py:279
  349.6 6.8 %collective-permute-done.27.refs_0_ = bf16[1,96,1920]{2,1,0:T(8,128)(2,1)S(1)} collective-permute-done((bf16[1,96,1920]{2,1,0:T(8,128)(2,1)}, bf16[1,96,1920]{2,1,0:T(8,128)(2,1)S(1)}, u32[]{:S(2)}, u32[]{:S(2)}) %collective-permute-start.27) | collective-permute-done | bytes 368672 | tf_op jit(solution)/shard_map/attn_last/ppermute | solution.py:45
  356.5 9.9 %collective-permute-done.28.refs_1_ = bf16[1,96,1920]{2,1,0:T(8,128)(2,1)} collective-permute-done((bf16[1,96,1920]{2,1,0:T(8,128)(2,1)}, bf16[1,96,1920]{2,1,0:T(8,128)(2,1)}, u32[]{:S(2)}, u32[]{:S(2)}) %collective-permute-start.28) | collective-permute-done | bytes 368672 | tf_op jit(solution)/shard_map/attn_last/ppermute | solution.py:45
  366.4 9.6 %collective-permute-start.30 = (bf16[1,96,1920]{2,1,0:T(8,128)(2,1)}, bf16[1,96,1920]{2,1,0:T(8,128)(2,1)S(1)}, u32[]{:S(2)}, u32[]{:S(2)}) collective-permute-start(bf16[1,96,1920]{2,1,0:T(8,128)(2,1)} %get-tuple-element.175), channel_id=1, source_target_pairs={{0,2},{2,0},{4,6},{6,4},{8,10},{10,8},{12,14},{14,12},{16,18},{18,... | collective-permute-start | bytes 1105928 | tf_op jit(solution)/shard_map/attn_far/ppermute | solution.py:45
  379.9 12.2 %collective-permute-done.34.refs_0_ = bf16[768,1152]{1,0:T(8,128)(2,1)} collective-permute-done((bf16[768,1152]{1,0:T(8,128)(2,1)}, bf16[768,1152]{1,0:T(8,128)(2,1)}, u32[]{:S(2)}, u32[]{:S(2)}) %collective-permute-start.34) | collective-permute-done | bytes 1769504 | tf_op jit(solution)/shard_map/expert_scatter/ppermute | solution.py:45
  392.0 4.5 add_convert_fusion.refs_5_
  407.8 4.6 all-to-all-start.7
  412.3 5.8 %give_branch.1 = (f32[256,1536]{1,0:T(8,128)}, bf16[256,1536]{1,0:T(8,128)(2,1)}) custom-call(s32[2]{0:T(128)} %pad_add_fusion.at_ref, bf16[512,512]{1,0:T(8,128)(2,1)} %get-tuple-element.126.refs_0_, bf16[640,512]{1,0:T(8,128)(2,1)} %get-tuple-element.127.refs_1_, bf16[8,144,1536]{2,1,0:T(8,128)(2,1)} %get-tuple-element.186.refs_2_), custom_call_target="tpu_custom_call" | custom-call | bytes 3000000 | tf_op jit(solution)/shard_map/give_branch/pallas_call | solution.py:279
  432.4 16.5 %collective-permute-done.39 = bf16[1,96,1920]{2,1,0:T(8,128)(2,1)S(1)} collective-permute-done((bf16[1,96,1920]{2,1,0:T(8,128)(2,1)S(1)}, bf16[1,96,1920]{2,1,0:T(8,128)(2,1)S(1)}, u32[]{:S(2)}, u32[]{:S(2)}) %collective-permute-start.39) | collective-permute-done | bytes 368672 | tf_op jit(solution)/shard_map/attn_outer/ppermute | solution.py:45
  449.0 9.2 %collective-permute-start.40 = (f32[96,128]{1,0:T(8,128)S(1)}, f32[96,128]{1,0:T(8,128)S(1)}, u32[]{:S(2)}, u32[]{:S(2)}) collective-permute-start(f32[96,128]{1,0:T(8,128)S(1)} %slice.91), channel_id=1, source_target_pairs={{0,1},{1,0},{2,3},{3,2},{4,5},{5,4},{6,7},{7,6},{8,9},{9,8},{10,11... | collective-permute-start | bytes 147464 | tf_op jit(solution)/shard_map/ppermute | solution.py:49
  (236 shorter events, 142.5 us)
Async XLA Ops:
  3.5 34.8 %all-to-all-start = ((bf16[8,96,1152]{2,1,0:T(8,128)(2,1)}), bf16[8,96,1152]{2,1,0:T(8,128)(2,1)S(1)}, u32[]{:S(2)}, u32[]{:S(2)}) async-start(bf16[8,96,1152]{2,1,0:T(8,128)(2,1)} %pad_maximum_fusion), calls=%async_computation | async-start | bytes 3538944 | tf_op jit(solution)/shard_map/all_to_all | solution.py:844
  8.3 30.0 %collective-permute-start.1 = (bf16[256,1536]{1,0:T(8,128)(2,1)}, bf16[256,1536]{1,0:T(8,128)(2,1)}, u32[]{:S(2)}, u32[]{:S(2)}) collective-permute-start(bf16[256,1536]{1,0:T(8,128)(2,1)} %grad_out.1), channel_id=1, source_target_pairs={{0,1},{1,0},{2,3},{3,2},{4,5},{5,4},{6,7},{7,6},{8,9},{9,8},{10,11... | collective-permute-start | bytes 2359304 | tf_op jit(solution)/shard_map/ppermute | solution.py:49
  9.6 28.7 %collective-permute-start = (bf16[256,1536]{1,0:T(8,128)(2,1)S(1)}, bf16[256,1536]{1,0:T(8,128)(2,1)S(1)}, u32[]{:S(2)}, u32[]{:S(2)}) collective-permute-start(bf16[256,1536]{1,0:T(8,128)(2,1)S(1)} %copy-done.6), channel_id=1, source_target_pairs={{0,1},{1,0},{2,3},{3,2},{4,5},{5,4},{6,7},{7,6},{8,9},{9,8},{10,11... | collective-permute-start | bytes 2359304 | tf_op jit(solution)/shard_map/ppermute | solution.py:49
  14.6 21.6 %collective-permute-start.2 = (bf16[1,96,1920]{2,1,0:T(8,128)(2,1)}, bf16[1,96,1920]{2,1,0:T(8,128)(2,1)}, u32[]{:S(2)}, u32[]{:S(2)}) collective-permute-start(bf16[1,96,1920]{2,1,0:T(8,128)(2,1)} %bitcast.7), channel_id=1, source_target_pairs={{0,16},{2,18},{4,20},{6,22},{8,24},{10,26},{12,28},{14,30},{16,0},... | collective-permute-start | bytes 1105928 | tf_op jit(solution)/shard_map/ppermute | solution.py:45
  39.9 32.2 %collective-permute-start.7 = (bf16[768,1152]{1,0:T(8,128)(2,1)}, bf16[768,1152]{1,0:T(8,128)(2,1)S(1)}, u32[]{:S(2)}, u32[]{:S(2)}) collective-permute-start(bf16[768,1152]{1,0:T(8,128)(2,1)} %get-tuple-element.111), channel_id=1, source_target_pairs={{0,1},{1,0},{2,3},{3,2},{4,5},{5,4},{6,7},{7,6},{8,9},{9,8},{10,11... | collective-permute-start | bytes 5308424 | tf_op jit(solution)/shard_map/ppermute | solution.py:49
  41.7 29.3 %collective-permute-start.3 = (bf16[2,96,1920]{2,1,0:T(8,128)(2,1)}, bf16[2,96,1920]{2,1,0:T(8,128)(2,1)}, u32[]{:S(2)}, u32[]{:S(2)}) collective-permute-start(bf16[2,96,1920]{2,1,0:T(8,128)(2,1)} %get-tuple-element.110.refs_1_.refs_0_), channel_id=1, source_target_pairs={{0,2},{2,0},{4,6},{6,4},{8,10},{10,8},{12,14},{14,12},{16,18},{18,... | collective-permute-start | bytes 2211848 | tf_op jit(solution)/shard_map/weights_near/ppermute | solution.py:45
  41.7 29.3 %collective-permute-start.4 = (bf16[2,96,1920]{2,1,0:T(8,128)(2,1)}, bf16[2,96,1920]{2,1,0:T(8,128)(2,1)}, u32[]{:S(2)}, u32[]{:S(2)}) collective-permute-start(bf16[2,96,1920]{2,1,0:T(8,128)(2,1)} %get-tuple-element.110.refs_1_.refs_0_), channel_id=1, source_target_pairs={{0,4},{2,6},{4,0},{6,2},{8,12},{10,14},{12,8},{14,10},{16,20},{18,... | collective-permute-start | bytes 2211848 | tf_op jit(solution)/shard_map/weights_near/ppermute | solution.py:45
  42.9 29.2 %collective-permute-start.5 = (bf16[2,96,1920]{2,1,0:T(8,128)(2,1)}, bf16[2,96,1920]{2,1,0:T(8,128)(2,1)}, u32[]{:S(2)}, u32[]{:S(2)}) collective-permute-start(bf16[2,96,1920]{2,1,0:T(8,128)(2,1)} %get-tuple-element.110.refs_1_.refs_0_), channel_id=1, source_target_pairs={{0,8},{2,10},{4,12},{6,14},{8,0},{10,2},{12,4},{14,6},{16,24},{18,... | collective-permute-start | bytes 2211848 | tf_op jit(solution)/shard_map/weights_near/ppermute | solution.py:45
  48.9 22.1 %collective-permute-start.6 = (bf16[1,160,1152]{2,1,0:T(8,128)(2,1)}, bf16[1,160,1152]{2,1,0:T(8,128)(2,1)}, u32[]{:S(2)}, u32[]{:S(2)}) collective-permute-start(bf16[1,160,1152]{2,1,0:T(8,128)(2,1)} %bitcast.54), channel_id=1, source_target_pairs={{0,16},{2,18},{4,20},{6,22},{8,24},{10,26},{12,28},{14,30},{16,0},... | collective-permute-start | bytes 1105928 | tf_op jit(solution)/shard_map/ppermute | solution.py:45
  73.3 28.6 %collective-permute-start.12 = (bf16[1,256,1152]{2,1,0:T(8,128)(2,1)}, bf16[1,256,1152]{2,1,0:T(8,128)(2,1)S(1)}, u32[]{:S(2)}, u32[]{:S(2)}) collective-permute-start(bf16[1,256,1152]{2,1,0:T(8,128)(2,1)} %bitcast.49), channel_id=1, source_target_pairs={{0,16},{2,18},{4,20},{6,22},{8,24},{10,26},{12,28},{14,30},{16,0},... | collective-permute-start | bytes 1769480 | tf_op jit(solution)/shard_map/ppermute | solution.py:45
  76.7 26.4 %collective-permute-start.10 = (bf16[2,96,1920]{2,1,0:T(8,128)(2,1)}, bf16[2,96,1920]{2,1,0:T(8,128)(2,1)}, u32[]{:S(2)}, u32[]{:S(2)}) collective-permute-start(bf16[2,96,1920]{2,1,0:T(8,128)(2,1)} %get-tuple-element.114.refs_4_), channel_id=1, source_target_pairs={{0,4},{2,6},{4,0},{6,2},{8,12},{10,14},{12,8},{14,10},{16,20},{18,... | collective-permute-start | bytes 2211848 | tf_op jit(solution)/shard_map/weights_far/ppermute | solution.py:45
  77.0 26.1 %collective-permute-start.11 = (bf16[2,96,1920]{2,1,0:T(8,128)(2,1)}, bf16[2,96,1920]{2,1,0:T(8,128)(2,1)}, u32[]{:S(2)}, u32[]{:S(2)}) collective-permute-start(bf16[2,96,1920]{2,1,0:T(8,128)(2,1)} %get-tuple-element.114.refs_4_), channel_id=1, source_target_pairs={{0,2},{2,0},{4,6},{6,4},{8,10},{10,8},{12,14},{14,12},{16,18},{18,... | collective-permute-start | bytes 2211848 | tf_op jit(solution)/shard_map/weights_far/ppermute | solution.py:45
  80.5 22.6 %collective-permute-start.8 = (bf16[1,96,1920]{2,1,0:T(8,128)(2,1)S(1)}, bf16[1,96,1920]{2,1,0:T(8,128)(2,1)S(1)}, u32[]{:S(2)}, u32[]{:S(2)}) collective-permute-start(bf16[1,96,1920]{2,1,0:T(8,128)(2,1)S(1)} %slice.68), channel_id=1, source_target_pairs={{0,2},{2,0},{4,6},{6,4},{8,10},{10,8},{12,14},{14,12},{16,18},{18,... | collective-permute-start | bytes 1105928 | tf_op jit(solution)/shard_map/weights_far/ppermute | solution.py:45
  80.6 22.5 %collective-permute-start.9 = (bf16[1,96,1920]{2,1,0:T(8,128)(2,1)S(1)}, bf16[1,96,1920]{2,1,0:T(8,128)(2,1)}, u32[]{:S(2)}, u32[]{:S(2)}) collective-permute-start(bf16[1,96,1920]{2,1,0:T(8,128)(2,1)S(1)} %slice.69), channel_id=1, source_target_pairs={{0,4},{2,6},{4,0},{6,2},{8,12},{10,14},{12,8},{14,10},{16,20},{18,... | collective-permute-start | bytes 1105928 | tf_op jit(solution)/shard_map/weights_far/ppermute | solution.py:45
  118.7 59.5 %all-to-all-start.1 = ((bf16[8,144,1664]{2,1,0:T(8,128)(2,1)}), bf16[8,144,1664]{2,1,0:T(8,128)(2,1)}, u32[]{:S(2)}, u32[]{:S(2)}) async-start(bf16[8,144,1664]{2,1,0:T(8,128)(2,1)} %get-tuple-element.132), calls=%async_computation.1 | async-start | bytes 7667712 | tf_op jit(solution)/shard_map/grads_rows/all_to_all | solution.py:878
  147.6 28.6 %collective-permute-start.19 = (bf16[1,176,1152]{2,1,0:T(8,128)(2,1)}, bf16[1,176,1152]{2,1,0:T(8,128)(2,1)S(1)}, u32[]{:S(2)}, u32[]{:S(2)}) collective-permute-start(bf16[1,176,1152]{2,1,0:T(8,128)(2,1)} %bitcast.53), channel_id=1, source_target_pairs={{0,16},{2,18},{4,20},{6,22},{8,24},{10,26},{12,28},{14,30},{16,0},... | collective-permute-start | bytes 1216520 | tf_op jit(solution)/shard_map/ppermute | solution.py:45
  178.1 29.3 %all-to-all-start.2 = ((bf16[8,64,1536]{2,1,0:T(8,128)(2,1)}), bf16[8,64,1536]{2,1,0:T(8,128)(2,1)S(1)}, u32[]{:S(2)}, u32[]{:S(2)}) async-start(bf16[8,64,1536]{2,1,0:T(8,128)(2,1)} %bitcast.47), calls=%async_computation.2 | async-start | bytes 3145728 | tf_op jit(solution)/shard_map/tokens_rows/all_to_all | solution.py:878
  185.9 19.8 %collective-permute-start.20 = (bf16[1,176,1152]{2,1,0:T(8,128)(2,1)}, bf16[1,176,1152]{2,1,0:T(8,128)(2,1)S(1)}, u32[]{:S(2)}, u32[]{:S(2)}) collective-permute-start(bf16[1,176,1152]{2,1,0:T(8,128)(2,1)} %bitcast.52), channel_id=1, source_target_pairs={{0,16},{2,18},{4,20},{6,22},{8,24},{10,26},{12,28},{14,30},{16,0},... | collective-permute-start | bytes 1216520 | tf_op jit(solution)/shard_map/ppermute | solution.py:45
  208.7 29.8 %all-to-all-start.3 = ((bf16[8,80,1536]{2,1,0:T(8,128)(2,1)}), bf16[8,80,1536]{2,1,0:T(8,128)(2,1)S(1)}, u32[]{:S(2)}, u32[]{:S(2)}) async-start(bf16[8,80,1536]{2,1,0:T(8,128)(2,1)} %bitcast.48), calls=%async_computation.3 | async-start | bytes 3932160 | tf_op jit(solution)/shard_map/tokens_rows/all_to_all | solution.py:878
  238.4 26.8 %all-to-all-start.5 = ((bf16[8,64,1664]{2,1,0:T(8,128)(2,1)}), bf16[8,64,1664]{2,1,0:T(8,128)(2,1)}, u32[]{:S(2)}, u32[]{:S(2)}) async-start(bf16[8,64,1664]{2,1,0:T(8,128)(2,1)} %bitcast.51), calls=%async_computation.5 | async-start | bytes 3407872 | tf_op jit(solution)/shard_map/gradn_rows/all_to_all | solution.py:878
  265.2 35.0 %all-to-all-start.4 = ((bf16[8,80,1664]{2,1,0:T(8,128)(2,1)}), bf16[8,80,1664]{2,1,0:T(8,128)(2,1)S(1)}, u32[]{:S(2)}, u32[]{:S(2)}) async-start(bf16[8,80,1664]{2,1,0:T(8,128)(2,1)} %bitcast.50), calls=%async_computation.4 | async-start | bytes 4259840 | tf_op jit(solution)/shard_map/gradn_rows/all_to_all | solution.py:878
  301.6 99.9 %all-to-all-start.6 = ((bf16[8,144,1536]{2,1,0:T(8,128)(2,1)}), bf16[8,144,1536]{2,1,0:T(8,128)(2,1)S(1)}, u32[]{:S(2)}, u32[]{:S(2)}) async-start(bf16[8,144,1536]{2,1,0:T(8,128)(2,1)} %gate.38), calls=%async_computation.6 | async-start | bytes 7077888 | tf_op jit(solution)/shard_map/branch_rows/all_to_all | solution.py:878
  313.2 32.8 %collective-permute-start.26 = (bf16[768,1152]{1,0:T(8,128)(2,1)}, bf16[768,1152]{1,0:T(8,128)(2,1)}, u32[]{:S(2)}, u32[]{:S(2)}) collective-permute-start(bf16[768,1152]{1,0:T(8,128)(2,1)} %get-tuple-element.169), channel_id=1, source_target_pairs={{0,1},{1,0},{2,3},{3,2},{4,5},{5,4},{6,7},{7,6},{8,9},{9,8},{10,11... | collective-permute-start | bytes 5308424 | tf_op jit(solution)/shard_map/ppermute | solution.py:49
  313.2 78.8 %collective-permute-start.34 = (bf16[768,1152]{1,0:T(8,128)(2,1)}, bf16[768,1152]{1,0:T(8,128)(2,1)}, u32[]{:S(2)}, u32[]{:S(2)}) collective-permute-start(bf16[768,1152]{1,0:T(8,128)(2,1)} %add_convert_fusion.1.refs_2_), channel_id=1, source_target_pairs={{0,16},{2,18},{4,20},{6,22},{8,24},{10,26},{12,28},{14,30},{16,0},... | collective-permute-start | bytes 5308424 | tf_op jit(solution)/shard_map/expert_scatter/ppermute | solution.py:45
  345.5 20.9 %collective-permute-start.29 = (bf16[256,1536]{1,0:T(8,128)(2,1)}, bf16[256,1536]{1,0:T(8,128)(2,1)}, u32[]{:S(2)}, u32[]{:S(2)}) collective-permute-start(bf16[256,1536]{1,0:T(8,128)(2,1)} %get-tuple-element.174), channel_id=1, source_target_pairs={{0,1},{1,0},{2,3},{3,2},{4,5},{5,4},{6,7},{7,6},{8,9},{9,8},{10,11... | collective-permute-start | bytes 2359304 | tf_op jit(solution)/shard_map/ppermute | solution.py:49
  345.9 20.4 %collective-permute-start.28 = (bf16[1,96,1920]{2,1,0:T(8,128)(2,1)}, bf16[1,96,1920]{2,1,0:T(8,128)(2,1)}, u32[]{:S(2)}, u32[]{:S(2)}) collective-permute-start(bf16[1,96,1920]{2,1,0:T(8,128)(2,1)} %get-tuple-element.171), channel_id=1, source_target_pairs={{0,4},{2,6},{4,0},{6,2},{8,12},{10,14},{12,8},{14,10},{16,20},{18,... | collective-permute-start | bytes 1105928 | tf_op jit(solution)/shard_map/attn_last/ppermute | solution.py:45
  366.4 31.8 %collective-permute-start.30 = (bf16[1,96,1920]{2,1,0:T(8,128)(2,1)}, bf16[1,96,1920]{2,1,0:T(8,128)(2,1)S(1)}, u32[]{:S(2)}, u32[]{:S(2)}) collective-permute-start(bf16[1,96,1920]{2,1,0:T(8,128)(2,1)} %get-tuple-element.175), channel_id=1, source_target_pairs={{0,2},{2,0},{4,6},{6,4},{8,10},{10,8},{12,14},{14,12},{16,18},{18,... | collective-permute-start | bytes 1105928 | tf_op jit(solution)/shard_map/attn_far/ppermute | solution.py:45
  376.0 22.2 %collective-permute-start.31 = (bf16[1,96,1920]{2,1,0:T(8,128)(2,1)}, bf16[1,96,1920]{2,1,0:T(8,128)(2,1)}, u32[]{:S(2)}, u32[]{:S(2)}) collective-permute-start(bf16[1,96,1920]{2,1,0:T(8,128)(2,1)} %get-tuple-element.176), channel_id=1, source_target_pairs={{0,4},{2,6},{4,0},{6,2},{8,12},{10,14},{12,8},{14,10},{16,20},{18,... | collective-permute-start | bytes 1105928 | tf_op jit(solution)/shard_map/attn_far/ppermute | solution.py:45
  378.9 22.5 %collective-permute-start.32 = (bf16[2,96,1920]{2,1,0:T(8,128)(2,1)}, bf16[2,96,1920]{2,1,0:T(8,128)(2,1)}, u32[]{:S(2)}, u32[]{:S(2)}) collective-permute-start(bf16[2,96,1920]{2,1,0:T(8,128)(2,1)} %get-tuple-element.181.refs_2_), channel_id=1, source_target_pairs={{0,4},{2,6},{4,0},{6,2},{8,12},{10,14},{12,8},{14,10},{16,20},{18,... | collective-permute-start | bytes 2211848 | tf_op jit(solution)/shard_map/attn_far/ppermute | solution.py:45
  379.8 21.7 %collective-permute-start.33 = (bf16[2,96,1920]{2,1,0:T(8,128)(2,1)}, bf16[2,96,1920]{2,1,0:T(8,128)(2,1)}, u32[]{:S(2)}, u32[]{:S(2)}) collective-permute-start(bf16[2,96,1920]{2,1,0:T(8,128)(2,1)} %get-tuple-element.182.refs_3_), channel_id=1, source_target_pairs={{0,2},{2,0},{4,6},{6,4},{8,10},{10,8},{12,14},{14,12},{16,18},{18,... | collective-permute-start | bytes 2211848 | tf_op jit(solution)/shard_map/attn_far/ppermute | solution.py:45
  407.8 53.3 %all-to-all-start.7 = ((bf16[8,96,1152]{2,1,0:T(8,128)(2,1)}), bf16[8,96,1152]{2,1,0:T(8,128)(2,1)S(1)}, u32[]{:S(2)}, u32[]{:S(2)}) async-start(bf16[8,96,1152]{2,1,0:T(8,128)(2,1)} %bitcast.29), calls=%async_computation.7 | async-start | bytes 3538944 | tf_op jit(solution)/shard_map/expert_scatter/all_to_all | solution.py:878
  428.8 20.1 %collective-permute-start.39 = (bf16[1,96,1920]{2,1,0:T(8,128)(2,1)S(1)}, bf16[1,96,1920]{2,1,0:T(8,128)(2,1)S(1)}, u32[]{:S(2)}, u32[]{:S(2)}) collective-permute-start(bf16[1,96,1920]{2,1,0:T(8,128)(2,1)S(1)} %slice.112), channel_id=1, source_target_pairs={{0,16},{2,18},{4,20},{6,22},{8,24},{10,26},{12,28},{14,30},{16,0},... | collective-permute-start | bytes 1105928 | tf_op jit(solution)/shard_map/attn_outer/ppermute | solution.py:45
  (58 other events, 391.2 us)

commit v6 on v5

--- a/solution.py
+++ b/solution.py
@@ -616,15 +616,15 @@
         copy.start()
     out_copies = []
     for block in range(blocks):
-        in_copies[2 * block].wait()
+        if block == 0:
+            for copy in in_copies:
+                copy.wait()
         x = xs[block]
         logits = lax.dot_general(x, router_ref[...], NN, preferred_element_type=f32)
         if block == 0:
             for k in weight_order:
-                if copies[k][5] < 2 * hidden:
-                    weight_copies[k].wait()
+                weight_copies[k].wait()
         pre = lax.dot_general(x, weights[:, : 2 * whole], NN, preferred_element_type=f32)
-        in_copies[2 * block + 1].wait()
         both = gs[block].reshape(rows, gs.shape[3])
         routed = both[:, width:].astype(f32) > 0.5
         lanes = lax.broadcasted_iota(jnp.int32, routed.shape, 1)
@@ -638,10 +638,6 @@
         gelu, slope = gelu_parts(gate_pre)
         act = (gelu * up_pre).astype(bf16)
         act_all[block] = act
-        if block == 0:
-            for k in weight_order:
-                if copies[k][5] == 2 * hidden:
-                    weight_copies[k].wait()
         down = weights[:, 2 * whole :]
         expert_out = lax.dot_general(act, down, NT, preferred_element_type=f32)
         branch[block] = (gate * expert_out).astype(bf16).reshape(branch.shape[1:])

time: 472 us -> 470 us (level)
  transfers between devices with their start and end apart: 49 -> 49, of which waited for: 21 -> 23; matrix products, arithmetic and copies ran while one was open for 11% -> 11% of each run, Pallas kernels for 28% -> 28%
where the time goes in v6:
time: 470 us; the launch traced here: 463 us
  waiting for transfers between devices  156 us (33%)
  Pallas kernels  132 us (28%)
  starting transfers between devices  101 us (21%)
  local copies, waits for them, and re-layouts  39.2 us (8%)
  other arithmetic  32.9 us (7%)
    ppermute x25, waiting for transfers between devices, swap(): return lax.ppermute(values, 'dp', [(i, i ^ bit) for i in range(count)])  142 us
    pallas_call x8, Pallas kernels, vmem_call(): pl.pallas_call(kernel, out_shape=out_shapes, in_specs=[pl.BlockSpec(memor...  68.6 us
    pallas_call x2, Pallas kernels, moe(): pl.pallas_call(functools.partial(moe_kernel, (copies, hidden, blocks, out...  35.6 us
    all_to_all x7, starting transfers between devices, exchange(): lax.all_to_all(rows, 'dp', 0, 0, tiled=True, axis_index_groups=groups)  33.4 us
    ppermute x16, starting transfers between devices, swap_core(): return lax.ppermute(values, 'tensor', [(0, 1), (1, 0)])  31.6 us
    ppermute x25, starting transfers between devices, swap(): return lax.ppermute(values, 'dp', [(i, i ^ bit) for i in range(count)])  31.6 us
    pallas_call x2, Pallas kernels, weight_grads(): pl.pallas_call(functools.partial(weight_grads_kernel, len(pre)), out_shap...  21.1 us
    unnamed x89, local copies, waits for them, and re-layouts  18.9 us
  transfers between devices with their start and end apart: 49, of which 23 were waited for; matrix products, arithmetic and copies ran while one was open for 11% of the time, Pallas kernels for 28%

profile of v6, /device:TPU:3, one launch (start us, length us, event | category | flops | bytes accessed | tf_op | source)
XLA Modules:
  0.0 462.9 jit_solution(6445633439279534656)
XLA Ops:
  3.5 4.8 %all-to-all-start = ((bf16[8,96,1152]{2,1,0:T(8,128)(2,1)}), bf16[8,96,1152]{2,1,0:T(8,128)(2,1)S(1)}, u32[]{:S(2)}, u32[]{:S(2)}) async-start(bf16[8,96,1152]{2,1,0:T(8,128)(2,1)} %pad_maximum_fusion), calls=%async_computation | async-start | bytes 3538944 | tf_op jit(solution)/shard_map/all_to_all | solution.py:840
  26.0 10.2 %collective-permute-done.2 = bf16[1,96,1920]{2,1,0:T(8,128)(2,1)} collective-permute-done((bf16[1,96,1920]{2,1,0:T(8,128)(2,1)}, bf16[1,96,1920]{2,1,0:T(8,128)(2,1)}, u32[]{:S(2)}, u32[]{:S(2)}) %collective-permute-start.2) | collective-permute-done | bytes 368672 | tf_op jit(solution)/shard_map/ppermute | solution.py:45
  49.5 6.7 %slots.1 = (bf16[512,512]{1,0:T(8,128)(2,1)}, bf16[640,512]{1,0:T(8,128)(2,1)}, bf16[8,144,1664]{2,1,0:T(8,128)(2,1)}) custom-call(s32[2]{0:T(128)} %pad_add_fusion.at_ref, s32[512,8]{1,0:T(8,128)} %copy.104.order_col, s32[8,512]{1,0:T(8,128)} %bitcast.57, bf16[256,1536]{1,0:T(8,128)(2,1)} %grad_out.1, ...), custom_call_target="tpu_custom_call" | custom-call | bytes 3000000 | tf_op jit(solution)/shard_map/slots/pallas_call | solution.py:279
  57.1 13.9 %collective-permute-done.6.refs_4_.refs_2_.refs_3_ = bf16[1,160,1152]{2,1,0:T(8,128)(2,1)} collective-permute-done((bf16[1,160,1152]{2,1,0:T(8,128)(2,1)}, bf16[1,160,1152]{2,1,0:T(8,128)(2,1)}, u32[]{:S(2)}, u32[]{:S(2)}) %collective-permute-start.6) | collective-permute-done | bytes 368672 | tf_op jit(solution)/shard_map/ppermute | solution.py:45
  81.9 20.1 %collective-permute-done.12.refs_4_.refs_5_ = bf16[1,256,1152]{2,1,0:T(8,128)(2,1)S(1)} collective-permute-done((bf16[1,256,1152]{2,1,0:T(8,128)(2,1)}, bf16[1,256,1152]{2,1,0:T(8,128)(2,1)S(1)}, u32[]{:S(2)}, u32[]{:S(2)}) %collective-permute-start.12) | collective-permute-done | bytes 589856 | tf_op jit(solution)/shard_map/ppermute | solution.py:45
  110.7 4.4 collective-permute-done.14.refs_0_
  118.7 4.8 %all-to-all-start.1 = ((bf16[8,144,1664]{2,1,0:T(8,128)(2,1)}), bf16[8,144,1664]{2,1,0:T(8,128)(2,1)}, u32[]{:S(2)}, u32[]{:S(2)}) async-start(bf16[8,144,1664]{2,1,0:T(8,128)(2,1)} %get-tuple-element.132), calls=%async_computation.1 | async-start | bytes 7667712 | tf_op jit(solution)/shard_map/grads_rows/all_to_all | solution.py:874
  123.5 13.7 %attend.1 = (bf16[512,1536]{1,0:T(8,128)(2,1)}, bf16[512,1536]{1,0:T(8,128)(2,1)}, bf16[512,768]{1,0:T(8,128)(2,1)}, bf16[512,128]{1,0:T(8,128)(2,1)}, bf16[512,...) custom-call(s32[2]{0:T(128)} %pad_add_fusion.at_ref, ...), custom_call_target="tpu_custom_call" | custom-call | tf_op jit(solution)/shard_map/attend/pallas_call | solution.py:279
  149.6 5.1 %take.1 = (bf16[512,1536]{1,0:T(8,128)(2,1)}, bf16[640,1536]{1,0:T(8,128)(2,1)}) custom-call(s32[2]{0:T(128)} %pad_add_fusion.at_ref, bf16[256,1536]{1,0:T(8,128)(2,1)} %get-tuple-element.128.own.normed, bf16[256,1536]{1,0:T(8,128)(2,1)} %copy-done.30, bf16[512,512]{1,0:T(8,128)(2,1)} %get-tuple-element.126.refs_0_, bf16[640,512]{1,0:T(8,128)(2,1)} %get-tuple-element.127.refs_1_), custom_call_target="tpu_custom_call" | custom-call | tf_op jit(solution)/shard_map/take/pallas_call | solution.py:279
  154.7 21.5 %collective-permute-done.19.refs_2_.refs_6_.refs_7_ = bf16[1,176,1152]{2,1,0:T(8,128)(2,1)S(1)} collective-permute-done((bf16[1,176,1152]{2,1,0:T(8,128)(2,1)}, bf16[1,176,1152]{2,1,0:T(8,128)(2,1)S(1)}, u32[]{:S(2)}, u32[]{:S(2)}) %collective-permute-start.19) | collective-permute-done | bytes 405536 | tf_op jit(solution)/shard_map/ppermute | solution.py:45
  187.4 18.3 %collective-permute-done.20.refs_2_.refs_8_.refs_9_ = bf16[1,176,1152]{2,1,0:T(8,128)(2,1)S(1)} collective-permute-done((bf16[1,176,1152]{2,1,0:T(8,128)(2,1)}, bf16[1,176,1152]{2,1,0:T(8,128)(2,1)S(1)}, u32[]{:S(2)}, u32[]{:S(2)}) %collective-permute-start.20) | collective-permute-done | bytes 405536 | tf_op jit(solution)/shard_map/ppermute | solution.py:45
  208.7 5.4 %all-to-all-start.3 = ((bf16[8,80,1536]{2,1,0:T(8,128)(2,1)}), bf16[8,80,1536]{2,1,0:T(8,128)(2,1)S(1)}, u32[]{:S(2)}, u32[]{:S(2)}) async-start(bf16[8,80,1536]{2,1,0:T(8,128)(2,1)} %bitcast.48), calls=%async_computation.3 | async-start | bytes 3932160 | tf_op jit(solution)/shard_map/tokens_rows/all_to_all | solution.py:874
  214.1 4.5 collective-permute-start.22
  220.7 16.4 %experts.2 = (bf16[8,144,1536]{2,1,0:T(8,128)(2,1)}, bf16[512,1664]{1,0:T(8,128)(2,1)}, bf16[512,768]{1,0:T(8,128)(2,1)}, bf16[512,1536]{1,0:T(8,128)(2,1)}, bf16[512,1536]{1,0:T(8,128)(2,1)}) custom-call(s32[2]{0:T(128)} %pad_add_fusion.at_ref, bf16[1536,128]{1,0:T(8,128)(2,1)} %get-tuple-element.130.router_ref.router, ...), custom_call_target="tpu_custom_call" | custom-call | bytes 3000000 | tf_op jit(solution)/shard_map/experts/pallas_call | solution.py:696
  237.6 4.7 %all-to-all-start.5 = ((bf16[8,64,1664]{2,1,0:T(8,128)(2,1)}), bf16[8,64,1664]{2,1,0:T(8,128)(2,1)}, u32[]{:S(2)}, u32[]{:S(2)}) async-start(bf16[8,64,1664]{2,1,0:T(8,128)(2,1)} %bitcast.51), calls=%async_computation.5 | async-start | bytes 3407872 | tf_op jit(solution)/shard_map/gradn_rows/all_to_all | solution.py:874
  243.1 19.2 %experts.3 = (bf16[8,144,1536]{2,1,0:T(8,128)(2,1)}, bf16[640,1664]{1,0:T(8,128)(2,1)}, bf16[640,768]{1,0:T(8,128)(2,1)}, bf16[640,1536]{1,0:T(8,128)(2,1)}, bf16[640,1536]{1,0:T(8,128)(2,1)}) custom-call(s32[2]{0:T(128)} %pad_add_fusion.at_ref, bf16[1536,128]{1,0:T(8,128)(2,1)} %gate.32.router_ref, ...), custom_call_target="tpu_custom_call", output_to_operand_aliasing={{0}: (4, {})} | custom-call | bytes 3000000 | tf_op jit(solution)/shard_map/experts/pallas_call | solution.py:696
  263.2 5.0 %all-to-all-start.4 = ((bf16[8,80,1664]{2,1,0:T(8,128)(2,1)}), bf16[8,80,1664]{2,1,0:T(8,128)(2,1)S(1)}, u32[]{:S(2)}, u32[]{:S(2)}) async-start(bf16[8,80,1664]{2,1,0:T(8,128)(2,1)} %bitcast.50), calls=%async_computation.4 | async-start | bytes 4259840 | tf_op jit(solution)/shard_map/gradn_rows/all_to_all | solution.py:874
  270.0 10.5 %weight_grads.2 = (bf16[768,1152]{1,0:T(8,128)(2,1)}, bf16[768,1152]{1,0:T(8,128)(2,1)}) custom-call(s32[3]{0:T(128)} %pad_add_fusion.1.at_ref, bf16[512,1536]{1,0:T(8,128)(2,1)} %get-tuple-element.135.x_in.refs_0_, bf16[640,1536]{1,0:T(8,128)(2,1)} %bitcast.42, bf16[512,1536]{1,0:T(8,128)(2,1)} %get-tuple-element.143.refs_2_, ...), custom_call_target="tpu_custom_call" | custom-call | tf_op jit(solution)/shard_map/weight_grads/pallas_call | solution.py:765
  284.4 10.6 %weight_grads.3 = (bf16[768,1152]{1,0:T(8,128)(2,1)}, bf16[768,1152]{1,0:T(8,128)(2,1)}) custom-call(s32[3]{0:T(128)} %pad_add_fusion.3.at_ref, bf16[512,1536]{1,0:T(8,128)(2,1)} %get-tuple-element.135.x_in.refs_0_, bf16[640,1536]{1,0:T(8,128)(2,1)} %bitcast.43, bf16[512,1536]{1,0:T(8,128)(2,1)} %get-tuple-element.143.refs_2_, ...), custom_call_target="tpu_custom_call" | custom-call | tf_op jit(solution)/shard_map/weight_grads/pallas_call | solution.py:765
  300.0 4.7 %all-to-all-start.6 = ((bf16[8,144,1536]{2,1,0:T(8,128)(2,1)}), bf16[8,144,1536]{2,1,0:T(8,128)(2,1)S(1)}, u32[]{:S(2)}, u32[]{:S(2)}) async-start(bf16[8,144,1536]{2,1,0:T(8,128)(2,1)} %gate.38), calls=%async_computation.6 | async-start | bytes 7077888 | tf_op jit(solution)/shard_map/branch_rows/all_to_all | solution.py:874
  304.7 6.3 %give_gradn.1 = (f32[256,1664]{1,0:T(8,128)}, bf16[256,1664]{1,0:T(8,128)(2,1)}) custom-call(s32[2]{0:T(128)} %pad_add_fusion.at_ref, bf16[512,512]{1,0:T(8,128)(2,1)} %get-tuple-element.126.refs_0_, bf16[640,512]{1,0:T(8,128)(2,1)} %get-tuple-element.127.refs_1_, bf16[512,1664]{1,0:T(8,128)(2,1)} %get-tuple-element.150.refs_2_, ...), custom_call_target="tpu_custom_call" | custom-call | tf_op jit(solution)/shard_map/give_gradn/pallas_call | solution.py:279
  314.0 6.4 %middle_back.1 = (f32[256,1536]{1,0:T(8,128)}, bf16[256,1536]{1,0:T(8,128)(2,1)}, f32[1536,128]{1,0:T(8,128)}) custom-call(f32[256,1536]{1,0:T(8,128)} %get-tuple-element.125.middle, bf16[256,1536]{1,0:T(8,128)(2,1)} %get-tuple-element.128.own.normed, bf16[256,1536]{1,0:T(8,128)(2,1)} %grad_out.1, bf16[256,128]{1,0:T(8,128)(2,1)} %get-tuple-element.129.code, ...), custom_call_target="tpu_custom_call" | custom-call | tf_op jit(solution)/shard_map/middle_back/pallas_call | solution.py:279
  323.0 20.9 %attend_back.1 = (f32[256,1536]{1,0:T(8,128)}, bf16[256,1536]{1,0:T(8,128)(2,1)}, bf16[2,96,1920]{2,1,0:T(8,128)(2,1)}, bf16[2,96,1920]{2,1,0:T(8,128)(2,1)}, bf...) custom-call(s32[2]{0:T(128)} %pad_add_fusion.at_ref, ...), custom_call_target="tpu_custom_call" | custom-call | tf_op jit(solution)/shard_map/attend_back/pallas_call | solution.py:279
  348.0 6.9 %collective-permute-done.27.refs_0_ = bf16[1,96,1920]{2,1,0:T(8,128)(2,1)S(1)} collective-permute-done((bf16[1,96,1920]{2,1,0:T(8,128)(2,1)}, bf16[1,96,1920]{2,1,0:T(8,128)(2,1)S(1)}, u32[]{:S(2)}, u32[]{:S(2)}) %collective-permute-start.27) | collective-permute-done | bytes 368672 | tf_op jit(solution)/shard_map/attn_last/ppermute | solution.py:45
  354.9 9.9 %collective-permute-done.28.refs_1_ = bf16[1,96,1920]{2,1,0:T(8,128)(2,1)} collective-permute-done((bf16[1,96,1920]{2,1,0:T(8,128)(2,1)}, bf16[1,96,1920]{2,1,0:T(8,128)(2,1)}, u32[]{:S(2)}, u32[]{:S(2)}) %collective-permute-start.28) | collective-permute-done | bytes 368672 | tf_op jit(solution)/shard_map/attn_last/ppermute | solution.py:45
  364.8 9.6 %collective-permute-start.30 = (bf16[1,96,1920]{2,1,0:T(8,128)(2,1)}, bf16[1,96,1920]{2,1,0:T(8,128)(2,1)S(1)}, u32[]{:S(2)}, u32[]{:S(2)}) collective-permute-start(bf16[1,96,1920]{2,1,0:T(8,128)(2,1)} %get-tuple-element.175), channel_id=1, source_target_pairs={{0,2},{2,0},{4,6},{6,4},{8,10},{10,8},{12,14},{14,12},{16,18},{18,... | collective-permute-start | bytes 1105928 | tf_op jit(solution)/shard_map/attn_far/ppermute | solution.py:45
  378.3 12.2 %collective-permute-done.34.refs_0_ = bf16[768,1152]{1,0:T(8,128)(2,1)} collective-permute-done((bf16[768,1152]{1,0:T(8,128)(2,1)}, bf16[768,1152]{1,0:T(8,128)(2,1)}, u32[]{:S(2)}, u32[]{:S(2)}) %collective-permute-start.34) | collective-permute-done | bytes 1769504 | tf_op jit(solution)/shard_map/expert_scatter/ppermute | solution.py:45
  390.5 4.5 add_convert_fusion.refs_5_
  406.2 4.6 all-to-all-start.7
  410.8 5.8 %give_branch.1 = (f32[256,1536]{1,0:T(8,128)}, bf16[256,1536]{1,0:T(8,128)(2,1)}) custom-call(s32[2]{0:T(128)} %pad_add_fusion.at_ref, bf16[512,512]{1,0:T(8,128)(2,1)} %get-tuple-element.126.refs_0_, bf16[640,512]{1,0:T(8,128)(2,1)} %get-tuple-element.127.refs_1_, bf16[8,144,1536]{2,1,0:T(8,128)(2,1)} %get-tuple-element.186.refs_2_), custom_call_target="tpu_custom_call" | custom-call | bytes 3000000 | tf_op jit(solution)/shard_map/give_branch/pallas_call | solution.py:279
  430.9 16.5 %collective-permute-done.39 = bf16[1,96,1920]{2,1,0:T(8,128)(2,1)S(1)} collective-permute-done((bf16[1,96,1920]{2,1,0:T(8,128)(2,1)S(1)}, bf16[1,96,1920]{2,1,0:T(8,128)(2,1)S(1)}, u32[]{:S(2)}, u32[]{:S(2)}) %collective-permute-start.39) | collective-permute-done | bytes 368672 | tf_op jit(solution)/shard_map/attn_outer/ppermute | solution.py:45
  447.4 9.2 %collective-permute-start.40 = (f32[96,128]{1,0:T(8,128)S(1)}, f32[96,128]{1,0:T(8,128)S(1)}, u32[]{:S(2)}, u32[]{:S(2)}) collective-permute-start(f32[96,128]{1,0:T(8,128)S(1)} %slice.91), channel_id=1, source_target_pairs={{0,1},{1,0},{2,3},{3,2},{4,5},{5,4},{6,7},{7,6},{8,9},{9,8},{10,11... | collective-permute-start | bytes 147464 | tf_op jit(solution)/shard_map/ppermute | solution.py:49
  (236 shorter events, 144.0 us)
Async XLA Ops:
  3.5 34.8 %all-to-all-start = ((bf16[8,96,1152]{2,1,0:T(8,128)(2,1)}), bf16[8,96,1152]{2,1,0:T(8,128)(2,1)S(1)}, u32[]{:S(2)}, u32[]{:S(2)}) async-start(bf16[8,96,1152]{2,1,0:T(8,128)(2,1)} %pad_maximum_fusion), calls=%async_computation | async-start | bytes 3538944 | tf_op jit(solution)/shard_map/all_to_all | solution.py:840
  8.3 30.0 %collective-permute-start.1 = (bf16[256,1536]{1,0:T(8,128)(2,1)}, bf16[256,1536]{1,0:T(8,128)(2,1)}, u32[]{:S(2)}, u32[]{:S(2)}) collective-permute-start(bf16[256,1536]{1,0:T(8,128)(2,1)} %grad_out.1), channel_id=1, source_target_pairs={{0,1},{1,0},{2,3},{3,2},{4,5},{5,4},{6,7},{7,6},{8,9},{9,8},{10,11... | collective-permute-start | bytes 2359304 | tf_op jit(solution)/shard_map/ppermute | solution.py:49
  9.6 28.7 %collective-permute-start = (bf16[256,1536]{1,0:T(8,128)(2,1)S(1)}, bf16[256,1536]{1,0:T(8,128)(2,1)S(1)}, u32[]{:S(2)}, u32[]{:S(2)}) collective-permute-start(bf16[256,1536]{1,0:T(8,128)(2,1)S(1)} %copy-done.6), channel_id=1, source_target_pairs={{0,1},{1,0},{2,3},{3,2},{4,5},{5,4},{6,7},{7,6},{8,9},{9,8},{10,11... | collective-permute-start | bytes 2359304 | tf_op jit(solution)/shard_map/ppermute | solution.py:49
  14.6 21.6 %collective-permute-start.2 = (bf16[1,96,1920]{2,1,0:T(8,128)(2,1)}, bf16[1,96,1920]{2,1,0:T(8,128)(2,1)}, u32[]{:S(2)}, u32[]{:S(2)}) collective-permute-start(bf16[1,96,1920]{2,1,0:T(8,128)(2,1)} %bitcast.7), channel_id=1, source_target_pairs={{0,16},{2,18},{4,20},{6,22},{8,24},{10,26},{12,28},{14,30},{16,0},... | collective-permute-start | bytes 1105928 | tf_op jit(solution)/shard_map/ppermute | solution.py:45
  39.9 32.2 %collective-permute-start.7 = (bf16[768,1152]{1,0:T(8,128)(2,1)}, bf16[768,1152]{1,0:T(8,128)(2,1)S(1)}, u32[]{:S(2)}, u32[]{:S(2)}) collective-permute-start(bf16[768,1152]{1,0:T(8,128)(2,1)} %get-tuple-element.111), channel_id=1, source_target_pairs={{0,1},{1,0},{2,3},{3,2},{4,5},{5,4},{6,7},{7,6},{8,9},{9,8},{10,11... | collective-permute-start | bytes 5308424 | tf_op jit(solution)/shard_map/ppermute | solution.py:49
  41.7 29.3 %collective-permute-start.3 = (bf16[2,96,1920]{2,1,0:T(8,128)(2,1)}, bf16[2,96,1920]{2,1,0:T(8,128)(2,1)}, u32[]{:S(2)}, u32[]{:S(2)}) collective-permute-start(bf16[2,96,1920]{2,1,0:T(8,128)(2,1)} %get-tuple-element.110.refs_1_.refs_0_), channel_id=1, source_target_pairs={{0,2},{2,0},{4,6},{6,4},{8,10},{10,8},{12,14},{14,12},{16,18},{18,... | collective-permute-start | bytes 2211848 | tf_op jit(solution)/shard_map/weights_near/ppermute | solution.py:45
  41.7 29.3 %collective-permute-start.4 = (bf16[2,96,1920]{2,1,0:T(8,128)(2,1)}, bf16[2,96,1920]{2,1,0:T(8,128)(2,1)}, u32[]{:S(2)}, u32[]{:S(2)}) collective-permute-start(bf16[2,96,1920]{2,1,0:T(8,128)(2,1)} %get-tuple-element.110.refs_1_.refs_0_), channel_id=1, source_target_pairs={{0,4},{2,6},{4,0},{6,2},{8,12},{10,14},{12,8},{14,10},{16,20},{18,... | collective-permute-start | bytes 2211848 | tf_op jit(solution)/shard_map/weights_near/ppermute | solution.py:45
  42.9 29.2 %collective-permute-start.5 = (bf16[2,96,1920]{2,1,0:T(8,128)(2,1)}, bf16[2,96,1920]{2,1,0:T(8,128)(2,1)}, u32[]{:S(2)}, u32[]{:S(2)}) collective-permute-start(bf16[2,96,1920]{2,1,0:T(8,128)(2,1)} %get-tuple-element.110.refs_1_.refs_0_), channel_id=1, source_target_pairs={{0,8},{2,10},{4,12},{6,14},{8,0},{10,2},{12,4},{14,6},{16,24},{18,... | collective-permute-start | bytes 2211848 | tf_op jit(solution)/shard_map/weights_near/ppermute | solution.py:45
  48.9 22.1 %collective-permute-start.6 = (bf16[1,160,1152]{2,1,0:T(8,128)(2,1)}, bf16[1,160,1152]{2,1,0:T(8,128)(2,1)}, u32[]{:S(2)}, u32[]{:S(2)}) collective-permute-start(bf16[1,160,1152]{2,1,0:T(8,128)(2,1)} %bitcast.54), channel_id=1, source_target_pairs={{0,16},{2,18},{4,20},{6,22},{8,24},{10,26},{12,28},{14,30},{16,0},... | collective-permute-start | bytes 1105928 | tf_op jit(solution)/shard_map/ppermute | solution.py:45
  73.3 28.6 %collective-permute-start.12 = (bf16[1,256,1152]{2,1,0:T(8,128)(2,1)}, bf16[1,256,1152]{2,1,0:T(8,128)(2,1)S(1)}, u32[]{:S(2)}, u32[]{:S(2)}) collective-permute-start(bf16[1,256,1152]{2,1,0:T(8,128)(2,1)} %bitcast.49), channel_id=1, source_target_pairs={{0,16},{2,18},{4,20},{6,22},{8,24},{10,26},{12,28},{14,30},{16,0},... | collective-permute-start | bytes 1769480 | tf_op jit(solution)/shard_map/ppermute | solution.py:45
  76.7 26.4 %collective-permute-start.10 = (bf16[2,96,1920]{2,1,0:T(8,128)(2,1)}, bf16[2,96,1920]{2,1,0:T(8,128)(2,1)}, u32[]{:S(2)}, u32[]{:S(2)}) collective-permute-start(bf16[2,96,1920]{2,1,0:T(8,128)(2,1)} %get-tuple-element.114.refs_4_), channel_id=1, source_target_pairs={{0,4},{2,6},{4,0},{6,2},{8,12},{10,14},{12,8},{14,10},{16,20},{18,... | collective-permute-start | bytes 2211848 | tf_op jit(solution)/shard_map/weights_far/ppermute | solution.py:45
  77.0 26.1 %collective-permute-start.11 = (bf16[2,96,1920]{2,1,0:T(8,128)(2,1)}, bf16[2,96,1920]{2,1,0:T(8,128)(2,1)}, u32[]{:S(2)}, u32[]{:S(2)}) collective-permute-start(bf16[2,96,1920]{2,1,0:T(8,128)(2,1)} %get-tuple-element.114.refs_4_), channel_id=1, source_target_pairs={{0,2},{2,0},{4,6},{6,4},{8,10},{10,8},{12,14},{14,12},{16,18},{18,... | collective-permute-start | bytes 2211848 | tf_op jit(solution)/shard_map/weights_far/ppermute | solution.py:45
  80.5 22.6 %collective-permute-start.8 = (bf16[1,96,1920]{2,1,0:T(8,128)(2,1)S(1)}, bf16[1,96,1920]{2,1,0:T(8,128)(2,1)S(1)}, u32[]{:S(2)}, u32[]{:S(2)}) collective-permute-start(bf16[1,96,1920]{2,1,0:T(8,128)(2,1)S(1)} %slice.68), channel_id=1, source_target_pairs={{0,2},{2,0},{4,6},{6,4},{8,10},{10,8},{12,14},{14,12},{16,18},{18,... | collective-permute-start | bytes 1105928 | tf_op jit(solution)/shard_map/weights_far/ppermute | solution.py:45
  80.6 22.5 %collective-permute-start.9 = (bf16[1,96,1920]{2,1,0:T(8,128)(2,1)S(1)}, bf16[1,96,1920]{2,1,0:T(8,128)(2,1)}, u32[]{:S(2)}, u32[]{:S(2)}) collective-permute-start(bf16[1,96,1920]{2,1,0:T(8,128)(2,1)S(1)} %slice.69), channel_id=1, source_target_pairs={{0,4},{2,6},{4,0},{6,2},{8,12},{10,14},{12,8},{14,10},{16,20},{18,... | collective-permute-start | bytes 1105928 | tf_op jit(solution)/shard_map/weights_far/ppermute | solution.py:45
  118.7 59.5 %all-to-all-start.1 = ((bf16[8,144,1664]{2,1,0:T(8,128)(2,1)}), bf16[8,144,1664]{2,1,0:T(8,128)(2,1)}, u32[]{:S(2)}, u32[]{:S(2)}) async-start(bf16[8,144,1664]{2,1,0:T(8,128)(2,1)} %get-tuple-element.132), calls=%async_computation.1 | async-start | bytes 7667712 | tf_op jit(solution)/shard_map/grads_rows/all_to_all | solution.py:874
  147.6 28.6 %collective-permute-start.19 = (bf16[1,176,1152]{2,1,0:T(8,128)(2,1)}, bf16[1,176,1152]{2,1,0:T(8,128)(2,1)S(1)}, u32[]{:S(2)}, u32[]{:S(2)}) collective-permute-start(bf16[1,176,1152]{2,1,0:T(8,128)(2,1)} %bitcast.53), channel_id=1, source_target_pairs={{0,16},{2,18},{4,20},{6,22},{8,24},{10,26},{12,28},{14,30},{16,0},... | collective-permute-start | bytes 1216520 | tf_op jit(solution)/shard_map/ppermute | solution.py:45
  178.2 29.3 %all-to-all-start.2 = ((bf16[8,64,1536]{2,1,0:T(8,128)(2,1)}), bf16[8,64,1536]{2,1,0:T(8,128)(2,1)S(1)}, u32[]{:S(2)}, u32[]{:S(2)}) async-start(bf16[8,64,1536]{2,1,0:T(8,128)(2,1)} %bitcast.47), calls=%async_computation.2 | async-start | bytes 3145728 | tf_op jit(solution)/shard_map/tokens_rows/all_to_all | solution.py:874
  186.0 19.8 %collective-permute-start.20 = (bf16[1,176,1152]{2,1,0:T(8,128)(2,1)}, bf16[1,176,1152]{2,1,0:T(8,128)(2,1)S(1)}, u32[]{:S(2)}, u32[]{:S(2)}) collective-permute-start(bf16[1,176,1152]{2,1,0:T(8,128)(2,1)} %bitcast.52), channel_id=1, source_target_pairs={{0,16},{2,18},{4,20},{6,22},{8,24},{10,26},{12,28},{14,30},{16,0},... | collective-permute-start | bytes 1216520 | tf_op jit(solution)/shard_map/ppermute | solution.py:45
  208.7 28.9 %all-to-all-start.3 = ((bf16[8,80,1536]{2,1,0:T(8,128)(2,1)}), bf16[8,80,1536]{2,1,0:T(8,128)(2,1)S(1)}, u32[]{:S(2)}, u32[]{:S(2)}) async-start(bf16[8,80,1536]{2,1,0:T(8,128)(2,1)} %bitcast.48), calls=%async_computation.3 | async-start | bytes 3932160 | tf_op jit(solution)/shard_map/tokens_rows/all_to_all | solution.py:874
  237.6 25.5 %all-to-all-start.5 = ((bf16[8,64,1664]{2,1,0:T(8,128)(2,1)}), bf16[8,64,1664]{2,1,0:T(8,128)(2,1)}, u32[]{:S(2)}, u32[]{:S(2)}) async-start(bf16[8,64,1664]{2,1,0:T(8,128)(2,1)} %bitcast.51), calls=%async_computation.5 | async-start | bytes 3407872 | tf_op jit(solution)/shard_map/gradn_rows/all_to_all | solution.py:874
  263.2 35.5 %all-to-all-start.4 = ((bf16[8,80,1664]{2,1,0:T(8,128)(2,1)}), bf16[8,80,1664]{2,1,0:T(8,128)(2,1)S(1)}, u32[]{:S(2)}, u32[]{:S(2)}) async-start(bf16[8,80,1664]{2,1,0:T(8,128)(2,1)} %bitcast.50), calls=%async_computation.4 | async-start | bytes 4259840 | tf_op jit(solution)/shard_map/gradn_rows/all_to_all | solution.py:874
  300.0 100.0 %all-to-all-start.6 = ((bf16[8,144,1536]{2,1,0:T(8,128)(2,1)}), bf16[8,144,1536]{2,1,0:T(8,128)(2,1)S(1)}, u32[]{:S(2)}, u32[]{:S(2)}) async-start(bf16[8,144,1536]{2,1,0:T(8,128)(2,1)} %gate.38), calls=%async_computation.6 | async-start | bytes 7077888 | tf_op jit(solution)/shard_map/branch_rows/all_to_all | solution.py:874
  311.6 32.8 %collective-permute-start.26 = (bf16[768,1152]{1,0:T(8,128)(2,1)}, bf16[768,1152]{1,0:T(8,128)(2,1)}, u32[]{:S(2)}, u32[]{:S(2)}) collective-permute-start(bf16[768,1152]{1,0:T(8,128)(2,1)} %get-tuple-element.169), channel_id=1, source_target_pairs={{0,1},{1,0},{2,3},{3,2},{4,5},{5,4},{6,7},{7,6},{8,9},{9,8},{10,11... | collective-permute-start | bytes 5308424 | tf_op jit(solution)/shard_map/ppermute | solution.py:49
  311.6 78.8 %collective-permute-start.34 = (bf16[768,1152]{1,0:T(8,128)(2,1)}, bf16[768,1152]{1,0:T(8,128)(2,1)}, u32[]{:S(2)}, u32[]{:S(2)}) collective-permute-start(bf16[768,1152]{1,0:T(8,128)(2,1)} %add_convert_fusion.1.refs_2_), channel_id=1, source_target_pairs={{0,16},{2,18},{4,20},{6,22},{8,24},{10,26},{12,28},{14,30},{16,0},... | collective-permute-start | bytes 5308424 | tf_op jit(solution)/shard_map/expert_scatter/ppermute | solution.py:45
  343.9 20.9 %collective-permute-start.29 = (bf16[256,1536]{1,0:T(8,128)(2,1)}, bf16[256,1536]{1,0:T(8,128)(2,1)}, u32[]{:S(2)}, u32[]{:S(2)}) collective-permute-start(bf16[256,1536]{1,0:T(8,128)(2,1)} %get-tuple-element.174), channel_id=1, source_target_pairs={{0,1},{1,0},{2,3},{3,2},{4,5},{5,4},{6,7},{7,6},{8,9},{9,8},{10,11... | collective-permute-start | bytes 2359304 | tf_op jit(solution)/shard_map/ppermute | solution.py:49
  344.4 20.4 %collective-permute-start.28 = (bf16[1,96,1920]{2,1,0:T(8,128)(2,1)}, bf16[1,96,1920]{2,1,0:T(8,128)(2,1)}, u32[]{:S(2)}, u32[]{:S(2)}) collective-permute-start(bf16[1,96,1920]{2,1,0:T(8,128)(2,1)} %get-tuple-element.171), channel_id=1, source_target_pairs={{0,4},{2,6},{4,0},{6,2},{8,12},{10,14},{12,8},{14,10},{16,20},{18,... | collective-permute-start | bytes 1105928 | tf_op jit(solution)/shard_map/attn_last/ppermute | solution.py:45
  364.8 31.8 %collective-permute-start.30 = (bf16[1,96,1920]{2,1,0:T(8,128)(2,1)}, bf16[1,96,1920]{2,1,0:T(8,128)(2,1)S(1)}, u32[]{:S(2)}, u32[]{:S(2)}) collective-permute-start(bf16[1,96,1920]{2,1,0:T(8,128)(2,1)} %get-tuple-element.175), channel_id=1, source_target_pairs={{0,2},{2,0},{4,6},{6,4},{8,10},{10,8},{12,14},{14,12},{16,18},{18,... | collective-permute-start | bytes 1105928 | tf_op jit(solution)/shard_map/attn_far/ppermute | solution.py:45
  374.5 22.2 %collective-permute-start.31 = (bf16[1,96,1920]{2,1,0:T(8,128)(2,1)}, bf16[1,96,1920]{2,1,0:T(8,128)(2,1)}, u32[]{:S(2)}, u32[]{:S(2)}) collective-permute-start(bf16[1,96,1920]{2,1,0:T(8,128)(2,1)} %get-tuple-element.176), channel_id=1, source_target_pairs={{0,4},{2,6},{4,0},{6,2},{8,12},{10,14},{12,8},{14,10},{16,20},{18,... | collective-permute-start | bytes 1105928 | tf_op jit(solution)/shard_map/attn_far/ppermute | solution.py:45
  377.4 22.5 %collective-permute-start.32 = (bf16[2,96,1920]{2,1,0:T(8,128)(2,1)}, bf16[2,96,1920]{2,1,0:T(8,128)(2,1)}, u32[]{:S(2)}, u32[]{:S(2)}) collective-permute-start(bf16[2,96,1920]{2,1,0:T(8,128)(2,1)} %get-tuple-element.181.refs_2_), channel_id=1, source_target_pairs={{0,4},{2,6},{4,0},{6,2},{8,12},{10,14},{12,8},{14,10},{16,20},{18,... | collective-permute-start | bytes 2211848 | tf_op jit(solution)/shard_map/attn_far/ppermute | solution.py:45
  378.2 21.7 %collective-permute-start.33 = (bf16[2,96,1920]{2,1,0:T(8,128)(2,1)}, bf16[2,96,1920]{2,1,0:T(8,128)(2,1)}, u32[]{:S(2)}, u32[]{:S(2)}) collective-permute-start(bf16[2,96,1920]{2,1,0:T(8,128)(2,1)} %get-tuple-element.182.refs_3_), channel_id=1, source_target_pairs={{0,2},{2,0},{4,6},{6,4},{8,10},{10,8},{12,14},{14,12},{16,18},{18,... | collective-permute-start | bytes 2211848 | tf_op jit(solution)/shard_map/attn_far/ppermute | solution.py:45
  406.2 53.3 %all-to-all-start.7 = ((bf16[8,96,1152]{2,1,0:T(8,128)(2,1)}), bf16[8,96,1152]{2,1,0:T(8,128)(2,1)S(1)}, u32[]{:S(2)}, u32[]{:S(2)}) async-start(bf16[8,96,1152]{2,1,0:T(8,128)(2,1)} %bitcast.29), calls=%async_computation.7 | async-start | bytes 3538944 | tf_op jit(solution)/shard_map/expert_scatter/all_to_all | solution.py:874
  427.2 20.1 %collective-permute-start.39 = (bf16[1,96,1920]{2,1,0:T(8,128)(2,1)S(1)}, bf16[1,96,1920]{2,1,0:T(8,128)(2,1)S(1)}, u32[]{:S(2)}, u32[]{:S(2)}) collective-permute-start(bf16[1,96,1920]{2,1,0:T(8,128)(2,1)S(1)} %slice.112), channel_id=1, source_target_pairs={{0,16},{2,18},{4,20},{6,22},{8,24},{10,26},{12,28},{14,30},{16,0},... | collective-permute-start | bytes 1105928 | tf_op jit(solution)/shard_map/attn_outer/ppermute | solution.py:45
  (58 other events, 391.1 us)
